TPU v7x, 512 devices: a whole 4x4x16 slice. The times are simulated.
512 devices in a mesh: gx: 32 (over z, y_lo), gy: 16 (over x, y_hi, core).
Axes of the slice: x: 4, y: 4 (y_hi: 2, y_lo: 2; y = y_hi * 2 + y_lo), z: 16, core: 2. Of those that a mesh axis runs over, the one named last changes fastest.
Arguments:
- e_fwd: float32 [3, 128, 512, 256], P(None, 'gx', 'gy'), may hold values from -6 to 6
- h_fwd: float32 [3, 128, 512, 256], P(None, 'gx', 'gy'), may hold values from -6 to 6
- e_adj: float32 [3, 128, 512, 256], P(None, 'gx', 'gy'), may hold values from -6 to 6
- h_adj: float32 [3, 128, 512, 256], P(None, 'gx', 'gy'), may hold values from -6 to 6
- eps_back: float32 [128, 512, 256], P('gx', 'gy'), may hold values from 1 to 12
- density: float32 [4, 128, 512], P(None, 'gx', 'gy'), may hold values from 0 to 1
- design_mask: int32 [4, 128, 512], P(None, 'gx', 'gy'), may hold values 0 or 1
- partner_map: int32 [4, 128, 512], P(None, 'gx', 'gy'), may hold values from 0 to 511, as said below
- mon_fwd: float32 [2, 3, 4, 128, 512], P(None, None, None, 'gx', 'gy'), may hold values from -6 to 6
- mon_adj: float32 [2, 3, 4, 128, 512], P(None, None, None, 'gx', 'gy'), may hold values from -6 to 6
Outputs:
- e_fwd_out: float32 [3, 128, 512, 256], P(None, 'gx', 'gy')
- h_fwd_out: float32 [3, 128, 512, 256], P(None, 'gx', 'gy')
- e_adj_out: float32 [3, 128, 512, 256], P(None, 'gx', 'gy')
- h_adj_out: float32 [3, 128, 512, 256], P(None, 'gx', 'gy')
- density_grad: float32 [4, 128, 512], P(None, 'gx', 'gy')
Inputs may be any that keep to these rules, and one draw needn't show every extreme that they name: partner_map pairs cells of mirrored blocks one to one and is an involution: the partner of a cell's partner is the cell itself.
All inputs are finite; a program needn't handle non-finite values. No bound on the sum of `design_mask` on one device may be relied on, other than what follows from the above.
Results may differ from a plain program's by a relative error of at most 0.0003.
Values sent between devices are 32-bit elements; how exact they have to be, the bound alone decides.
No kernel may reach another device: no remote copies, remote signals or barrier semaphores. Data moves between devices by JAX's collectives and lax.ppermute only.
A program may use at most 64 MiB of HBM per device.

v0:
```python
import math

import jax
import jax.numpy as jnp
from jax import lax
from jax.sharding import PartitionSpec as P

PLANES = 4
STEPS = 2
Z0 = 126


COURANT = 0.5
OMEGA = 0.7
CONTRAST = 10.0


def shifted(block, axis, distance):
    devices = range(lax.axis_size(axis))
    route = [(i - distance, i) for i in devices if i - distance in devices]
    return lax.ppermute(block, axis, route)


def swapped(value, axis, bit):
    return lax.ppermute(value, axis, [(i, i ^ 1 << bit) for i in range(lax.axis_size(axis))])


def ahead_diff(field, upper, axis):
    extended = jnp.concatenate([field, upper], axis)
    return lax.slice_in_dim(extended, 1, extended.shape[axis], axis=axis) - field


def behind_diff(field, lower, axis):
    extended = jnp.concatenate([lower, field], axis)
    return field - lax.slice_in_dim(extended, 0, field.shape[axis], axis=axis)


def curl_ahead(pair, rim_x, rim_y):
    fx, fy, fz = (pair[:, 0], pair[:, 1], pair[:, 2])
    zero_plane = jnp.zeros_like(fx[..., :1])
    return jnp.stack(
        [
            ahead_diff(fz, rim_y[:, 1], 2) - ahead_diff(fy, zero_plane, 3),
            ahead_diff(fx, zero_plane, 3) - ahead_diff(fz, rim_x[:, 1], 1),
            ahead_diff(fy, rim_x[:, 0], 1) - ahead_diff(fx, rim_y[:, 0], 2),
        ],
        axis=1,
    )


def curl_behind(pair, rim_x, rim_y):
    fx, fy, fz = (pair[:, 0], pair[:, 1], pair[:, 2])
    zero_plane = jnp.zeros_like(fx[..., :1])
    return jnp.stack(
        [
            behind_diff(fz, rim_y[:, 1], 2) - behind_diff(fy, zero_plane, 3),
            behind_diff(fx, zero_plane, 3) - behind_diff(fz, rim_x[:, 1], 1),
            behind_diff(fy, rim_x[:, 0], 1) - behind_diff(fx, rim_y[:, 0], 2),
        ],
        axis=1,
    )


def slab_of(pair):
    return jnp.transpose(pair[:, :, :, :, Z0 : Z0 + PLANES], (0, 1, 4, 2, 3))


def electric_upper_x(values):
    return shifted(values, "gx", -1)


def electric_upper_y(values):
    return shifted(values, "gy", -1)


def magnetic_lower_x(values):
    return shifted(values, "gx", 1)


def magnetic_lower_y(values):
    return shifted(values, "gy", 1)


def per_device(
    e_fwd, h_fwd, e_adj, h_adj, eps_back, density, design_mask, partner_map, mon_fwd, mon_adj
):
    count = density.size
    partner_flat = partner_map.reshape(count)
    flat_density = density.reshape(count)
    mirrored = flat_density
    for bit_number in range(lax.axis_size("gx").bit_length() - 1):
        mirrored = swapped(mirrored, "gx", bit_number)
    sym = 0.5 * (density + jnp.take(mirrored, partner_flat).reshape(density.shape))
    weight = CONTRAST * design_mask.astype(jnp.float32)
    slab_eps = jnp.transpose(eps_back[:, :, Z0 : Z0 + PLANES], (2, 0, 1)) + weight * sym
    eps = eps_back.at[:, :, Z0 : Z0 + PLANES].set(jnp.transpose(slab_eps, (1, 2, 0)))
    electric = jnp.stack([e_fwd, e_adj])
    magnetic = jnp.stack([h_fwd, h_adj])
    monitors = jnp.stack([mon_fwd, mon_adj])
    for step in range(STEPS):
        upper_x = jnp.concatenate(
            [electric_upper_x(electric[which : which + 1, 1:, :1]) for which in range(2)], 0
        )
        upper_y = jnp.concatenate(
            [electric_upper_y(electric[which : which + 1, 0::2, :, :1]) for which in range(2)], 0
        )
        magnetic = magnetic - COURANT * curl_ahead(electric, upper_x, upper_y)
        lower_x = jnp.concatenate(
            [magnetic_lower_x(magnetic[which : which + 1, 1:, -1:]) for which in range(2)], 0
        )
        lower_y = jnp.concatenate(
            [magnetic_lower_y(magnetic[which : which + 1, 0::2, :, -1:]) for which in range(2)], 0
        )
        electric = electric + COURANT / eps * curl_behind(magnetic, lower_x, lower_y)
        phase = OMEGA * (step + 1)
        slab_values = slab_of(electric)
        monitors = monitors + jnp.stack(
            [math.cos(phase) * slab_values, -math.sin(phase) * slab_values], axis=1
        )
    local_grad = weight * jnp.sum(
        monitors[0, 0] * monitors[1, 0] - monitors[0, 1] * monitors[1, 1], axis=0
    )
    flat_grad = local_grad.reshape(count)
    mirrored_grad = flat_grad
    for bit_number in range(lax.axis_size("gx").bit_length() - 1):
        mirrored_grad = swapped(mirrored_grad, "gx", bit_number)
    density_grad = 0.5 * (
        local_grad + jnp.take(mirrored_grad, partner_flat).reshape(local_grad.shape)
    )
    return (electric[0], magnetic[0], electric[1], magnetic[1], density_grad)


def solution(mesh):
    placed = (
        P(None, "gx", "gy", None),
        P(None, "gx", "gy", None),
        P(None, "gx", "gy", None),
        P(None, "gx", "gy", None),
        P("gx", "gy", None),
        P(None, "gx", "gy"),
        P(None, "gx", "gy"),
        P(None, "gx", "gy"),
        P(None, None, None, "gx", "gy"),
        P(None, None, None, "gx", "gy"),
    )
    return jax.shard_map(
        per_device,
        mesh=mesh,
        in_specs=placed,
        out_specs=(
            P(None, "gx", "gy", None),
            P(None, "gx", "gy", None),
            P(None, "gx", "gy", None),
            P(None, "gx", "gy", None),
            P(None, "gx", "gy"),
        ),
        check_vma=False,
    )
```

profile of v0, /device:TPU:20, one launch (start us, length us, event | category | flops | bytes accessed | tf_op | source)
XLA Modules:
  0.0 186.9 jit_solution(14190325789189313367)
XLA Ops:
  0.6 0.9 copy.580
  1.6 3.3 %collective-permute-start = (f32[512]{0:T(512)S(1)}, f32[512]{0:T(512)S(1)}, u32[]{:S(2)}, u32[]{:S(2)}) collective-permute-start(f32[512]{0:T(512)S(1)} %reshape.65), channel_id=1, source_target_pairs={{0,16},{16,0},{32,48},{48,32},{64,80},{80,64},{96,112},{112,96},{1... | collective-permute-start | bytes 6152 | tf_op jit(solution)/shard_map/ppermute | solution.py:25
  5.0 1.3 copy.559
  6.2 1.9 %collective-permute-start.5 = (f32[1,2,4,1,256]{4,2,3,1,0:T(4,128)S(1)}, f32[1,2,4,1,256]{4,2,3,1,0:T(4,128)S(1)}, u32[]{:S(2)}, u32[]{:S(2)}) collective-permute-start(f32[1,2,4,1,256]{4,2,3,1,0:T(4,128)S(1)} %slice.261), channel_id=1, source_target_pairs={{1,0},{2,1},{3,2},{4,3},{5,4},{6,5},{7,6},{8,7},{9,8},{10,9},{11,1... | collective-permute-start | bytes 24584 | tf_op jit(solution)/shard_map/ppermute | solution.py:21
  8.8 1.3 collective-permute-start.7
  10.4 2.6 %collective-permute-start.6 = (f32[1,2,4,1,256]{4,2,3,1,0:T(4,128)S(1)}, f32[1,2,4,1,256]{4,2,3,1,0:T(4,128)S(1)}, u32[]{:S(2)}, u32[]{:S(2)}) collective-permute-start(f32[1,2,4,1,256]{4,2,3,1,0:T(4,128)S(1)} %slice.262), channel_id=1, source_target_pairs={{1,0},{2,1},{3,2},{4,3},{5,4},{6,5},{7,6},{8,7},{9,8},{10,9},{11,1... | collective-permute-start | bytes 24584 | tf_op jit(solution)/shard_map/ppermute | solution.py:21
  13.7 1.3 collective-permute-start.8
  16.0 6.9 %collective-permute-start.1 = (f32[512]{0:T(512)S(1)}, f32[512]{0:T(512)S(1)}, u32[]{:S(2)}, u32[]{:S(2)}) collective-permute-start(f32[512]{0:T(512)S(1)} %collective-permute-done), channel_id=1, source_target_pairs={{0,32},{16,48},{32,0},{48,16},{64,96},{80,112},{96,64},{112,80},{1... | collective-permute-start | bytes 6152 | tf_op jit(solution)/shard_map/ppermute | solution.py:25
  23.0 1.5 collective-permute-done.1
  24.5 5.3 %collective-permute-start.2 = (f32[512]{0:T(512)S(1)}, f32[512]{0:T(512)S(1)}, u32[]{:S(2)}, u32[]{:S(2)}) collective-permute-start(f32[512]{0:T(512)S(1)} %collective-permute-done.1), channel_id=1, source_target_pairs={{0,64},{16,80},{32,96},{48,112},{64,0},{80,16},{96,32},{112,48},{1... | collective-permute-start | bytes 6152 | tf_op jit(solution)/shard_map/ppermute | solution.py:25
  29.8 1.2 pad_maximum_fusion.1
  31.3 9.1 %collective-permute-start.3 = (f32[512]{0:T(512)S(1)}, f32[512]{0:T(512)S(1)}, u32[]{:S(2)}, u32[]{:S(2)}) collective-permute-start(f32[512]{0:T(512)S(1)} %collective-permute-done.2), channel_id=1, source_target_pairs={{0,128},{16,144},{32,160},{48,176},{64,192},{80,208},{96,224},{112... | collective-permute-start | bytes 6152 | tf_op jit(solution)/shard_map/ppermute | solution.py:25
  40.7 1.3 collective-permute-done.3
  42.0 14.1 %collective-permute-start.4 = (f32[512]{0:T(512)S(1)}, f32[512]{0:T(512)S(1)}, u32[]{:S(2)}, u32[]{:S(2)}) collective-permute-start(f32[512]{0:T(512)S(1)} %collective-permute-done.3), channel_id=1, source_target_pairs={{0,256},{16,272},{32,288},{48,304},{64,320},{80,336},{96,352},{112... | collective-permute-start | bytes 6152 | tf_op jit(solution)/shard_map/ppermute | solution.py:25
  56.2 1.5 collective-permute-done.4
  57.6 3.5 %gather_fusion = f32[512]{0:T(512)S(1)} fusion(f32[512]{0:T(512)S(1)} %collective-permute-done.4, s32[1024]{0:T(1024)S(1)} %pad_clamp_fusion), kind=kCustom, calls=%fused_computation.clone | custom fusion | bytes 6144 | tf_op jit(solution)/shard_map/jit(_take)/gather | solution.py:93
  61.9 0.9 scatter.4
  62.9 0.7 copy.537
  63.6 0.8 constant_dynamic-update-slice_fusion.3
  64.5 0.9 constant_dynamic-update-slice_fusion.2
  66.9 1.2 fusion
  68.1 1.2 slice.278
  69.4 0.7 fusion.60
  70.7 1.9 %collective-permute-start.9 = (f32[1,2,4,1,256]{4,2,3,1,0:T(4,128)}, f32[1,2,4,1,256]{4,2,3,1,0:T(4,128)}, u32[]{:S(2)}, u32[]{:S(2)}) collective-permute-start(f32[1,2,4,1,256]{4,2,3,1,0:T(4,128)} %copy.486), channel_id=1, source_target_pairs={{0,1},{1,2},{2,3},{3,4},{4,5},{5,6},{6,7},{7,8},{8,9},{9,10},{10,1... | collective-permute-start | bytes 24584 | tf_op jit(solution)/shard_map/ppermute | solution.py:21
  72.6 0.7 fusion.61
  73.3 1.2 slice.279
  75.3 4.6 %collective-permute-start.10 = (f32[1,2,4,1,256]{4,2,3,1,0:T(4,128)S(1)}, f32[1,2,4,1,256]{4,2,3,1,0:T(4,128)S(1)}, u32[]{:S(2)}, u32[]{:S(2)}) collective-permute-start(f32[1,2,4,1,256]{4,2,3,1,0:T(4,128)S(1)} %copy.487), channel_id=1, source_target_pairs={{0,1},{1,2},{2,3},{3,4},{4,5},{5,6},{6,7},{7,8},{8,9},{9,10},{10,1... | collective-permute-start | bytes 24584 | tf_op jit(solution)/shard_map/ppermute | solution.py:21
  79.9 0.8 copy-done.11
  80.7 3.9 %collective-permute-start.12 = (f32[1,2,1,32,256]{4,1,3,2,0:T(2,128)S(1)}, f32[1,2,1,32,256]{4,1,3,2,0:T(2,128)S(1)}, u32[]{:S(2)}, u32[]{:S(2)}) collective-permute-start(f32[1,2,1,32,256]{4,1,3,2,0:T(2,128)S(1)} %copy-done.11), channel_id=1, source_target_pairs={{0,16},{16,32},{32,48},{48,64},{64,80},{80,96},{96,112},{112,128},... | collective-permute-start | bytes 196616 | tf_op jit(solution)/shard_map/ppermute | solution.py:21
  84.6 3.3 %collective-permute-start.11 = (f32[1,2,1,32,256]{4,1,3,2,0:T(2,128)S(1)}, f32[1,2,1,32,256]{4,1,3,2,0:T(2,128)S(1)}, u32[]{:S(2)}, u32[]{:S(2)}) collective-permute-start(f32[1,2,1,32,256]{4,1,3,2,0:T(2,128)S(1)} %copy-done.12), channel_id=1, source_target_pairs={{0,16},{16,32},{32,48},{48,64},{64,80},{80,96},{96,112},{112,128},... | collective-permute-start | bytes 196616 | tf_op jit(solution)/shard_map/ppermute | solution.py:21
  88.7 1.1 collective-permute-done.11
  90.9 0.9 fusion.62
  92.1 1.9 %collective-permute-start.13 = (f32[1,2,4,1,256]{4,2,3,1,0:T(4,128)S(1)}, f32[1,2,4,1,256]{4,2,3,1,0:T(4,128)S(1)}, u32[]{:S(2)}, u32[]{:S(2)}) collective-permute-start(f32[1,2,4,1,256]{4,2,3,1,0:T(4,128)S(1)} %get-tuple-element.82), channel_id=1, source_target_pairs={{1,0},{2,1},{3,2},{4,3},{5,4},{6,5},{7,6},{8,7},{9,8},{10,9},{11,1... | collective-permute-start | bytes 24584 | tf_op jit(solution)/shard_map/ppermute | solution.py:21
  94.2 3.0 %collective-permute-start.14 = (f32[1,2,4,1,256]{4,2,3,1,0:T(4,128)S(1)}, f32[1,2,4,1,256]{4,2,3,1,0:T(4,128)S(1)}, u32[]{:S(2)}, u32[]{:S(2)}) collective-permute-start(f32[1,2,4,1,256]{4,2,3,1,0:T(4,128)S(1)} %get-tuple-element.81), channel_id=1, source_target_pairs={{1,0},{2,1},{3,2},{4,3},{5,4},{6,5},{7,6},{8,7},{9,8},{10,9},{11,1... | collective-permute-start | bytes 24584 | tf_op jit(solution)/shard_map/ppermute | solution.py:21
  98.4 1.3 collective-permute-start.15
  99.7 1.5 collective-permute-start.16
  101.6 0.7 copy-done.7
  102.4 0.9 copy-done.6
  103.5 2.9 %collective-permute-done.15 = f32[1,2,1,32,256]{4,3,0,2,1:T(8,128)} collective-permute-done((f32[1,2,1,32,256]{4,3,0,2,1:T(8,128)}, f32[1,2,1,32,256]{4,3,0,2,1:T(8,128)}, u32[]{:S(2)}, u32[]{:S(2)}) %collective-permute-start.15) | collective-permute-done | bytes 65568 | tf_op jit(solution)/shard_map/ppermute | solution.py:21
  106.4 0.8 constant_dynamic-update-slice_fusion.11
  107.7 0.8 constant_dynamic-update-slice_fusion.10
  110.4 2.0 %fusion.1 = f32[2,3,4,32,256]{4,1,3,2,0:T(4,128)S(1)} fusion(f32[2,1,4,32,256]{4,1,3,2,0:T(1,128)S(1)} %stack.109, f32[2,1,4,32,256]{4,1,3,2,0:T(1,128)S(1)} %copy.503, f32[2,1,4,32,256]{4,1,3,2,0:T(1,128)S(1)} %copy.502, f32[2,1,4,32,256]{4,1,3,2,0:T(1,128)S(1)} %copy-done.5, f32[2,1,4,32,256]{4,1,3,2,0:T(1,128)S(1)} %copy-done.3, ...), kind=kLoop, calls=%fused_computation.12 | loop fusion | flops 1572864 | bytes 3145728 | tf_op jit(solution)/shard_map/sub | solution.py:107
  112.5 1.4 fusion.58
  114.0 1.9 %collective-permute-start.17 = (f32[1,2,4,1,256]{4,2,3,1,0:T(4,128)S(1)}, f32[1,2,4,1,256]{4,2,3,1,0:T(4,128)S(1)}, u32[]{:S(2)}, u32[]{:S(2)}) collective-permute-start(f32[1,2,4,1,256]{4,2,3,1,0:T(4,128)S(1)} %copy.505), channel_id=1, source_target_pairs={{0,1},{1,2},{2,3},{3,4},{4,5},{5,6},{6,7},{7,8},{8,9},{9,10},{10,1... | collective-permute-start | bytes 24584 | tf_op jit(solution)/shard_map/ppermute | solution.py:21
  115.9 0.7 fusion.59
  116.7 4.5 %collective-permute-start.18 = (f32[1,2,4,1,256]{4,2,3,1,0:T(4,128)S(1)}, f32[1,2,4,1,256]{4,2,3,1,0:T(4,128)S(1)}, u32[]{:S(2)}, u32[]{:S(2)}) collective-permute-start(f32[1,2,4,1,256]{4,2,3,1,0:T(4,128)S(1)} %copy.506), channel_id=1, source_target_pairs={{0,1},{1,2},{2,3},{3,4},{4,5},{5,6},{6,7},{7,8},{8,9},{9,10},{10,1... | collective-permute-start | bytes 24584 | tf_op jit(solution)/shard_map/ppermute | solution.py:21
  121.3 5.7 %collective-permute-start.20 = (f32[1,2,1,32,256]{4,1,3,2,0:T(2,128)}, f32[1,2,1,32,256]{4,1,3,2,0:T(2,128)S(1)}, u32[]{:S(2)}, u32[]{:S(2)}) collective-permute-start(f32[1,2,1,32,256]{4,1,3,2,0:T(2,128)} %get-tuple-element.63), channel_id=1, source_target_pairs={{0,16},{16,32},{32,48},{48,64},{64,80},{80,96},{96,112},{112,128},... | collective-permute-start | bytes 196616 | tf_op jit(solution)/shard_map/ppermute | solution.py:21
  127.0 3.3 %collective-permute-start.19 = (f32[1,2,1,32,256]{4,1,3,2,0:T(2,128)}, f32[1,2,1,32,256]{4,1,3,2,0:T(2,128)S(1)}, u32[]{:S(2)}, u32[]{:S(2)}) collective-permute-start(f32[1,2,1,32,256]{4,1,3,2,0:T(2,128)} %get-tuple-element.64), channel_id=1, source_target_pairs={{0,16},{16,32},{32,48},{48,64},{64,80},{80,96},{96,112},{112,128},... | collective-permute-start | bytes 196616 | tf_op jit(solution)/shard_map/ppermute | solution.py:21
  130.7 0.8 copy-done.8
  131.7 0.8 collective-permute-done.19
  133.6 0.8 fusion.3
  135.9 5.4 %collective-permute-start.21 = (f32[512]{0:T(512)S(1)}, f32[512]{0:T(512)S(1)}, u32[]{:S(2)}, u32[]{:S(2)}) collective-permute-start(f32[512]{0:T(512)S(1)} %reshape.68), channel_id=1, source_target_pairs={{0,16},{16,0},{32,48},{48,32},{64,80},{80,64},{96,112},{112,96},{1... | collective-permute-start | bytes 6152 | tf_op jit(solution)/shard_map/ppermute | solution.py:25
  141.3 1.5 collective-permute-done.21
  142.9 5.6 %collective-permute-start.22 = (f32[512]{0:T(512)S(1)}, f32[512]{0:T(512)S(1)}, u32[]{:S(2)}, u32[]{:S(2)}) collective-permute-start(f32[512]{0:T(512)S(1)} %collective-permute-done.21), channel_id=1, source_target_pairs={{0,32},{16,48},{32,0},{48,16},{64,96},{80,112},{96,64},{112,80},{1... | collective-permute-start | bytes 6152 | tf_op jit(solution)/shard_map/ppermute | solution.py:25
  148.5 1.5 collective-permute-done.22
  150.0 4.6 %collective-permute-start.23 = (f32[512]{0:T(512)S(1)}, f32[512]{0:T(512)S(1)}, u32[]{:S(2)}, u32[]{:S(2)}) collective-permute-start(f32[512]{0:T(512)S(1)} %collective-permute-done.22), channel_id=1, source_target_pairs={{0,64},{16,80},{32,96},{48,112},{64,0},{80,16},{96,32},{112,48},{1... | collective-permute-start | bytes 6152 | tf_op jit(solution)/shard_map/ppermute | solution.py:25
  154.6 1.8 collective-permute-done.23
  156.4 8.9 %collective-permute-start.24 = (f32[512]{0:T(512)S(1)}, f32[512]{0:T(512)S(1)}, u32[]{:S(2)}, u32[]{:S(2)}) collective-permute-start(f32[512]{0:T(512)S(1)} %collective-permute-done.23), channel_id=1, source_target_pairs={{0,128},{16,144},{32,160},{48,176},{64,192},{80,208},{96,224},{112... | collective-permute-start | bytes 6152 | tf_op jit(solution)/shard_map/ppermute | solution.py:25
  165.5 0.8 copy.523
  166.3 0.8 copy.521
  167.1 13.8 %collective-permute-start.25 = (f32[512]{0:T(512)S(1)}, f32[512]{0:T(512)S(1)}, u32[]{:S(2)}, u32[]{:S(2)}) collective-permute-start(f32[512]{0:T(512)S(1)} %collective-permute-done.24), channel_id=1, source_target_pairs={{0,256},{16,272},{32,288},{48,304},{64,320},{80,336},{96,352},{112... | collective-permute-start | bytes 6152 | tf_op jit(solution)/shard_map/ppermute | solution.py:25
  181.1 0.8 copy.522
  181.9 0.8 copy.520
  182.7 3.5 %gather_fusion.1 = f32[512]{0:T(512)S(1)} fusion(f32[512]{0:T(512)S(1)} %collective-permute-done.25, s32[1024]{0:T(1024)S(1)} %pad_clamp_fusion), kind=kCustom, calls=%fused_computation.1.clone | custom fusion | bytes 6144 | tf_op jit(solution)/shard_map/jit(_take)/gather | solution.py:128
  (146 shorter events, 17.6 us)
Async XLA Ops:
  0.6 0.9 copy-start.15
  1.6 8.5 %copy-start.10 = (f32[3,4,32,256]{3,2,1,0:T(8,128)S(1)}, f32[3,4,32,256]{3,2,1,0:T(8,128)}, u32[]{:S(2)}) copy-start(f32[3,4,32,256]{3,2,1,0:T(8,128)} %param.16) | copy-start | bytes 1179652
  1.6 14.4 %collective-permute-start = (f32[512]{0:T(512)S(1)}, f32[512]{0:T(512)S(1)}, u32[]{:S(2)}, u32[]{:S(2)}) collective-permute-start(f32[512]{0:T(512)S(1)} %reshape.65), channel_id=1, source_target_pairs={{0,16},{16,0},{32,48},{48,32},{64,80},{80,64},{96,112},{112,96},{1... | collective-permute-start | bytes 6152 | tf_op jit(solution)/shard_map/ppermute | solution.py:25
  6.2 49.8 %collective-permute-start.5 = (f32[1,2,4,1,256]{4,2,3,1,0:T(4,128)S(1)}, f32[1,2,4,1,256]{4,2,3,1,0:T(4,128)S(1)}, u32[]{:S(2)}, u32[]{:S(2)}) collective-permute-start(f32[1,2,4,1,256]{4,2,3,1,0:T(4,128)S(1)} %slice.261), channel_id=1, source_target_pairs={{1,0},{2,1},{3,2},{4,3},{5,4},{6,5},{7,6},{8,7},{9,8},{10,9},{11,1... | collective-permute-start | bytes 24584 | tf_op jit(solution)/shard_map/ppermute | solution.py:21
  8.8 54.8 %collective-permute-start.7 = (f32[1,2,1,32,256]{4,2,3,1,0:T(1,128)}, f32[1,2,1,32,256]{4,2,3,1,0:T(1,128)}, u32[]{:S(2)}, u32[]{:S(2)}) collective-permute-start(f32[1,2,1,32,256]{4,2,3,1,0:T(1,128)} %slice.349), channel_id=1, source_target_pairs={{16,0},{32,16},{48,32},{64,48},{80,64},{96,80},{112,96},{128,112},... | collective-permute-start | bytes 196616 | tf_op jit(solution)/shard_map/ppermute | solution.py:21
  10.4 45.7 %collective-permute-start.6 = (f32[1,2,4,1,256]{4,2,3,1,0:T(4,128)S(1)}, f32[1,2,4,1,256]{4,2,3,1,0:T(4,128)S(1)}, u32[]{:S(2)}, u32[]{:S(2)}) collective-permute-start(f32[1,2,4,1,256]{4,2,3,1,0:T(4,128)S(1)} %slice.262), channel_id=1, source_target_pairs={{1,0},{2,1},{3,2},{4,3},{5,4},{6,5},{7,6},{8,7},{9,8},{10,9},{11,1... | collective-permute-start | bytes 24584 | tf_op jit(solution)/shard_map/ppermute | solution.py:21
  13.7 50.8 %collective-permute-start.8 = (f32[1,2,1,32,256]{4,2,3,1,0:T(1,128)}, f32[1,2,1,32,256]{4,2,3,1,0:T(1,128)}, u32[]{:S(2)}, u32[]{:S(2)}) collective-permute-start(f32[1,2,1,32,256]{4,2,3,1,0:T(1,128)} %slice.350), channel_id=1, source_target_pairs={{16,0},{32,16},{48,32},{64,48},{80,64},{96,80},{112,96},{128,112},... | collective-permute-start | bytes 196616 | tf_op jit(solution)/shard_map/ppermute | solution.py:21
  15.2 0.7 copy-start.18
  16.0 8.5 %collective-permute-start.1 = (f32[512]{0:T(512)S(1)}, f32[512]{0:T(512)S(1)}, u32[]{:S(2)}, u32[]{:S(2)}) collective-permute-start(f32[512]{0:T(512)S(1)} %collective-permute-done), channel_id=1, source_target_pairs={{0,32},{16,48},{32,0},{48,16},{64,96},{80,112},{96,64},{112,80},{1... | collective-permute-start | bytes 6152 | tf_op jit(solution)/shard_map/ppermute | solution.py:25
  24.5 6.8 %collective-permute-start.2 = (f32[512]{0:T(512)S(1)}, f32[512]{0:T(512)S(1)}, u32[]{:S(2)}, u32[]{:S(2)}) collective-permute-start(f32[512]{0:T(512)S(1)} %collective-permute-done.1), channel_id=1, source_target_pairs={{0,64},{16,80},{32,96},{48,112},{64,0},{80,16},{96,32},{112,48},{1... | collective-permute-start | bytes 6152 | tf_op jit(solution)/shard_map/ppermute | solution.py:25
  31.3 10.6 %collective-permute-start.3 = (f32[512]{0:T(512)S(1)}, f32[512]{0:T(512)S(1)}, u32[]{:S(2)}, u32[]{:S(2)}) collective-permute-start(f32[512]{0:T(512)S(1)} %collective-permute-done.2), channel_id=1, source_target_pairs={{0,128},{16,144},{32,160},{48,176},{64,192},{80,208},{96,224},{112... | collective-permute-start | bytes 6152 | tf_op jit(solution)/shard_map/ppermute | solution.py:25
  42.0 15.6 %collective-permute-start.4 = (f32[512]{0:T(512)S(1)}, f32[512]{0:T(512)S(1)}, u32[]{:S(2)}, u32[]{:S(2)}) collective-permute-start(f32[512]{0:T(512)S(1)} %collective-permute-done.3), channel_id=1, source_target_pairs={{0,256},{16,272},{32,288},{48,304},{64,320},{80,336},{96,352},{112... | collective-permute-start | bytes 6152 | tf_op jit(solution)/shard_map/ppermute | solution.py:25
  61.1 0.7 copy-start.16
  65.9 0.7 copy-start
  66.2 0.7 copy-start.2
  66.9 1.2 copy-start.4
  69.4 0.7 copy-start.17
  70.7 17.3 %collective-permute-start.9 = (f32[1,2,4,1,256]{4,2,3,1,0:T(4,128)}, f32[1,2,4,1,256]{4,2,3,1,0:T(4,128)}, u32[]{:S(2)}, u32[]{:S(2)}) collective-permute-start(f32[1,2,4,1,256]{4,2,3,1,0:T(4,128)} %copy.486), channel_id=1, source_target_pairs={{0,1},{1,2},{2,3},{3,4},{4,5},{5,6},{6,7},{7,8},{8,9},{9,10},{10,1... | collective-permute-start | bytes 24584 | tf_op jit(solution)/shard_map/ppermute | solution.py:21
  75.3 13.4 %collective-permute-start.10 = (f32[1,2,4,1,256]{4,2,3,1,0:T(4,128)S(1)}, f32[1,2,4,1,256]{4,2,3,1,0:T(4,128)S(1)}, u32[]{:S(2)}, u32[]{:S(2)}) collective-permute-start(f32[1,2,4,1,256]{4,2,3,1,0:T(4,128)S(1)} %copy.487), channel_id=1, source_target_pairs={{0,1},{1,2},{2,3},{3,4},{4,5},{5,6},{6,7},{7,8},{8,9},{9,10},{10,1... | collective-permute-start | bytes 24584 | tf_op jit(solution)/shard_map/ppermute | solution.py:21
  79.9 0.8 copy-start.11
  79.9 4.7 %copy-start.12 = (f32[1,2,1,32,256]{4,1,3,2,0:T(2,128)S(1)}, f32[1,2,1,32,256]{4,1,3,2,0:T(2,128)}, u32[]{:S(2)}) copy-start(f32[1,2,1,32,256]{4,1,3,2,0:T(2,128)} %get-tuple-element.69) | copy-start | bytes 196612
  80.7 9.1 %collective-permute-start.12 = (f32[1,2,1,32,256]{4,1,3,2,0:T(2,128)S(1)}, f32[1,2,1,32,256]{4,1,3,2,0:T(2,128)S(1)}, u32[]{:S(2)}, u32[]{:S(2)}) collective-permute-start(f32[1,2,1,32,256]{4,1,3,2,0:T(2,128)S(1)} %copy-done.11), channel_id=1, source_target_pairs={{0,16},{16,32},{32,48},{48,64},{64,80},{80,96},{96,112},{112,128},... | collective-permute-start | bytes 196616 | tf_op jit(solution)/shard_map/ppermute | solution.py:21
  84.6 5.2 %collective-permute-start.11 = (f32[1,2,1,32,256]{4,1,3,2,0:T(2,128)S(1)}, f32[1,2,1,32,256]{4,1,3,2,0:T(2,128)S(1)}, u32[]{:S(2)}, u32[]{:S(2)}) collective-permute-start(f32[1,2,1,32,256]{4,1,3,2,0:T(2,128)S(1)} %copy-done.12), channel_id=1, source_target_pairs={{0,16},{16,32},{32,48},{48,64},{64,80},{80,96},{96,112},{112,128},... | collective-permute-start | bytes 196616 | tf_op jit(solution)/shard_map/ppermute | solution.py:21
  92.1 11.3 %collective-permute-start.13 = (f32[1,2,4,1,256]{4,2,3,1,0:T(4,128)S(1)}, f32[1,2,4,1,256]{4,2,3,1,0:T(4,128)S(1)}, u32[]{:S(2)}, u32[]{:S(2)}) collective-permute-start(f32[1,2,4,1,256]{4,2,3,1,0:T(4,128)S(1)} %get-tuple-element.82), channel_id=1, source_target_pairs={{1,0},{2,1},{3,2},{4,3},{5,4},{6,5},{7,6},{8,7},{9,8},{10,9},{11,1... | collective-permute-start | bytes 24584 | tf_op jit(solution)/shard_map/ppermute | solution.py:21
  94.2 9.2 %collective-permute-start.14 = (f32[1,2,4,1,256]{4,2,3,1,0:T(4,128)S(1)}, f32[1,2,4,1,256]{4,2,3,1,0:T(4,128)S(1)}, u32[]{:S(2)}, u32[]{:S(2)}) collective-permute-start(f32[1,2,4,1,256]{4,2,3,1,0:T(4,128)S(1)} %get-tuple-element.81), channel_id=1, source_target_pairs={{1,0},{2,1},{3,2},{4,3},{5,4},{6,5},{7,6},{8,7},{9,8},{10,9},{11,1... | collective-permute-start | bytes 24584 | tf_op jit(solution)/shard_map/ppermute | solution.py:21
  98.4 8.0 %collective-permute-start.15 = (f32[1,2,1,32,256]{4,3,0,2,1:T(8,128)}, f32[1,2,1,32,256]{4,3,0,2,1:T(8,128)}, u32[]{:S(2)}, u32[]{:S(2)}) collective-permute-start(f32[1,2,1,32,256]{4,3,0,2,1:T(8,128)} %copy.535), channel_id=1, source_target_pairs={{16,0},{32,16},{48,32},{64,48},{80,64},{96,80},{112,96},{128,112},... | collective-permute-start | bytes 196616 | tf_op jit(solution)/shard_map/ppermute | solution.py:21
  99.7 8.1 %collective-permute-start.16 = (f32[1,2,1,32,256]{4,3,0,2,1:T(8,128)}, f32[1,2,1,32,256]{4,3,0,2,1:T(8,128)}, u32[]{:S(2)}, u32[]{:S(2)}) collective-permute-start(f32[1,2,1,32,256]{4,3,0,2,1:T(8,128)} %copy.536), channel_id=1, source_target_pairs={{16,0},{32,16},{48,32},{64,48},{80,64},{96,80},{112,96},{128,112},... | collective-permute-start | bytes 196616 | tf_op jit(solution)/shard_map/ppermute | solution.py:21
  101.4 1.0 copy-start.7
  102.4 0.9 copy-start.6
  109.1 1.0 copy-start.5
  109.4 1.0 copy-start.1
  109.4 1.0 copy-start.3
  114.0 17.7 %collective-permute-start.17 = (f32[1,2,4,1,256]{4,2,3,1,0:T(4,128)S(1)}, f32[1,2,4,1,256]{4,2,3,1,0:T(4,128)S(1)}, u32[]{:S(2)}, u32[]{:S(2)}) collective-permute-start(f32[1,2,4,1,256]{4,2,3,1,0:T(4,128)S(1)} %copy.505), channel_id=1, source_target_pairs={{0,1},{1,2},{2,3},{3,4},{4,5},{5,6},{6,7},{7,8},{8,9},{9,10},{10,1... | collective-permute-start | bytes 24584 | tf_op jit(solution)/shard_map/ppermute | solution.py:21
  116.7 14.9 %collective-permute-start.18 = (f32[1,2,4,1,256]{4,2,3,1,0:T(4,128)S(1)}, f32[1,2,4,1,256]{4,2,3,1,0:T(4,128)S(1)}, u32[]{:S(2)}, u32[]{:S(2)}) collective-permute-start(f32[1,2,4,1,256]{4,2,3,1,0:T(4,128)S(1)} %copy.506), channel_id=1, source_target_pairs={{0,1},{1,2},{2,3},{3,4},{4,5},{5,6},{6,7},{7,8},{8,9},{9,10},{10,1... | collective-permute-start | bytes 24584 | tf_op jit(solution)/shard_map/ppermute | solution.py:21
  121.3 11.3 %collective-permute-start.20 = (f32[1,2,1,32,256]{4,1,3,2,0:T(2,128)}, f32[1,2,1,32,256]{4,1,3,2,0:T(2,128)S(1)}, u32[]{:S(2)}, u32[]{:S(2)}) collective-permute-start(f32[1,2,1,32,256]{4,1,3,2,0:T(2,128)} %get-tuple-element.63), channel_id=1, source_target_pairs={{0,16},{16,32},{32,48},{48,64},{64,80},{80,96},{96,112},{112,128},... | collective-permute-start | bytes 196616 | tf_op jit(solution)/shard_map/ppermute | solution.py:21
  127.0 5.5 %collective-permute-start.19 = (f32[1,2,1,32,256]{4,1,3,2,0:T(2,128)}, f32[1,2,1,32,256]{4,1,3,2,0:T(2,128)S(1)}, u32[]{:S(2)}, u32[]{:S(2)}) collective-permute-start(f32[1,2,1,32,256]{4,1,3,2,0:T(2,128)} %get-tuple-element.64), channel_id=1, source_target_pairs={{0,16},{16,32},{32,48},{48,64},{64,80},{80,96},{96,112},{112,128},... | collective-permute-start | bytes 196616 | tf_op jit(solution)/shard_map/ppermute | solution.py:21
  130.5 1.0 copy-start.8
  132.7 0.9 copy-start.9
  134.9 0.8 copy-start.13
  134.9 0.8 copy-start.14
  135.9 7.0 %collective-permute-start.21 = (f32[512]{0:T(512)S(1)}, f32[512]{0:T(512)S(1)}, u32[]{:S(2)}, u32[]{:S(2)}) collective-permute-start(f32[512]{0:T(512)S(1)} %reshape.68), channel_id=1, source_target_pairs={{0,16},{16,0},{32,48},{48,32},{64,80},{80,64},{96,112},{112,96},{1... | collective-permute-start | bytes 6152 | tf_op jit(solution)/shard_map/ppermute | solution.py:25
  142.9 7.2 %collective-permute-start.22 = (f32[512]{0:T(512)S(1)}, f32[512]{0:T(512)S(1)}, u32[]{:S(2)}, u32[]{:S(2)}) collective-permute-start(f32[512]{0:T(512)S(1)} %collective-permute-done.21), channel_id=1, source_target_pairs={{0,32},{16,48},{32,0},{48,16},{64,96},{80,112},{96,64},{112,80},{1... | collective-permute-start | bytes 6152 | tf_op jit(solution)/shard_map/ppermute | solution.py:25
  150.0 6.4 %collective-permute-start.23 = (f32[512]{0:T(512)S(1)}, f32[512]{0:T(512)S(1)}, u32[]{:S(2)}, u32[]{:S(2)}) collective-permute-start(f32[512]{0:T(512)S(1)} %collective-permute-done.22), channel_id=1, source_target_pairs={{0,64},{16,80},{32,96},{48,112},{64,0},{80,16},{96,32},{112,48},{1... | collective-permute-start | bytes 6152 | tf_op jit(solution)/shard_map/ppermute | solution.py:25
  156.4 10.7 %collective-permute-start.24 = (f32[512]{0:T(512)S(1)}, f32[512]{0:T(512)S(1)}, u32[]{:S(2)}, u32[]{:S(2)}) collective-permute-start(f32[512]{0:T(512)S(1)} %collective-permute-done.23), channel_id=1, source_target_pairs={{0,128},{16,144},{32,160},{48,176},{64,192},{80,208},{96,224},{112... | collective-permute-start | bytes 6152 | tf_op jit(solution)/shard_map/ppermute | solution.py:25
  167.1 15.6 %collective-permute-start.25 = (f32[512]{0:T(512)S(1)}, f32[512]{0:T(512)S(1)}, u32[]{:S(2)}, u32[]{:S(2)}) collective-permute-start(f32[512]{0:T(512)S(1)} %collective-permute-done.24), channel_id=1, source_target_pairs={{0,256},{16,272},{32,288},{48,304},{64,320},{80,336},{96,352},{112... | collective-permute-start | bytes 6152 | tf_op jit(solution)/shard_map/ppermute | solution.py:25
where the time goes:
time: 188 us; the launch traced here: 187 us
  starting transfers between devices  121 us (64%)
  local copies, waits for them, and re-layouts  41 us (22%)
  waiting for transfers between devices  14.9 us (8%)
  other arithmetic  8.51 us (5%)
    ppermute x10, starting transfers between devices, swapped(): lax.ppermute(value, axis, [(i, i ^ 1 << bit) for i in range(lax.axis_size...  77 us
    ppermute x16, starting transfers between devices, shifted(): return lax.ppermute(block, axis, route)  43.9 us
    unnamed x64, local copies, waits for them, and re-layouts  17.2 us
    ppermute x10, waiting for transfers between devices, swapped(): lax.ppermute(value, axis, [(i, i ^ 1 << bit) for i in range(lax.axis_size...  9.54 us
    ppermute x16, waiting for transfers between devices, shifted(): return lax.ppermute(block, axis, route)  5.34 us
    slice x8, local copies, waits for them, and re-layouts, per_device(): magnetic[which:which + 1, 0::2, :, -1:]  3.96 us
  transfers between devices with their start and end apart: 26, of which 11 were waited for; matrix products, arithmetic and copies ran while one was open for 12% of the time, Pallas kernels for 0%

commit v1 on v0

v1 whole, which is shorter than its diff:
```python
import math

import jax
import jax.numpy as jnp
from jax import lax
from jax.experimental import pallas as pl
from jax.experimental.pallas import tpu as pltpu
from jax.sharding import PartitionSpec as P

PLANES = 4
Z0 = 126
COURANT = 0.5
OMEGA = 0.7
CONTRAST = 10.0
F32 = jnp.float32
VMEM_LIMIT = 24 * 1024 * 1024


def up_y(a, row):
    n = a.shape[0]
    at = lax.broadcasted_iota(jnp.int32, a.shape, 0)
    return jnp.where(at == n - 1, row, pltpu.roll(a, n - 1, 0))


def up_z(a):
    n = a.shape[1]
    at = lax.broadcasted_iota(jnp.int32, a.shape, 1)
    return jnp.where(at == n - 1, 0.0, pltpu.roll(a, n - 1, 1))


def down_y(a, row):
    at = lax.broadcasted_iota(jnp.int32, a.shape, 0)
    return jnp.where(at == 0, row, pltpu.roll(a, 1, 0))


def down_z(a):
    at = lax.broadcasted_iota(jnp.int32, a.shape, 1)
    return jnp.where(at == 0, 0.0, pltpu.roll(a, 1, 1))


def pick_z(nz):
    plane = lax.broadcasted_iota(jnp.int32, (8, nz), 0)
    z = lax.broadcasted_iota(jnp.int32, (8, nz), 1)
    return jnp.where((z == plane + Z0) & (plane < PLANES), 1.0, 0.0).astype(F32)


def face_low(ef, ea, xpay, ypay):
    nx = ef.shape[1]
    for f, e in enumerate((ef, ea)):
        for k, c in enumerate((1, 2)):
            xpay[f, k] = e[c, 0]
        for k, c in enumerate((0, 2)):
            for x in range(nx):
                r = (f * 2 + k) * nx + x
                ypay[pl.ds(r, 1), :] = e[c, x, pl.ds(0, 1), :]


def magnetic_kernel(ef, ea, hf, ha, xin, yin, of, oa, xpay, ypay):
    nx, ny = ef.shape[1], ef.shape[2]
    for f, (e, h, o) in enumerate(((ef, hf, of), (ea, ha, oa))):
        for x in range(nx):
            ex, ey, ez = e[0, x], e[1, x], e[2, x]
            ey_n = e[1, x + 1] if x + 1 < nx else xin[f, 0]
            ez_n = e[2, x + 1] if x + 1 < nx else xin[f, 1]
            row_x = yin[pl.ds((f * 2) * nx + x, 1), :]
            row_z = yin[pl.ds((f * 2 + 1) * nx + x, 1), :]
            hx = h[0, x] - COURANT * ((up_y(ez, row_z) - ez) - (up_z(ey) - ey))
            hy = h[1, x] - COURANT * ((up_z(ex) - ex) - (ez_n - ez))
            hz = h[2, x] - COURANT * ((ey_n - ey) - (up_y(ex, row_x) - ex))
            o[0, x] = hx
            o[1, x] = hy
            o[2, x] = hz
            if x == nx - 1:
                xpay[f, 0] = hy
                xpay[f, 1] = hz
            ypay[pl.ds((f * 2) * nx + x, 1), :] = hx[ny - 1:, :]
            ypay[pl.ds((f * 2 + 1) * nx + x, 1), :] = hz[ny - 1:, :]


def electric_step(ef, ea, hf, ha, coef, xin, yin, of, oa):
    nx = ef.shape[1]
    for f, (e, h, o) in enumerate(((ef, hf, of), (ea, ha, oa))):
        for x in range(nx):
            hx, hy, hz = h[0, x], h[1, x], h[2, x]
            hy_p = h[1, x - 1] if x else xin[f, 0]
            hz_p = h[2, x - 1] if x else xin[f, 1]
            row_x = yin[pl.ds((f * 2) * nx + x, 1), :]
            row_z = yin[pl.ds((f * 2 + 1) * nx + x, 1), :]
            k = coef[x]
            o[0, x] = e[0, x] + k * ((hz - down_y(hz, row_z)) - (hy - down_z(hy)))
            o[1, x] = e[1, x] + k * ((hx - down_z(hx)) - (hz - hz_p))
            o[2, x] = e[2, x] + k * ((hy - hy_p) - (hx - down_y(hx, row_x)))


def electric_kernel(ef, ea, hf, ha, coef, xin, yin, of, oa, xpay, ypay):
    electric_step(ef, ea, hf, ha, coef, xin, yin, of, oa)
    face_low(of, oa, xpay, ypay)


def slab_of(e, c, x, pick):
    return lax.dot_general(pick, e[c, x], (((1,), (1,)), ((), ())),
                           precision=lax.Precision.HIGHEST,
                           preferred_element_type=F32)[:PLANES]


def last_kernel(ef, ea, hf, ha, coef, xin, yin, mask, mon_f, mon_a, of, oa, grad):
    nx, nz = ef.shape[1], ef.shape[3]
    electric_step(ef, ea, hf, ha, coef, xin, yin, of, oa)
    pick = pick_z(nz)
    for x in range(nx):
        total = None
        for c in range(3):
            one_f, two_f = slab_of(ef, c, x, pick), slab_of(of, c, x, pick)
            one_a, two_a = slab_of(ea, c, x, pick), slab_of(oa, c, x, pick)
            cos = [math.cos(OMEGA), math.cos(2 * OMEGA)]
            sin = [math.sin(OMEGA), math.sin(2 * OMEGA)]
            re_f = mon_f[0, c, :, x, :] + cos[0] * one_f + cos[1] * two_f
            im_f = mon_f[1, c, :, x, :] - sin[0] * one_f - sin[1] * two_f
            re_a = mon_a[0, c, :, x, :] + cos[0] * one_a + cos[1] * two_a
            im_a = mon_a[1, c, :, x, :] - sin[0] * one_a - sin[1] * two_a
            term = re_f * re_a - im_f * im_a
            total = term if total is None else total + term
        grad[:, x, :] = CONTRAST * mask[:, x, :].astype(F32) * total


def mirror_take(other, partner, rows, index):
    planes, nx, ny = other.shape
    rows[...] = jnp.zeros_like(rows)
    index[...] = jnp.zeros_like(index)
    for p in range(planes):
        rows[pl.ds(p * nx, nx), pl.ds(0, ny)] = other[p]
        index[pl.ds(p * nx, nx), pl.ds(0, ny)] = partner[p]
    at = index[...]
    row, lane = at // ny, at % ny
    got = jnp.zeros(at.shape, F32)
    for r in range(planes * nx):
        line = jnp.broadcast_to(rows[pl.ds(r, 1), :], at.shape)
        got = jnp.where(row == r, jnp.take_along_axis(line, lane, axis=1), got)
    return got


def coef_kernel(eps, density, mask, partner, other, coef, rows, index):
    nx, ny, nz = eps.shape
    got = mirror_take(other, partner, rows, index)
    rows[...] = got
    pick = pick_z(nz)[:PLANES]
    for x in range(nx):
        theirs = jnp.concatenate([rows[pl.ds(p * nx + x, 1), pl.ds(0, ny)] for p in range(PLANES)], 0)
        sym = 0.5 * (density[:, x, :] + theirs)
        extra = CONTRAST * mask[:, x, :].astype(F32) * sym
        spread = lax.dot_general(extra, pick, (((0,), (0,)), ((), ())),
                                 precision=lax.Precision.HIGHEST, preferred_element_type=F32)
        coef[x] = COURANT / (eps[x] + spread)


def gradient_kernel(grad, partner, other, out, rows, index):
    nx, ny = grad.shape[1], grad.shape[2]
    got = mirror_take(other, partner, rows, index)
    rows[...] = got
    for p in range(PLANES):
        out[p] = 0.5 * (grad[p] + rows[pl.ds(p * nx, nx), pl.ds(0, ny)])


def call(kernel, outs, args, scratch=(), name=None, nbytes=4_000_000, flops=4_000_000):
    return pl.pallas_call(
        kernel,
        out_shape=outs,
        in_specs=[pl.BlockSpec(memory_space=pltpu.VMEM)] * len(args),
        out_specs=[pl.BlockSpec(memory_space=pltpu.VMEM)] * len(outs),
        scratch_shapes=list(scratch),
        compiler_params=pltpu.CompilerParams(vmem_limit_bytes=VMEM_LIMIT),
        cost_estimate=pl.CostEstimate(flops=flops, bytes_accessed=nbytes, transcendentals=0),
        name=name,
    )(*args)


def shifted(block, axis, distance):
    devices = range(lax.axis_size(axis))
    return lax.ppermute(block, axis, [(i - distance, i) for i in devices if i - distance in devices])


def mirrored(block, axis):
    size = lax.axis_size(axis)
    return lax.ppermute(block, axis, [(i, size - 1 - i) for i in range(size)])


def per_device(e_fwd, h_fwd, e_adj, h_adj, eps_back, density, design_mask, partner_map, mon_fwd, mon_adj):
    _, nx, ny, nz = e_fwd.shape
    field = jax.ShapeDtypeStruct(e_fwd.shape, F32)
    xface = jax.ShapeDtypeStruct((2, 2, ny, nz), F32)
    yface = jax.ShapeDtypeStruct((4 * nx, nz), F32)
    slab = jax.ShapeDtypeStruct(density.shape, F32)
    picks = [pltpu.VMEM((PLANES * nx, 128), F32), pltpu.VMEM((PLANES * nx, 128), jnp.int32)]

    other = mirrored(density, "gx")

    xpay, ypay = call(face_low, [xface, yface], [e_fwd, e_adj], name="faces")
    yin, xin = shifted(ypay, "gy", -1), shifted(xpay, "gx", -1)
    hf, ha, xpay, ypay = call(magnetic_kernel, [field, field, xface, yface],
                              [e_fwd, e_adj, h_fwd, h_adj, xin, yin], name="magnetic_1")
    yin, xin = shifted(ypay, "gy", 1), shifted(xpay, "gx", 1)
    coef, = call(coef_kernel, [jax.ShapeDtypeStruct(eps_back.shape, F32)],
                 [eps_back, density, design_mask, partner_map, other], picks, name="coefficient")
    ef, ea, xpay, ypay = call(electric_kernel, [field, field, xface, yface],
                              [e_fwd, e_adj, hf, ha, coef, xin, yin], name="electric_1")
    yin, xin = shifted(ypay, "gy", -1), shifted(xpay, "gx", -1)
    hf, ha, xpay, ypay = call(magnetic_kernel, [field, field, xface, yface],
                              [ef, ea, hf, ha, xin, yin], name="magnetic_2")
    yin, xin = shifted(ypay, "gy", 1), shifted(xpay, "gx", 1)
    ef, ea, grad = call(last_kernel, [field, field, slab],
                        [ef, ea, hf, ha, coef, xin, yin, design_mask, mon_fwd, mon_adj], name="electric_2")
    theirs = mirrored(grad, "gx")
    density_grad, = call(gradient_kernel, [slab], [grad, partner_map, theirs], picks, name="gradient")
    return ef, hf, ea, ha, density_grad


def solution(mesh):
    grid = P(None, "gx", "gy", None)
    slab = P(None, "gx", "gy")
    monitor = P(None, None, None, "gx", "gy")
    return jax.shard_map(
        per_device,
        mesh=mesh,
        in_specs=(grid, grid, grid, grid, P("gx", "gy", None), slab, slab, slab, monitor, monitor),
        out_specs=(grid, grid, grid, grid, slab),
        check_vma=False,
    )
```

time: 188 us -> 74.4 us (0.40)
  the two profiles are of different devices: /device:TPU:20 before, /device:TPU:134 now
where the time goes in v1:
time: 74.4 us; the launch traced here: 73.9 us
  starting transfers between devices  52.3 us (70%)
  waiting for transfers between devices  11.9 us (16%)
  Pallas kernels  4.74 us (6%)
  local copies, waits for them, and re-layouts  4.02 us (5%)
  between operations  0.84 us (1%)
    ppermute x2, starting transfers between devices, mirrored(): return lax.ppermute(block, axis, [(i, size - 1 - i) for i in range(size)])  27 us
    ppermute x8, starting transfers between devices, shifted(): lax.ppermute(block, axis, [(i - distance, i) for i in devices if i - dist...  25.3 us
    ppermute x8, waiting for transfers between devices, shifted(): lax.ppermute(block, axis, [(i - distance, i) for i in devices if i - dist...  8.7 us
    pallas_call x7, Pallas kernels, call(): pl.pallas_call(kernel, out_shape=outs, in_specs=[pl.BlockSpec(memory_spac...  4.74 us
    unnamed x26, local copies, waits for them, and re-layouts  4.02 us
    ppermute x2, waiting for transfers between devices, mirrored(): return lax.ppermute(block, axis, [(i, size - 1 - i) for i in range(size)])  3.23 us
  transfers between devices with their start and end apart: 10, of which 5 were waited for; matrix products, arithmetic and copies ran while one was open for 0% of the time, Pallas kernels for 1%

profile of v1, /device:TPU:134, one launch (start us, length us, event | category | flops | bytes accessed | tf_op | source)
XLA Modules:
  0.0 73.9 jit_solution(4412628746773796704)
XLA Ops:
  0.6 0.0 copy-start
  0.6 1.0 %copy-done = f32[3,4,32,256]{3,2,1,0:T(8,128)S(1)} copy-done((f32[3,4,32,256]{3,2,1,0:T(8,128)S(1)}, f32[3,4,32,256]{3,2,1,0:T(8,128)}, u32[]{:S(2)}) %copy-start) | copy-done | bytes 393240
  1.6 0.0 copy-start.2
  1.6 1.0 %copy-done.2 = f32[3,4,32,256]{3,2,1,0:T(8,128)S(1)} copy-done((f32[3,4,32,256]{3,2,1,0:T(8,128)S(1)}, f32[3,4,32,256]{3,2,1,0:T(8,128)}, u32[]{:S(2)}) %copy-start.2) | copy-done | bytes 393240
  2.6 0.0 copy-start.3
  2.6 0.0 copy-start.4
  2.7 3.2 %collective-permute-start = (f32[2,2,32,256]{3,2,1,0:T(8,128)S(1)}, f32[2,2,32,256]{3,2,1,0:T(8,128)S(1)}, u32[]{:S(2)}, u32[]{:S(2)}) collective-permute-start(f32[2,2,32,256]{3,2,1,0:T(8,128)S(1)} %get-tuple-element.22), channel_id=1, source_target_pairs={{16,0},{32,16},{48,32},{64,48},{80,64},{96,80},{112,96},{128,112},... | collective-permute-start | bytes 393224 | tf_op jit(solution)/shard_map/ppermute | solution.py:179
  5.8 0.0 copy-start.12
  5.8 0.0 copy-start.7
  5.8 4.4 %collective-permute-start.1 = (f32[16,256]{1,0:T(8,128)S(1)}, f32[16,256]{1,0:T(8,128)S(1)}, u32[]{:S(2)}, u32[]{:S(2)}) collective-permute-start(f32[16,256]{1,0:T(8,128)S(1)} %get-tuple-element.23), channel_id=1, source_target_pairs={{1,0},{2,1},{3,2},{4,3},{5,4},{6,5},{7,6},{8,7},{9,8},{10,9},{11,1... | collective-permute-start | bytes 49160 | tf_op jit(solution)/shard_map/ppermute | solution.py:179
  10.2 1.4 %collective-permute-done.1.yin = f32[16,256]{1,0:T(8,128)S(1)} collective-permute-done((f32[16,256]{1,0:T(8,128)S(1)}, f32[16,256]{1,0:T(8,128)S(1)}, u32[]{:S(2)}, u32[]{:S(2)}) %collective-permute-start.1) | collective-permute-done | bytes 16416 | tf_op jit(solution)/shard_map/ppermute | solution.py:179
  11.6 0.0 collective-permute-done.xin
  11.6 0.0 copy-done.3
  11.6 0.0 copy-done.4
  11.6 0.0 copy-start.10
  11.7 0.0 copy-start.11
  11.7 0.0 copy-start.1
  11.7 0.2 magnetic_1.1
  11.9 2.6 %collective-permute-start.3 = (f32[2,2,32,256]{3,2,1,0:T(8,128)S(1)}, f32[2,2,32,256]{3,2,1,0:T(8,128)S(1)}, u32[]{:S(2)}, u32[]{:S(2)}) collective-permute-start(f32[2,2,32,256]{3,2,1,0:T(8,128)S(1)} %get-tuple-element.26), channel_id=1, source_target_pairs={{0,16},{16,32},{32,48},{48,64},{64,80},{80,96},{96,112},{112,128},... | collective-permute-start | bytes 393224 | tf_op jit(solution)/shard_map/ppermute | solution.py:179
  14.6 2.8 %collective-permute-start.4 = (f32[16,256]{1,0:T(8,128)S(1)}, f32[16,256]{1,0:T(8,128)S(1)}, u32[]{:S(2)}, u32[]{:S(2)}) collective-permute-start(f32[16,256]{1,0:T(8,128)S(1)} %get-tuple-element.27), channel_id=1, source_target_pairs={{0,1},{1,2},{2,3},{3,4},{4,5},{5,6},{6,7},{7,8},{8,9},{9,10},{10,1... | collective-permute-start | bytes 49160 | tf_op jit(solution)/shard_map/ppermute | solution.py:179
  17.4 0.0 copy-done.12
  17.4 13.3 %collective-permute-start.2 = (f32[4,4,32]{2,1,0:T(4,128)S(1)}, f32[4,4,32]{2,1,0:T(4,128)S(1)}, u32[]{:S(2)}, u32[]{:S(2)}) collective-permute-start(f32[4,4,32]{2,1,0:T(4,128)S(1)} %copy-done.12), channel_id=1, source_target_pairs={{0,496},{16,480},{32,464},{48,448},{64,432},{80,416},{96,400},{112... | collective-permute-start | bytes 6152 | tf_op jit(solution)/shard_map/ppermute | solution.py:184
  30.7 1.6 %collective-permute-done.2.other = f32[4,4,32]{2,1,0:T(4,128)S(1)} collective-permute-done((f32[4,4,32]{2,1,0:T(4,128)S(1)}, f32[4,4,32]{2,1,0:T(4,128)S(1)}, u32[]{:S(2)}, u32[]{:S(2)}) %collective-permute-start.2) | collective-permute-done | bytes 2080 | tf_op jit(solution)/shard_map/ppermute | solution.py:184
  32.3 0.0 copy-done.7
  32.3 0.0 copy-done.10
  32.3 0.0 copy-done.11
  32.3 0.5 coefficient.1.coef
  32.7 0.0 collective-permute-done.4.yin
  32.8 0.0 collective-permute-done.3.xin
  32.8 0.0 copy-done.1
  32.8 0.3 electric_1.1
  33.0 3.9 %collective-permute-start.5 = (f32[2,2,32,256]{3,2,1,0:T(8,128)S(1)}, f32[2,2,32,256]{3,2,1,0:T(8,128)S(1)}, u32[]{:S(2)}, u32[]{:S(2)}) collective-permute-start(f32[2,2,32,256]{3,2,1,0:T(8,128)S(1)} %get-tuple-element.30), channel_id=1, source_target_pairs={{16,0},{32,16},{48,32},{64,48},{80,64},{96,80},{112,96},{128,112},... | collective-permute-start | bytes 393224 | tf_op jit(solution)/shard_map/ppermute | solution.py:179
  37.0 4.2 %collective-permute-start.6 = (f32[16,256]{1,0:T(8,128)S(1)}, f32[16,256]{1,0:T(8,128)S(1)}, u32[]{:S(2)}, u32[]{:S(2)}) collective-permute-start(f32[16,256]{1,0:T(8,128)S(1)} %get-tuple-element.31), channel_id=1, source_target_pairs={{1,0},{2,1},{3,2},{4,3},{5,4},{6,5},{7,6},{8,7},{9,8},{10,9},{11,1... | collective-permute-start | bytes 49160 | tf_op jit(solution)/shard_map/ppermute | solution.py:179
  41.2 1.4 %collective-permute-done.6.yin = f32[16,256]{1,0:T(8,128)S(1)} collective-permute-done((f32[16,256]{1,0:T(8,128)S(1)}, f32[16,256]{1,0:T(8,128)S(1)}, u32[]{:S(2)}, u32[]{:S(2)}) %collective-permute-start.6) | collective-permute-done | bytes 16416 | tf_op jit(solution)/shard_map/ppermute | solution.py:179
  42.6 0.0 collective-permute-done.5.xin
  42.6 0.0 copy-start.8
  42.6 0.0 copy-start.9
  42.6 1.0 %magnetic_2.1 = (f32[3,4,32,256]{3,2,1,0:T(8,128)}, f32[3,4,32,256]{3,2,1,0:T(8,128)}, f32[2,2,32,256]{3,2,1,0:T(8,128)S(1)}, f32[16,256]{1,0:T(8,128)S(1)}) custom-call(f32[3,4,32,256]{3,2,1,0:T(8,128)S(1)} %get-tuple-element.28.ef, f32[3,4,32,256]{3,2,1,0:T(8,128)S(1)} %get-tuple-element.29.ea, f32[3,4,32,256]{3,2,1,0:T(8,128)S(1)} %get-tuple-element.24.hf, ...), custom_call_target="tpu_custom_call" | custom-call | flops 4000000 | bytes 4000000 | tf_op jit(solution)/shard_map/magnetic_2/pallas_call | solution.py:165
  43.7 2.3 %collective-permute-start.7 = (f32[2,2,32,256]{3,2,1,0:T(8,128)S(1)}, f32[2,2,32,256]{3,2,1,0:T(8,128)S(1)}, u32[]{:S(2)}, u32[]{:S(2)}) collective-permute-start(f32[2,2,32,256]{3,2,1,0:T(8,128)S(1)} %get-tuple-element.34), channel_id=1, source_target_pairs={{0,16},{16,32},{32,48},{48,64},{64,80},{80,96},{96,112},{112,128},... | collective-permute-start | bytes 393224 | tf_op jit(solution)/shard_map/ppermute | solution.py:179
  46.0 1.9 %collective-permute-start.8 = (f32[16,256]{1,0:T(8,128)S(1)}, f32[16,256]{1,0:T(8,128)S(1)}, u32[]{:S(2)}, u32[]{:S(2)}) collective-permute-start(f32[16,256]{1,0:T(8,128)S(1)} %get-tuple-element.35), channel_id=1, source_target_pairs={{0,1},{1,2},{2,3},{3,4},{4,5},{5,6},{6,7},{7,8},{8,9},{9,10},{10,1... | collective-permute-start | bytes 49160 | tf_op jit(solution)/shard_map/ppermute | solution.py:179
  47.9 5.8 %collective-permute-done.8.yin = f32[16,256]{1,0:T(8,128)S(1)} collective-permute-done((f32[16,256]{1,0:T(8,128)S(1)}, f32[16,256]{1,0:T(8,128)S(1)}, u32[]{:S(2)}, u32[]{:S(2)}) %collective-permute-start.8) | collective-permute-done | bytes 16416 | tf_op jit(solution)/shard_map/ppermute | solution.py:179
  53.7 0.0 collective-permute-done.7.xin
  53.7 0.0 copy-done.8
  53.7 0.0 copy-done.9
  53.7 0.0 copy-start.5
  53.8 1.0 %copy-done.5 = f32[3,4,32,256]{3,2,1,0:T(8,128)S(1)} copy-done((f32[3,4,32,256]{3,2,1,0:T(8,128)S(1)}, f32[3,4,32,256]{3,2,1,0:T(8,128)}, u32[]{:S(2)}) %copy-start.5) | copy-done | bytes 393240
  54.7 0.0 copy-start.6
  54.7 1.0 %copy-done.6 = f32[3,4,32,256]{3,2,1,0:T(8,128)S(1)} copy-done((f32[3,4,32,256]{3,2,1,0:T(8,128)S(1)}, f32[3,4,32,256]{3,2,1,0:T(8,128)}, u32[]{:S(2)}) %copy-start.6) | copy-done | bytes 393240
  55.7 2.0 %electric_2.1 = (f32[3,4,32,256]{3,2,1,0:T(8,128)}, f32[3,4,32,256]{3,2,1,0:T(8,128)}, f32[4,4,32]{2,1,0:T(4,128)S(1)}) custom-call(f32[3,4,32,256]{3,2,1,0:T(8,128)S(1)} %get-tuple-element.28.ef, f32[3,4,32,256]{3,2,1,0:T(8,128)S(1)} %get-tuple-element.29.ea, f32[3,4,32,256]{3,2,1,0:T(8,128)S(1)} %copy-done.5, f32[3,4,32,256]{3,2,1,0:T(8,128)S(1)} %copy-done.6, ...), custom_call_target="tpu_custom_call" | custom-call | flops 4000000 | bytes 4000000 | tf_op jit(solution)/shard_map/electric_2/pallas_call | solution.py:165
  57.7 13.8 %collective-permute-start.9 = (f32[4,4,32]{2,1,0:T(4,128)S(1)}, f32[4,4,32]{2,1,0:T(4,128)S(1)}, u32[]{:S(2)}, u32[]{:S(2)}) collective-permute-start(f32[4,4,32]{2,1,0:T(4,128)S(1)} %get-tuple-element.38.grad), channel_id=1, source_target_pairs={{0,496},{16,480},{32,464},{48,448},{64,432},{80,416},{96,400},{112... | collective-permute-start | bytes 6152 | tf_op jit(solution)/shard_map/ppermute | solution.py:184
  71.5 1.6 %collective-permute-done.9.other = f32[4,4,32]{2,1,0:T(4,128)S(1)} collective-permute-done((f32[4,4,32]{2,1,0:T(4,128)S(1)}, f32[4,4,32]{2,1,0:T(4,128)S(1)}, u32[]{:S(2)}, u32[]{:S(2)}) %collective-permute-start.9) | collective-permute-done | bytes 2080 | tf_op jit(solution)/shard_map/ppermute | solution.py:184
  73.1 0.7 gradient.1
  (1 shorter events, 0.0 us)
Async XLA Ops:
  0.6 1.0 %copy-start = (f32[3,4,32,256]{3,2,1,0:T(8,128)S(1)}, f32[3,4,32,256]{3,2,1,0:T(8,128)}, u32[]{:S(2)}) copy-start(f32[3,4,32,256]{3,2,1,0:T(8,128)} %ef.5) | copy-start | bytes 1179652
  1.6 1.0 %copy-start.2 = (f32[3,4,32,256]{3,2,1,0:T(8,128)S(1)}, f32[3,4,32,256]{3,2,1,0:T(8,128)}, u32[]{:S(2)}) copy-start(f32[3,4,32,256]{3,2,1,0:T(8,128)} %ea.5) | copy-start | bytes 1179652
  2.6 9.0 %copy-start.3 = (f32[3,4,32,256]{3,2,1,0:T(8,128)S(1)}, f32[3,4,32,256]{3,2,1,0:T(8,128)}, u32[]{:S(2)}) copy-start(f32[3,4,32,256]{3,2,1,0:T(8,128)} %hf.1) | copy-start | bytes 1179652
  2.6 9.0 %copy-start.4 = (f32[3,4,32,256]{3,2,1,0:T(8,128)S(1)}, f32[3,4,32,256]{3,2,1,0:T(8,128)}, u32[]{:S(2)}) copy-start(f32[3,4,32,256]{3,2,1,0:T(8,128)} %ha.1) | copy-start | bytes 1179652
  2.7 9.0 %collective-permute-start = (f32[2,2,32,256]{3,2,1,0:T(8,128)S(1)}, f32[2,2,32,256]{3,2,1,0:T(8,128)S(1)}, u32[]{:S(2)}, u32[]{:S(2)}) collective-permute-start(f32[2,2,32,256]{3,2,1,0:T(8,128)S(1)} %get-tuple-element.22), channel_id=1, source_target_pairs={{16,0},{32,16},{48,32},{64,48},{80,64},{96,80},{112,96},{128,112},... | collective-permute-start | bytes 393224 | tf_op jit(solution)/shard_map/ppermute | solution.py:179
  5.8 11.6 %copy-start.12 = (f32[4,4,32]{2,1,0:T(4,128)S(1)}, f32[4,4,32]{2,1,0:T(4,128)}, u32[]{:S(2)}) copy-start(f32[4,4,32]{2,1,0:T(4,128)} %density.1) | copy-start | bytes 6148
  5.8 26.4 %copy-start.7 = (f32[4,32,256]{2,1,0:T(8,128)S(1)}, f32[4,32,256]{2,1,0:T(8,128)}, u32[]{:S(2)}) copy-start(f32[4,32,256]{2,1,0:T(8,128)} %eps.1) | copy-start | bytes 393220
  5.8 5.8 %collective-permute-start.1 = (f32[16,256]{1,0:T(8,128)S(1)}, f32[16,256]{1,0:T(8,128)S(1)}, u32[]{:S(2)}, u32[]{:S(2)}) collective-permute-start(f32[16,256]{1,0:T(8,128)S(1)} %get-tuple-element.23), channel_id=1, source_target_pairs={{1,0},{2,1},{3,2},{4,3},{5,4},{6,5},{7,6},{8,7},{9,8},{10,9},{11,1... | collective-permute-start | bytes 49160 | tf_op jit(solution)/shard_map/ppermute | solution.py:179
  11.6 20.6 %copy-start.10 = (s32[4,4,32]{2,1,0:T(4,128)S(1)}, s32[4,4,32]{2,1,0:T(4,128)}, u32[]{:S(2)}) copy-start(s32[4,4,32]{2,1,0:T(4,128)} %mask.3) | copy-start | bytes 6148
  11.7 20.6 %copy-start.11 = (s32[4,4,32]{2,1,0:T(4,128)S(1)}, s32[4,4,32]{2,1,0:T(4,128)}, u32[]{:S(2)}) copy-start(s32[4,4,32]{2,1,0:T(4,128)} %partner.3) | copy-start | bytes 6148
  11.7 21.1 %copy-start.1 = (f32[3,4,32,256]{3,2,1,0:T(8,128)S(1)}, f32[3,4,32,256]{3,2,1,0:T(8,128)}, u32[]{:S(2)}) copy-start(f32[3,4,32,256]{3,2,1,0:T(8,128)} %ef.5) | copy-start | bytes 1179652
  11.9 20.8 %collective-permute-start.3 = (f32[2,2,32,256]{3,2,1,0:T(8,128)S(1)}, f32[2,2,32,256]{3,2,1,0:T(8,128)S(1)}, u32[]{:S(2)}, u32[]{:S(2)}) collective-permute-start(f32[2,2,32,256]{3,2,1,0:T(8,128)S(1)} %get-tuple-element.26), channel_id=1, source_target_pairs={{0,16},{16,32},{32,48},{48,64},{64,80},{80,96},{96,112},{112,128},... | collective-permute-start | bytes 393224 | tf_op jit(solution)/shard_map/ppermute | solution.py:179
  14.6 18.2 %collective-permute-start.4 = (f32[16,256]{1,0:T(8,128)S(1)}, f32[16,256]{1,0:T(8,128)S(1)}, u32[]{:S(2)}, u32[]{:S(2)}) collective-permute-start(f32[16,256]{1,0:T(8,128)S(1)} %get-tuple-element.27), channel_id=1, source_target_pairs={{0,1},{1,2},{2,3},{3,4},{4,5},{5,6},{6,7},{7,8},{8,9},{9,10},{10,1... | collective-permute-start | bytes 49160 | tf_op jit(solution)/shard_map/ppermute | solution.py:179
  17.4 14.9 %collective-permute-start.2 = (f32[4,4,32]{2,1,0:T(4,128)S(1)}, f32[4,4,32]{2,1,0:T(4,128)S(1)}, u32[]{:S(2)}, u32[]{:S(2)}) collective-permute-start(f32[4,4,32]{2,1,0:T(4,128)S(1)} %copy-done.12), channel_id=1, source_target_pairs={{0,496},{16,480},{32,464},{48,448},{64,432},{80,416},{96,400},{112... | collective-permute-start | bytes 6152 | tf_op jit(solution)/shard_map/ppermute | solution.py:184
  33.0 9.6 %collective-permute-start.5 = (f32[2,2,32,256]{3,2,1,0:T(8,128)S(1)}, f32[2,2,32,256]{3,2,1,0:T(8,128)S(1)}, u32[]{:S(2)}, u32[]{:S(2)}) collective-permute-start(f32[2,2,32,256]{3,2,1,0:T(8,128)S(1)} %get-tuple-element.30), channel_id=1, source_target_pairs={{16,0},{32,16},{48,32},{64,48},{80,64},{96,80},{112,96},{128,112},... | collective-permute-start | bytes 393224 | tf_op jit(solution)/shard_map/ppermute | solution.py:179
  37.0 5.6 %collective-permute-start.6 = (f32[16,256]{1,0:T(8,128)S(1)}, f32[16,256]{1,0:T(8,128)S(1)}, u32[]{:S(2)}, u32[]{:S(2)}) collective-permute-start(f32[16,256]{1,0:T(8,128)S(1)} %get-tuple-element.31), channel_id=1, source_target_pairs={{1,0},{2,1},{3,2},{4,3},{5,4},{6,5},{7,6},{8,7},{9,8},{10,9},{11,1... | collective-permute-start | bytes 49160 | tf_op jit(solution)/shard_map/ppermute | solution.py:179
  42.6 11.1 %copy-start.8 = (f32[2,3,4,4,32]{4,3,2,1,0:T(4,128)S(1)}, f32[2,3,4,4,32]{4,3,2,1,0:T(4,128)}, u32[]{:S(2)}) copy-start(f32[2,3,4,4,32]{4,3,2,1,0:T(4,128)} %mon_f.1) | copy-start | bytes 36868
  42.6 11.1 %copy-start.9 = (f32[2,3,4,4,32]{4,3,2,1,0:T(4,128)S(1)}, f32[2,3,4,4,32]{4,3,2,1,0:T(4,128)}, u32[]{:S(2)}) copy-start(f32[2,3,4,4,32]{4,3,2,1,0:T(4,128)} %mon_a.1) | copy-start | bytes 36868
  43.7 10.1 %collective-permute-start.7 = (f32[2,2,32,256]{3,2,1,0:T(8,128)S(1)}, f32[2,2,32,256]{3,2,1,0:T(8,128)S(1)}, u32[]{:S(2)}, u32[]{:S(2)}) collective-permute-start(f32[2,2,32,256]{3,2,1,0:T(8,128)S(1)} %get-tuple-element.34), channel_id=1, source_target_pairs={{0,16},{16,32},{32,48},{48,64},{64,80},{80,96},{96,112},{112,128},... | collective-permute-start | bytes 393224 | tf_op jit(solution)/shard_map/ppermute | solution.py:179
  46.0 7.8 %collective-permute-start.8 = (f32[16,256]{1,0:T(8,128)S(1)}, f32[16,256]{1,0:T(8,128)S(1)}, u32[]{:S(2)}, u32[]{:S(2)}) collective-permute-start(f32[16,256]{1,0:T(8,128)S(1)} %get-tuple-element.35), channel_id=1, source_target_pairs={{0,1},{1,2},{2,3},{3,4},{4,5},{5,6},{6,7},{7,8},{8,9},{9,10},{10,1... | collective-permute-start | bytes 49160 | tf_op jit(solution)/shard_map/ppermute | solution.py:179
  53.7 1.0 %copy-start.5 = (f32[3,4,32,256]{3,2,1,0:T(8,128)S(1)}, f32[3,4,32,256]{3,2,1,0:T(8,128)}, u32[]{:S(2)}) copy-start(f32[3,4,32,256]{3,2,1,0:T(8,128)} %get-tuple-element.18.hf) | copy-start | bytes 1179652
  54.7 1.0 %copy-start.6 = (f32[3,4,32,256]{3,2,1,0:T(8,128)S(1)}, f32[3,4,32,256]{3,2,1,0:T(8,128)}, u32[]{:S(2)}) copy-start(f32[3,4,32,256]{3,2,1,0:T(8,128)} %get-tuple-element.20.ha) | copy-start | bytes 1179652
  57.7 15.4 %collective-permute-start.9 = (f32[4,4,32]{2,1,0:T(4,128)S(1)}, f32[4,4,32]{2,1,0:T(4,128)S(1)}, u32[]{:S(2)}, u32[]{:S(2)}) collective-permute-start(f32[4,4,32]{2,1,0:T(4,128)S(1)} %get-tuple-element.38.grad), channel_id=1, source_target_pairs={{0,496},{16,480},{32,464},{48,448},{64,432},{80,416},{96,400},{112... | collective-permute-start | bytes 6152 | tf_op jit(solution)/shard_map/ppermute | solution.py:184

commit v2 on v1

v2 whole, which is shorter than its diff:
```python
import math

import jax
import jax.numpy as jnp
from jax import lax
from jax.experimental import pallas as pl
from jax.experimental.pallas import tpu as pltpu
from jax.sharding import PartitionSpec as P

PLANES = 4
Z0 = 126
COURANT = 0.5
OMEGA = 0.7
CONTRAST = 10.0
F32 = jnp.float32
VMEM_LIMIT = 32 * 1024 * 1024

LANES = 128
FRAME = 48
TOP, END = 8, 40
WINDOW = 8
SHIFT = LANES - (Z0 - 2)
ROW_EPS, ROW_MON, MESSAGE = 96, 128, 192


def lane_of(shape):
    return lax.broadcasted_iota(jnp.int32, shape, len(shape) - 1)


def row_of(shape):
    return lax.broadcasted_iota(jnp.int32, shape, len(shape) - 2)


def turn(a, shift):
    shift = shift % a.shape[1]
    return pltpu.roll(a, shift, 1) if shift else a


def up_y(a):
    return pltpu.roll(a, a.shape[0] - 1, 0)


def down_y(a):
    return pltpu.roll(a, 1, 0)


def up_z(a):
    n = a.shape[1]
    return jnp.where(lane_of(a.shape) == n - 1, 0.0, pltpu.roll(a, n - 1, 1))


def down_z(a):
    return jnp.where(lane_of(a.shape) == 0, 0.0, pltpu.roll(a, 1, 1))


def pack_planes(planes):
    total = None
    for offset, plane in planes:
        near = jnp.where(lane_of((plane.shape[0], LANES)) >= LANES // 2,
                         plane[:, :LANES], plane[:, LANES:2 * LANES])
        part = turn(near, SHIFT + offset)
        lane = lane_of(part.shape)
        inside = (lane >= offset) & (lane < offset + WINDOW)
        total = jnp.where(inside, part, 0.0 if total is None else total)
    return total


def flipped(a, square):
    square[...] = jnp.zeros_like(square)
    square[pl.ds(0, a.shape[0]), pl.ds(0, a.shape[1])] = a
    return jnp.transpose(square[...])


def load_kernel(ef, hf, ea, ha, eps, density, mask, partner, mon_f, mon_a,
                message, fields, eps_out,
                small_f, small_i, mons, square, sems):
    nx, ny = ef.shape[1], ef.shape[2]
    copies = []
    for f, (e, h) in enumerate(((ef, hf), (ea, ha))):
        for k, source in enumerate((e, h)):
            copies.append(pltpu.make_async_copy(
                source, fields.at[f, k], sems.at[2 * f + k]))
    copies.append(pltpu.make_async_copy(eps, eps_out, sems.at[4]))
    copies.append(pltpu.make_async_copy(density, small_f, sems.at[5]))
    copies.append(pltpu.make_async_copy(mask, small_i.at[0], sems.at[6]))
    copies.append(pltpu.make_async_copy(partner, small_i.at[1], sems.at[7]))
    copies.append(pltpu.make_async_copy(mon_f, mons.at[0], sems.at[8]))
    copies.append(pltpu.make_async_copy(mon_a, mons.at[1], sems.at[9]))
    for copy in copies:
        copy.start()
    message[pl.ds(ROW_EPS, MESSAGE - ROW_EPS), :] = jnp.zeros((MESSAGE - ROW_EPS, LANES), F32)
    for copy in copies[4:]:
        copy.wait()
    for half, components in ((0, (0, 1)), (1, (2,))):
        square[...] = jnp.zeros_like(square)
        for k, c in enumerate(components):
            for f in range(2):
                for x in range(nx):
                    base = k * 64 + x * 16 + f * 8 + 2
                    square[pl.ds(base, PLANES), pl.ds(0, ny)] = mons[f, 0, c, :, x, :]
                    for p in range(PLANES):
                        at = (base + 4 + p) % LANES
                        square[pl.ds(at, 1), pl.ds(0, ny)] = mons[f, 1, c, p, pl.ds(x, 1), :]
        message[pl.ds(ROW_MON + 32 * half, ny), :] = jnp.transpose(square[...])[:ny]
    own_eps = [(x * 16 + f * 8, eps_out[x]) for x in range(nx) for f in range(2)]
    square[...] = jnp.zeros_like(square)
    for p in range(PLANES):
        square[pl.ds(p * nx, nx), pl.ds(0, ny)] = CONTRAST * small_i[0, p].astype(F32)
        square[pl.ds(16 + p * nx, nx), pl.ds(0, ny)] = small_f[p]
        square[pl.ds(32 + p * nx, nx), pl.ds(0, ny)] = small_i[1, p].astype(F32)
    small = turn(square[pl.ds(0, 32), :], 64)
    index = turn(square[pl.ds(32, 32), :], 96)
    message[pl.ds(ROW_EPS, ny), :] = pack_planes(own_eps) + small + index
    for copy in copies[:4]:
        copy.wait()
    for c in range(3):
        message[pl.ds(c * 32, ny), :] = pack_planes(
            [(k * 64 + x * 16 + f * 8, fields[f, k, c, x])
             for k in range(2) for x in range(nx) for f in range(2)])


def small_parts(message):
    weight = turn(message[pl.ds(ROW_EPS, 16), :], -64)
    density = turn(message[pl.ds(ROW_EPS + 16, 16), :], -64)
    partner = turn(message[pl.ds(ROW_EPS, 16), :], -96)
    return weight, density, partner


def mirror_take(table, partner, ny):
    inside = lane_of(partner.shape) < ny
    at = jnp.where(inside, partner, 0.0).astype(jnp.int32)
    row, lane = at // ny, at % ny
    got = jnp.zeros(at.shape, F32)
    for r in range(table.shape[0]):
        line = jnp.broadcast_to(table[pl.ds(r, 1), :], at.shape)
        got = jnp.where(row == r, jnp.take_along_axis(line, lane, axis=1), got)
    return got


def spread_slab(values, lines, square, nx, ny):
    lines[...] = values
    square[...] = jnp.zeros_like(square)
    for p in range(PLANES):
        for x in range(nx):
            row = lines[pl.ds(p * nx + x, 1), :]
            square[pl.ds(x * 16 + 2 + p, 1), :] = row
            square[pl.ds(x * 16 + 10 + p, 1), :] = row
    return jnp.transpose(square[...])[:ny]


def coef_kernel(eps, mine, theirs, fields, coef, mirror_coef, y_up, y_down, table, lines, square):
    nx = eps.shape[0]
    ny = END - TOP
    weight, density, partner = small_parts(mine)
    weight_m, density_m, partner_m = small_parts(theirs)
    table[...] = density_m
    extra = weight * (0.5 * (density + mirror_take(table, partner, ny)))
    table[...] = density
    extra_m = weight_m * (0.5 * (density_m + mirror_take(table, partner_m, ny)))
    packed = spread_slab(extra, lines, square, nx, ny)
    lane = lane_of(packed.shape)
    for x in range(nx):
        part = turn(packed, -16 * x - SHIFT)
        low = jnp.where(lane >= Z0, part, 0.0)
        high = jnp.where(lane < Z0 + PLANES - LANES, part, 0.0)
        coef[x] = COURANT / (eps[x] + jnp.concatenate([low, high], 1))
    packed = theirs[pl.ds(ROW_EPS, ny), :] + spread_slab(extra_m, lines, square, nx, ny)
    mirror_coef[...] = jnp.where(lane < 64, COURANT / jnp.where(lane < 64, packed, 1.0), 0.0)
    for out, first in ((y_up, ny - 2), (y_down, 0)):
        at = 0
        for f in range(2):
            for k in range(2):
                for c in range(3):
                    for x in range(nx):
                        out[pl.ds(at, 2), :] = fields[f, k, c, x, pl.ds(first, 2), :]
                        at += 2
        for x in range(nx):
            out[pl.ds(at, 2), :] = coef[x, pl.ds(first, 2), :]
            at += 2
        out[pl.ds(at, 8), :] = jnp.zeros((8, out.shape[1]), F32)
        for c in range(3):
            out[pl.ds(at, 2), pl.ds(0, LANES)] = theirs[pl.ds(c * 32 + first, 2), :]
            at += 2
        out[pl.ds(at, 2), pl.ds(0, LANES)] = mirror_coef[pl.ds(first, 2), :]


def plane_index(f, k, c, x, nx):
    return ((f * 2 + k) * 3 + c) * nx + x


def framed(middle, tops, ends, i):
    return jnp.concatenate([tops[i], middle, ends[i]], 0)


def edges_kernel(fields, coef, mirror_coef, theirs, y_low, y_high,
                 tops, ends, mirror, x_up, x_down):
    nx, ny = coef.shape[0], coef.shape[1]
    tops[...] = jnp.zeros_like(tops)
    ends[...] = jnp.zeros_like(ends)
    mirror[...] = jnp.zeros_like(mirror)
    for c in range(3):
        mirror[c, pl.ds(TOP, ny), :] = theirs[pl.ds(c * 32, ny), :]
    mirror[3, pl.ds(TOP, ny), :] = mirror_coef[...]
    for source, out, first in ((y_low, tops, TOP - 2), (y_high, ends, 0)):
        for i in range(13 * nx):
            out[i, pl.ds(first, 2), :] = source[pl.ds(2 * i, 2), :]
        for c in range(4):
            row = TOP - 2 if out is tops else END
            mirror[c, pl.ds(row, 2), :] = source[pl.ds(26 * nx + 2 * c, 2), pl.ds(0, LANES)]

    def put(out, plane, value):
        out[pl.ds(plane * ny, ny), :] = value[TOP:END]
        out[pl.ds(10 * ny + 4 * plane, 2), :] = value[TOP - 2:TOP]
        out[pl.ds(10 * ny + 4 * plane + 2, 2), :] = value[END:END + 2]

    def part(f, k, c, x):
        return framed(fields[f, k, c, x], tops, ends, plane_index(f, k, c, x, nx))

    ks = [framed(coef[x], tops, ends, 12 * nx + x) for x in range(nx)]
    last = nx - 1
    for f in range(2):
        e = lambda c, x: part(f, 0, c, x)
        h = lambda c, x: part(f, 1, c, x)
        k, before = ks[last], ks[last - 1] > 0
        inside = k > 0
        ex, ey, ez = e(0, last), e(1, last), e(2, last)
        ex_b, ey_b, ez_b = e(0, last - 1), e(1, last - 1), e(2, last - 1)
        hy_b = jnp.where(before, h(1, last - 1) - COURANT * ((up_z(ex_b) - ex_b) - (ez - ez_b)), 0.0)
        hz_b = jnp.where(before, h(2, last - 1) - COURANT * ((ey - ey_b) - (up_y(ex_b) - ex_b)), 0.0)
        hx = jnp.where(inside, h(0, last) - COURANT * ((up_y(ez) - ez) - (up_z(ey) - ey)), 0.0)
        hy = jnp.where(inside, h(1, last) - COURANT * ((up_z(ex) - ex) + ez), 0.0)
        hz = jnp.where(inside, h(2, last) - COURANT * (-ey - (up_y(ex) - ex)), 0.0)
        ex = ex + k * ((hz - down_y(hz)) - (hy - down_z(hy)))
        ey = ey + k * ((hx - down_z(hx)) - (hz - hz_b))
        ez = ez + k * ((hy - hy_b) - (hx - down_y(hx)))
        put(x_up, 4 * f, hy)
        put(x_up, 4 * f + 1, hz)
        put(x_up, 4 * f + 2, jnp.where(inside, hy - COURANT * ((up_z(ex) - ex) + ez), 0.0))
        put(x_up, 4 * f + 3, jnp.where(inside, hz - COURANT * (-ey - (up_y(ex) - ex)), 0.0))
        k = ks[0]
        inside = k > 0
        ex, ey, ez = e(0, 0), e(1, 0), e(2, 0)
        hx = jnp.where(inside, h(0, 0) - COURANT * ((up_y(ez) - ez) - (up_z(ey) - ey)), 0.0)
        hy = jnp.where(inside, h(1, 0) - COURANT * ((up_z(ex) - ex) - (e(2, 1) - ez)), 0.0)
        hz = jnp.where(inside, h(2, 0) - COURANT * ((e(1, 1) - ey) - (up_y(ex) - ex)), 0.0)
        put(x_down, 4 * f, ey)
        put(x_down, 4 * f + 1, ez)
        put(x_down, 4 * f + 2, ey + k * ((hx - down_z(hx)) - hz))
        put(x_down, 4 * f + 3, ez + k * (hy - (hx - down_y(hx))))
    put(x_up, 8, ks[last])
    put(x_down, 8, ks[0])
    m = [mirror[c] for c in range(3)]
    km = mirror[3]
    first = lane_of(km.shape) % 64 < 32
    put(x_up, 9, jnp.concatenate([jnp.where(first, m[0], turn(m[1], 32)),
                                  jnp.where(first, m[2], turn(km, 32))], 1))
    put(x_down, 9, jnp.concatenate([jnp.where(first, turn(m[1], -32), m[0]),
                                    jnp.where(first, turn(km, -32), m[2])], 1))


def slab_gradient(message, first, second, ny):
    total = None
    for c in range(3):
        mon = message[pl.ds(ROW_MON + 32 * (c // 2), ny), :]
        real = turn(mon, -64 * (c % 2))
        imag = turn(real, -4)
        real = real + math.cos(OMEGA) * first[c] + math.cos(2 * OMEGA) * second[c]
        imag = imag - math.sin(OMEGA) * first[c] - math.sin(2 * OMEGA) * second[c]
        term = real * turn(real, -8) - imag * turn(imag, -8)
        total = term if total is None else total + term
    return total


def slab_rows(packed, out, square, nx):
    square[...] = flipped(packed, square)
    for p in range(PLANES):
        for x in range(nx):
            out[pl.ds(p * nx + x, 1), :] = square[pl.ds(x * 16 + 2 + p, 1), :]


def step_kernel(fields, coef, tops, ends, mirror, x_low, x_high, mine, theirs,
                ef_out, hf_out, ea_out, ha_out, grad,
                ee, hh, halo, square, table, lines, sems):
    nx, ny, nz = coef.shape

    def take(source, plane, slot):
        halo[slot, pl.ds(0, TOP), :] = jnp.zeros((TOP, nz), F32)
        halo[slot, pl.ds(END, TOP), :] = jnp.zeros((TOP, nz), F32)
        halo[slot, pl.ds(TOP, ny), :] = source[pl.ds(plane * ny, ny), :]
        halo[slot, pl.ds(TOP - 2, 2), :] = source[pl.ds(10 * ny + 4 * plane, 2), :]
        halo[slot, pl.ds(END, 2), :] = source[pl.ds(10 * ny + 4 * plane + 2, 2), :]

    for plane in range(10):
        take(x_low, plane, plane)
        take(x_high, plane, 10 + plane)
    k_low, k_high = halo[8], halo[18]

    def part(f, k, c, x):
        return framed(fields[f, k, c, x], tops, ends, plane_index(f, k, c, x, nx))

    def inverse(x):
        return framed(coef[x], tops, ends, 12 * nx + x)

    copies = []
    first_slab, second_slab = [], []
    for f in range(2):
        ey0, ez0 = part(f, 0, 1, 0), part(f, 0, 2, 0)
        dhy = jnp.where(k_low > 0, COURANT * ez0, 0.0)
        dhz = jnp.where(k_low > 0, -COURANT * ey0, 0.0)
        hh[f, 1, 0] = halo[4 * f] + dhy
        hh[f, 2, 0] = halo[4 * f + 1] + dhz
        for x in range(nx):
            inside = inverse(x) > 0
            ex, ey, ez = part(f, 0, 0, x), part(f, 0, 1, x), part(f, 0, 2, x)
            ey_n = part(f, 0, 1, x + 1) if x + 1 < nx else halo[10 + 4 * f]
            ez_n = part(f, 0, 2, x + 1) if x + 1 < nx else halo[10 + 4 * f + 1]
            hx, hy, hz = part(f, 1, 0, x), part(f, 1, 1, x), part(f, 1, 2, x)
            hh[f, 0, x + 1] = jnp.where(inside, hx - COURANT * ((up_y(ez) - ez) - (up_z(ey) - ey)), 0.0)
            hh[f, 1, x + 1] = jnp.where(inside, hy - COURANT * ((up_z(ex) - ex) - (ez_n - ez)), 0.0)
            hh[f, 2, x + 1] = jnp.where(inside, hz - COURANT * ((ey_n - ey) - (up_y(ex) - ex)), 0.0)
        for x in range(nx):
            k = inverse(x)
            hx, hy, hz = hh[f, 0, x + 1], hh[f, 1, x + 1], hh[f, 2, x + 1]
            ee[f, 0, x] = part(f, 0, 0, x) + k * ((hz - down_y(hz)) - (hy - down_z(hy)))
            ee[f, 1, x] = part(f, 0, 1, x) + k * ((hx - down_z(hx)) - (hz - hh[f, 2, x]))
            ee[f, 2, x] = part(f, 0, 2, x) + k * ((hy - hh[f, 1, x]) - (hx - down_y(hx)))
        ee[f, 1, nx] = halo[10 + 4 * f + 2] + k_high * hh[f, 2, nx]
        ee[f, 2, nx] = halo[10 + 4 * f + 3] - k_high * hh[f, 1, nx]
        dex = k_low * ((dhz - down_y(dhz)) - (dhy - down_z(dhy)))
        dey = -k_low * dhz
        dez = k_low * dhy
        hh[f, 1, 0] = jnp.where(
            k_low > 0, halo[4 * f + 2] + dhy - COURANT * ((up_z(dex) - dex) - (ee[f, 2, 0] - dez)), 0.0)
        hh[f, 2, 0] = jnp.where(
            k_low > 0, halo[4 * f + 3] + dhz - COURANT * ((ee[f, 1, 0] - dey) - (up_y(dex) - dex)), 0.0)
        for x in range(nx):
            inside = inverse(x) > 0
            ex, ey, ez = ee[f, 0, x], ee[f, 1, x], ee[f, 2, x]
            hh[f, 0, x + 1] = jnp.where(
                inside, hh[f, 0, x + 1] - COURANT * ((up_y(ez) - ez) - (up_z(ey) - ey)), 0.0)
            hh[f, 1, x + 1] = jnp.where(
                inside, hh[f, 1, x + 1] - COURANT * ((up_z(ex) - ex) - (ee[f, 2, x + 1] - ez)), 0.0)
            hh[f, 2, x + 1] = jnp.where(
                inside, hh[f, 2, x + 1] - COURANT * ((ee[f, 1, x + 1] - ey) - (up_y(ex) - ex)), 0.0)
        copies.append(pltpu.make_async_copy(
            hh.at[f, :, pl.ds(1, nx), pl.ds(TOP, ny), :], (hf_out, ha_out)[f], sems.at[2 * f]))
        copies[-1].start()
    for c in range(3):
        first_slab.append(pack_planes([(x * 16 + f * 8, ee[f, c, x, pl.ds(TOP, ny), :])
                                       for x in range(nx) for f in range(2)]))
    for f in range(2):
        for x in range(nx):
            k = inverse(x)
            hx, hy, hz = hh[f, 0, x + 1], hh[f, 1, x + 1], hh[f, 2, x + 1]
            ee[f, 0, x] = ee[f, 0, x] + k * ((hz - down_y(hz)) - (hy - down_z(hy)))
            ee[f, 1, x] = ee[f, 1, x] + k * ((hx - down_z(hx)) - (hz - hh[f, 2, x]))
            ee[f, 2, x] = ee[f, 2, x] + k * ((hy - hh[f, 1, x]) - (hx - down_y(hx)))
        copies.append(pltpu.make_async_copy(
            ee.at[f, :, pl.ds(0, nx), pl.ds(TOP, ny), :], (ef_out, ea_out)[f], sems.at[2 * f + 1]))
        copies[-1].start()
    for c in range(3):
        second_slab.append(pack_planes([(x * 16 + f * 8, ee[f, c, x, pl.ds(TOP, ny), :])
                                        for x in range(nx) for f in range(2)]))
    own = slab_gradient(mine, first_slab, second_slab, ny)

    low01, low2 = halo[9, :, pl.ds(0, LANES)], halo[9, :, pl.ds(LANES, LANES)]
    high01, high2 = halo[19, :, pl.ds(0, LANES)], halo[19, :, pl.ds(LANES, LANES)]
    lane = lane_of(low01.shape)

    def join(below, middle, above):
        return jnp.where(lane < 32, below, jnp.where(lane < 96, middle, above))

    m = [mirror[c] for c in range(3)]
    e = [join(turn(high01, -32), turn(m[0], 32), turn(low01, 96)),
         join(high01, turn(m[1], 32), turn(low01, 64)),
         join(turn(high2, -32), turn(m[2], 32), turn(low2, 96))]
    h = [join(turn(high01, -96), turn(m[0], -32), turn(low01, 32)),
         join(turn(high01, -64), turn(m[1], -32), low01),
         join(turn(high2, -96), turn(m[2], -32), turn(low2, 32))]
    k = join(high2, turn(mirror[3], 32), turn(low2, 64))
    inside = k > 0

    def ahead(a, axis):
        return (turn(a, -16), up_y(a), turn(a, -1))[axis] - a

    def behind(a, axis):
        return a - (turn(a, 16), down_y(a), turn(a, 1))[axis]

    slabs = []
    for _ in range(2):
        h = [jnp.where(inside, h[c] - COURANT * (ahead(e[(c + 2) % 3], (c + 1) % 3)
                                                 - ahead(e[(c + 1) % 3], (c + 2) % 3)), 0.0)
             for c in range(3)]
        e = [e[c] + k * (behind(h[(c + 2) % 3], (c + 1) % 3) - behind(h[(c + 1) % 3], (c + 2) % 3))
             for c in range(3)]
        slabs.append([turn(e[c], -32)[TOP:END] for c in range(3)])
    other = slab_gradient(theirs, slabs[0], slabs[1], ny)

    weight, _, partner = small_parts(mine)
    weight_m, _, _ = small_parts(theirs)
    slab_rows(other, table, square, nx)
    table[...] = table[...] * weight_m
    got = mirror_take(table, partner, ny)
    slab_rows(own, lines, square, nx)
    lines[...] = 0.5 * (lines[...] * weight + got)
    for p in range(PLANES):
        grad[p] = lines[pl.ds(p * nx, nx), pl.ds(0, ny)]
    for copy in copies:
        copy.wait()


def call(kernel, outs, args, scratch=(), name=None, any_in=False, any_out=0):
    spaces = lambda count, far: [pl.BlockSpec(memory_space=pltpu.HBM if i < far else pltpu.VMEM)
                                 for i in range(count)]
    return pl.pallas_call(
        kernel,
        out_shape=outs,
        in_specs=spaces(len(args), len(args) if any_in else 0),
        out_specs=spaces(len(outs), any_out),
        scratch_shapes=list(scratch),
        compiler_params=pltpu.CompilerParams(vmem_limit_bytes=VMEM_LIMIT),
        cost_estimate=pl.CostEstimate(flops=4_000_000, bytes_accessed=4_000_000, transcendentals=0),
        name=name,
    )(*args)


def shifted(block, axis, distance):
    devices = range(lax.axis_size(axis))
    return lax.ppermute(block, axis, [(i - distance, i) for i in devices if i - distance in devices])


def mirrored(block, axis):
    size = lax.axis_size(axis)
    return lax.ppermute(block, axis, [(i, size - 1 - i) for i in range(size)])


def per_device(e_fwd, h_fwd, e_adj, h_adj, eps_back, density, design_mask, partner_map, mon_fwd, mon_adj):
    _, nx, ny, nz = e_fwd.shape
    shape = lambda *dims: jax.ShapeDtypeStruct(dims, F32)
    vmem = lambda *dims: pltpu.VMEM(dims, F32)
    square = vmem(LANES, LANES)
    lines = vmem(PLANES * nx, LANES)
    fields_shape = shape(2, 2, 3, nx, ny, nz)
    block = shape(nx, ny, nz)

    mine, fields, eps = call(
        load_kernel, [shape(MESSAGE, LANES), fields_shape, block],
        [e_fwd, h_fwd, e_adj, h_adj, eps_back, density, design_mask, partner_map, mon_fwd, mon_adj],
        [vmem(*density.shape), pltpu.VMEM((2,) + density.shape, jnp.int32), vmem(2, *mon_fwd.shape),
         square, pltpu.SemaphoreType.DMA((10,))], name="load", any_in=True)
    theirs = mirrored(mine, "gx")
    y_shape = shape(2 * (13 * nx) + 8, nz)
    coef, mirror_coef, y_up, y_down = call(
        coef_kernel, [block, shape(ny, LANES), y_shape, y_shape], [eps, mine, theirs, fields],
        [lines, lines, square], name="coefficient")
    y_low, y_high = shifted(y_up, "gy", 1), shifted(y_down, "gy", -1)
    x_shape = shape(10 * (ny + 4), nz)
    tile = shape(13 * nx, 8, nz)
    tops, ends, mirror, x_up, x_down = call(
        edges_kernel, [tile, tile, shape(4, FRAME, LANES), x_shape, x_shape],
        [fields, coef, mirror_coef, theirs, y_low, y_high], name="edges")
    x_low, x_high = shifted(x_up, "gx", 1), shifted(x_down, "gx", -1)
    ef, hf, ea, ha, grad = call(
        step_kernel, [shape(*e_fwd.shape)] * 4 + [shape(*density.shape)],
        [fields, coef, tops, ends, mirror, x_low, x_high, mine, theirs],
        [vmem(2, 3, nx + 1, FRAME, nz), vmem(2, 3, nx + 1, FRAME, nz), vmem(20, FRAME, nz),
         square, lines, lines, pltpu.SemaphoreType.DMA((4,))], name="steps", any_out=4)
    return ef, hf, ea, ha, grad


def solution(mesh):
    grid = P(None, "gx", "gy", None)
    slab = P(None, "gx", "gy")
    monitor = P(None, None, None, "gx", "gy")
    return jax.shard_map(
        per_device,
        mesh=mesh,
        in_specs=(grid, grid, grid, grid, P("gx", "gy", None), slab, slab, slab, monitor, monitor),
        out_specs=(grid, grid, grid, grid, slab),
        check_vma=False,
    )
```

time: 74.4 us -> 68.7 us (0.923)
  the two profiles are of different devices: /device:TPU:134 before, /device:TPU:37 now
where the time goes in v2:
time: 68.7 us; the launch traced here: 68 us
  waiting for transfers between devices  26.5 us (39%)
  starting transfers between devices  25.6 us (37%)
  local copies, waits for them, and re-layouts  8.56 us (12%)
  Pallas kernels  6.62 us (10%)
  between operations  0.72 us (1%)
    ppermute x4, waiting for transfers between devices, shifted(): lax.ppermute(block, axis, [(i - distance, i) for i in devices if i - dist...  19.5 us
    ppermute x4, starting transfers between devices, shifted(): lax.ppermute(block, axis, [(i - distance, i) for i in devices if i - dist...  13.5 us
    ppermute x1, starting transfers between devices, mirrored(): return lax.ppermute(block, axis, [(i, size - 1 - i) for i in range(size)])  12.1 us
    unnamed x20, local copies, waits for them, and re-layouts  8.56 us
    ppermute x1, waiting for transfers between devices, mirrored(): return lax.ppermute(block, axis, [(i, size - 1 - i) for i in range(size)])  7.07 us
    pallas_call x4, Pallas kernels, call(): pl.pallas_call(kernel, out_shape=outs, in_specs=spaces(len(args), len(arg...  6.62 us
  transfers between devices with their start and end apart: 5, of which 4 were waited for; matrix products, arithmetic and copies ran while one was open for 0% of the time, Pallas kernels for 0%

profile of v2, /device:TPU:37, one launch (start us, length us, event | category | flops | bytes accessed | tf_op | source)
XLA Modules:
  0.0 68.0 jit_solution(16124385513335570932)
XLA Ops:
  0.6 0.0 copy-start
  0.6 1.0 %copy-done = f32[3,4,32,256]{3,2,1,0:T(8,128)S(1)} copy-done((f32[3,4,32,256]{3,2,1,0:T(8,128)S(1)}, f32[3,4,32,256]{3,2,1,0:T(8,128)}, u32[]{:S(2)}) %copy-start) | copy-done | bytes 393240
  1.6 0.0 copy-start.1
  1.6 1.0 %copy-done.1 = f32[3,4,32,256]{3,2,1,0:T(8,128)S(1)} copy-done((f32[3,4,32,256]{3,2,1,0:T(8,128)S(1)}, f32[3,4,32,256]{3,2,1,0:T(8,128)}, u32[]{:S(2)}) %copy-start.1) | copy-done | bytes 393240
  2.6 0.0 copy-start.2
  2.6 1.0 %copy-done.2 = f32[3,4,32,256]{3,2,1,0:T(8,128)S(1)} copy-done((f32[3,4,32,256]{3,2,1,0:T(8,128)S(1)}, f32[3,4,32,256]{3,2,1,0:T(8,128)}, u32[]{:S(2)}) %copy-start.2) | copy-done | bytes 393240
  3.6 0.0 copy-start.3
  3.6 1.0 %copy-done.3 = f32[3,4,32,256]{3,2,1,0:T(8,128)S(1)} copy-done((f32[3,4,32,256]{3,2,1,0:T(8,128)S(1)}, f32[3,4,32,256]{3,2,1,0:T(8,128)}, u32[]{:S(2)}) %copy-start.3) | copy-done | bytes 393240
  4.6 0.0 copy-start.4
  4.6 0.9 %copy-done.4 = f32[4,32,256]{2,1,0:T(8,128)S(1)} copy-done((f32[4,32,256]{2,1,0:T(8,128)S(1)}, f32[4,32,256]{2,1,0:T(8,128)}, u32[]{:S(2)}) %copy-start.4) | copy-done | bytes 131096
  5.5 0.0 copy-start.5
  5.5 0.8 %copy-done.5 = f32[2,3,4,4,32]{4,3,2,1,0:T(4,128)S(1)} copy-done((f32[2,3,4,4,32]{4,3,2,1,0:T(4,128)S(1)}, f32[2,3,4,4,32]{4,3,2,1,0:T(4,128)}, u32[]{:S(2)}) %copy-start.5) | copy-done | bytes 12312
  6.3 0.0 copy-start.6
  6.3 0.8 %copy-done.6 = f32[2,3,4,4,32]{4,3,2,1,0:T(4,128)S(1)} copy-done((f32[2,3,4,4,32]{4,3,2,1,0:T(4,128)S(1)}, f32[2,3,4,4,32]{4,3,2,1,0:T(4,128)}, u32[]{:S(2)}) %copy-start.6) | copy-done | bytes 12312
  7.1 0.0 copy-start.7
  7.1 0.7 %copy-done.7 = f32[4,4,32]{2,1,0:T(4,128)S(1)} copy-done((f32[4,4,32]{2,1,0:T(4,128)S(1)}, f32[4,4,32]{2,1,0:T(4,128)}, u32[]{:S(2)}) %copy-start.7) | copy-done | bytes 2072
  7.8 0.0 copy-start.8
  7.8 0.7 %copy-done.8 = s32[4,4,32]{2,1,0:T(4,128)S(1)} copy-done((s32[4,4,32]{2,1,0:T(4,128)S(1)}, s32[4,4,32]{2,1,0:T(4,128)}, u32[]{:S(2)}) %copy-start.8) | copy-done | bytes 2072
  8.5 0.0 copy-start.9
  8.5 0.7 %copy-done.9 = s32[4,4,32]{2,1,0:T(4,128)S(1)} copy-done((s32[4,4,32]{2,1,0:T(4,128)S(1)}, s32[4,4,32]{2,1,0:T(4,128)}, u32[]{:S(2)}) %copy-start.9) | copy-done | bytes 2072
  9.2 1.7 %load.1 = (f32[192,128]{1,0:T(8,128)S(1)}, f32[2,2,3,4,32,256]{5,4,3,2,1,0:T(8,128)S(1)}, f32[4,32,256]{2,1,0:T(8,128)S(1)}) custom-call(f32[3,4,32,256]{3,2,1,0:T(8,128)S(1)} %copy-done, f32[3,4,32,256]{3,2,1,0:T(8,128)S(1)} %copy-done.1, f32[3,4,32,256]{3,2,1,0:T(8,128)S(1)} %copy-done.2, f32[3,4,32,256]{3,2,1,0:T(8,128)S(1)} %copy-done.3, ...), custom_call_target="tpu_custom_call" | custom-call | flops 4000000 | bytes 4000000 | tf_op jit(solution)/shard_map/load/pallas_call | solution.py:415
  10.9 12.1 %collective-permute-start = (f32[192,128]{1,0:T(8,128)S(1)}, f32[192,128]{1,0:T(8,128)S(1)}, u32[]{:S(2)}, u32[]{:S(2)}) collective-permute-start(f32[192,128]{1,0:T(8,128)S(1)} %get-tuple-element.19.mine), channel_id=1, source_target_pairs={{0,496},{16,480},{32,464},{48,448},{64,432},{80,416},{96,400},{112... | collective-permute-start | bytes 294920 | tf_op jit(solution)/shard_map/ppermute | solution.py:434
  23.0 7.1 %collective-permute-done.theirs = f32[192,128]{1,0:T(8,128)S(1)} collective-permute-done((f32[192,128]{1,0:T(8,128)S(1)}, f32[192,128]{1,0:T(8,128)S(1)}, u32[]{:S(2)}, u32[]{:S(2)}) %collective-permute-start) | collective-permute-done | bytes 98336 | tf_op jit(solution)/shard_map/ppermute | solution.py:434
  30.1 0.5 coefficient.1
  30.6 5.4 %collective-permute-start.1 = (f32[112,256]{1,0:T(8,128)S(1)}, f32[112,256]{1,0:T(8,128)S(1)}, u32[]{:S(2)}, u32[]{:S(2)}) collective-permute-start(f32[112,256]{1,0:T(8,128)S(1)} %get-tuple-element.22), channel_id=1, source_target_pairs={{0,1},{1,2},{2,3},{3,4},{4,5},{5,6},{6,7},{7,8},{8,9},{9,10},{10,1... | collective-permute-start | bytes 344072 | tf_op jit(solution)/shard_map/ppermute | solution.py:429
  36.0 1.9 %collective-permute-start.2 = (f32[112,256]{1,0:T(8,128)S(1)}, f32[112,256]{1,0:T(8,128)S(1)}, u32[]{:S(2)}, u32[]{:S(2)}) collective-permute-start(f32[112,256]{1,0:T(8,128)S(1)} %get-tuple-element.23), channel_id=1, source_target_pairs={{1,0},{2,1},{3,2},{4,3},{5,4},{6,5},{7,6},{8,7},{9,8},{10,9},{11,1... | collective-permute-start | bytes 344072 | tf_op jit(solution)/shard_map/ppermute | solution.py:429
  37.9 0.0 collective-permute-done.1.y_low
  37.9 5.7 %collective-permute-done.2.y_high = f32[112,256]{1,0:T(8,128)S(1)} collective-permute-done((f32[112,256]{1,0:T(8,128)S(1)}, f32[112,256]{1,0:T(8,128)S(1)}, u32[]{:S(2)}, u32[]{:S(2)}) %collective-permute-start.2) | collective-permute-done | bytes 114720 | tf_op jit(solution)/shard_map/ppermute | solution.py:429
  43.6 0.7 %edges.1 = (f32[52,8,256]{2,1,0:T(8,128)S(1)}, f32[52,8,256]{2,1,0:T(8,128)S(1)}, f32[4,48,128]{2,1,0:T(8,128)S(1)}, f32[360,256]{1,0:T(8,128)S(1)}, f32[360,256]{1,0:T(8,128)S(1)}) custom-call(f32[2,2,3,4,32,256]{5,4,3,2,1,0:T(8,128)S(1)} %get-tuple-element.17.fields, f32[4,32,256]{2,1,0:T(8,128)S(1)} %get-tuple-element.20.coef, ...), custom_call_target="tpu_custom_call" | custom-call | flops 4000000 | bytes 4000000 | tf_op jit(solution)/shard_map/edges/pallas_call | solution.py:415
  44.3 1.9 %collective-permute-start.3 = (f32[360,256]{1,0:T(8,128)S(1)}, f32[360,256]{1,0:T(8,128)S(1)}, u32[]{:S(2)}, u32[]{:S(2)}) collective-permute-start(f32[360,256]{1,0:T(8,128)S(1)} %get-tuple-element.27), channel_id=1, source_target_pairs={{0,16},{16,32},{32,48},{48,64},{64,80},{80,96},{96,112},{112,128},... | collective-permute-start | bytes 1105928 | tf_op jit(solution)/shard_map/ppermute | solution.py:429
  46.2 4.3 %collective-permute-start.4 = (f32[360,256]{1,0:T(8,128)S(1)}, f32[360,256]{1,0:T(8,128)S(1)}, u32[]{:S(2)}, u32[]{:S(2)}) collective-permute-start(f32[360,256]{1,0:T(8,128)S(1)} %get-tuple-element.28), channel_id=1, source_target_pairs={{16,0},{32,16},{48,32},{64,48},{80,64},{96,80},{112,96},{128,112},... | collective-permute-start | bytes 1105928 | tf_op jit(solution)/shard_map/ppermute | solution.py:429
  50.5 10.9 %collective-permute-done.3.x_low = f32[360,256]{1,0:T(8,128)S(1)} collective-permute-done((f32[360,256]{1,0:T(8,128)S(1)}, f32[360,256]{1,0:T(8,128)S(1)}, u32[]{:S(2)}, u32[]{:S(2)}) %collective-permute-start.3) | collective-permute-done | bytes 368672 | tf_op jit(solution)/shard_map/ppermute | solution.py:429
  61.4 2.9 %collective-permute-done.4.x_high = f32[360,256]{1,0:T(8,128)S(1)} collective-permute-done((f32[360,256]{1,0:T(8,128)S(1)}, f32[360,256]{1,0:T(8,128)S(1)}, u32[]{:S(2)}, u32[]{:S(2)}) %collective-permute-start.4) | collective-permute-done | bytes 368672 | tf_op jit(solution)/shard_map/ppermute | solution.py:429
  64.2 3.8 %steps.1 = (f32[3,4,32,256]{3,2,1,0:T(8,128)}, f32[3,4,32,256]{3,2,1,0:T(8,128)}, f32[3,4,32,256]{3,2,1,0:T(8,128)}, f32[3,4,32,256]{3,2,1,0:T(8,128)}, f32[4,4,32]{2,1,0:T(4,128)}) custom-call(f32[2,2,3,4,32,256]{5,4,3,2,1,0:T(8,128)S(1)} %get-tuple-element.17.fields, f32[4,32,256]{2,1,0:T(8,128)S(1)} %get-tuple-element.20.coef, ...), custom_call_target="tpu_custom_call" | custom-call | flops 4000000 | bytes 4000000 | tf_op jit(solution)/shard_map/steps/pallas_call | solution.py:415
Async XLA Ops:
  0.6 1.0 %copy-start = (f32[3,4,32,256]{3,2,1,0:T(8,128)S(1)}, f32[3,4,32,256]{3,2,1,0:T(8,128)}, u32[]{:S(2)}) copy-start(f32[3,4,32,256]{3,2,1,0:T(8,128)} %ef.1) | copy-start | bytes 1179652
  1.6 1.0 %copy-start.1 = (f32[3,4,32,256]{3,2,1,0:T(8,128)S(1)}, f32[3,4,32,256]{3,2,1,0:T(8,128)}, u32[]{:S(2)}) copy-start(f32[3,4,32,256]{3,2,1,0:T(8,128)} %hf.1) | copy-start | bytes 1179652
  2.6 1.0 %copy-start.2 = (f32[3,4,32,256]{3,2,1,0:T(8,128)S(1)}, f32[3,4,32,256]{3,2,1,0:T(8,128)}, u32[]{:S(2)}) copy-start(f32[3,4,32,256]{3,2,1,0:T(8,128)} %ea.1) | copy-start | bytes 1179652
  3.6 1.0 %copy-start.3 = (f32[3,4,32,256]{3,2,1,0:T(8,128)S(1)}, f32[3,4,32,256]{3,2,1,0:T(8,128)}, u32[]{:S(2)}) copy-start(f32[3,4,32,256]{3,2,1,0:T(8,128)} %ha.1) | copy-start | bytes 1179652
  4.6 0.9 %copy-start.4 = (f32[4,32,256]{2,1,0:T(8,128)S(1)}, f32[4,32,256]{2,1,0:T(8,128)}, u32[]{:S(2)}) copy-start(f32[4,32,256]{2,1,0:T(8,128)} %eps.1) | copy-start | bytes 393220
  5.5 0.8 %copy-start.5 = (f32[2,3,4,4,32]{4,3,2,1,0:T(4,128)S(1)}, f32[2,3,4,4,32]{4,3,2,1,0:T(4,128)}, u32[]{:S(2)}) copy-start(f32[2,3,4,4,32]{4,3,2,1,0:T(4,128)} %mon_f.1) | copy-start | bytes 36868
  6.3 0.8 %copy-start.6 = (f32[2,3,4,4,32]{4,3,2,1,0:T(4,128)S(1)}, f32[2,3,4,4,32]{4,3,2,1,0:T(4,128)}, u32[]{:S(2)}) copy-start(f32[2,3,4,4,32]{4,3,2,1,0:T(4,128)} %mon_a.1) | copy-start | bytes 36868
  7.1 0.7 %copy-start.7 = (f32[4,4,32]{2,1,0:T(4,128)S(1)}, f32[4,4,32]{2,1,0:T(4,128)}, u32[]{:S(2)}) copy-start(f32[4,4,32]{2,1,0:T(4,128)} %density.1) | copy-start | bytes 6148
  7.8 0.7 %copy-start.8 = (s32[4,4,32]{2,1,0:T(4,128)S(1)}, s32[4,4,32]{2,1,0:T(4,128)}, u32[]{:S(2)}) copy-start(s32[4,4,32]{2,1,0:T(4,128)} %mask.1) | copy-start | bytes 6148
  8.5 0.7 %copy-start.9 = (s32[4,4,32]{2,1,0:T(4,128)S(1)}, s32[4,4,32]{2,1,0:T(4,128)}, u32[]{:S(2)}) copy-start(s32[4,4,32]{2,1,0:T(4,128)} %partner.1) | copy-start | bytes 6148
  10.9 19.2 %collective-permute-start = (f32[192,128]{1,0:T(8,128)S(1)}, f32[192,128]{1,0:T(8,128)S(1)}, u32[]{:S(2)}, u32[]{:S(2)}) collective-permute-start(f32[192,128]{1,0:T(8,128)S(1)} %get-tuple-element.19.mine), channel_id=1, source_target_pairs={{0,496},{16,480},{32,464},{48,448},{64,432},{80,416},{96,400},{112... | collective-permute-start | bytes 294920 | tf_op jit(solution)/shard_map/ppermute | solution.py:434
  30.6 7.3 %collective-permute-start.1 = (f32[112,256]{1,0:T(8,128)S(1)}, f32[112,256]{1,0:T(8,128)S(1)}, u32[]{:S(2)}, u32[]{:S(2)}) collective-permute-start(f32[112,256]{1,0:T(8,128)S(1)} %get-tuple-element.22), channel_id=1, source_target_pairs={{0,1},{1,2},{2,3},{3,4},{4,5},{5,6},{6,7},{7,8},{8,9},{9,10},{10,1... | collective-permute-start | bytes 344072 | tf_op jit(solution)/shard_map/ppermute | solution.py:429
  36.0 7.6 %collective-permute-start.2 = (f32[112,256]{1,0:T(8,128)S(1)}, f32[112,256]{1,0:T(8,128)S(1)}, u32[]{:S(2)}, u32[]{:S(2)}) collective-permute-start(f32[112,256]{1,0:T(8,128)S(1)} %get-tuple-element.23), channel_id=1, source_target_pairs={{1,0},{2,1},{3,2},{4,3},{5,4},{6,5},{7,6},{8,7},{9,8},{10,9},{11,1... | collective-permute-start | bytes 344072 | tf_op jit(solution)/shard_map/ppermute | solution.py:429
  44.3 17.1 %collective-permute-start.3 = (f32[360,256]{1,0:T(8,128)S(1)}, f32[360,256]{1,0:T(8,128)S(1)}, u32[]{:S(2)}, u32[]{:S(2)}) collective-permute-start(f32[360,256]{1,0:T(8,128)S(1)} %get-tuple-element.27), channel_id=1, source_target_pairs={{0,16},{16,32},{32,48},{48,64},{64,80},{80,96},{96,112},{112,128},... | collective-permute-start | bytes 1105928 | tf_op jit(solution)/shard_map/ppermute | solution.py:429
  46.2 18.0 %collective-permute-start.4 = (f32[360,256]{1,0:T(8,128)S(1)}, f32[360,256]{1,0:T(8,128)S(1)}, u32[]{:S(2)}, u32[]{:S(2)}) collective-permute-start(f32[360,256]{1,0:T(8,128)S(1)} %get-tuple-element.28), channel_id=1, source_target_pairs={{16,0},{32,16},{48,32},{64,48},{80,64},{96,80},{112,96},{128,112},... | collective-permute-start | bytes 1105928 | tf_op jit(solution)/shard_map/ppermute | solution.py:429

commit v3 on v2

--- a/solution.py
+++ b/solution.py
@@ -14,6 +14,7 @@
 CONTRAST = 10.0
 F32 = jnp.float32
 VMEM_LIMIT = 32 * 1024 * 1024
+FAR_LIMIT = 60 * 1024 * 1024
 
 LANES = 128
 FRAME = 48
@@ -71,16 +72,14 @@
     return jnp.transpose(square[...])
 
 
-def load_kernel(ef, hf, ea, ha, eps, density, mask, partner, mon_f, mon_a,
-                message, fields, eps_out,
-                small_f, small_i, mons, square, sems):
+def message_kernel(ef, hf, ea, ha, eps, density, mask, partner, mon_f, mon_a, message,
+                   fields, eps_in, small_f, small_i, mons, square, sems):
     nx, ny = ef.shape[1], ef.shape[2]
     copies = []
     for f, (e, h) in enumerate(((ef, hf), (ea, ha))):
         for k, source in enumerate((e, h)):
-            copies.append(pltpu.make_async_copy(
-                source, fields.at[f, k], sems.at[2 * f + k]))
-    copies.append(pltpu.make_async_copy(eps, eps_out, sems.at[4]))
+            copies.append(pltpu.make_async_copy(source, fields.at[f, k], sems.at[2 * f + k]))
+    copies.append(pltpu.make_async_copy(eps, eps_in, sems.at[4]))
     copies.append(pltpu.make_async_copy(density, small_f, sems.at[5]))
     copies.append(pltpu.make_async_copy(mask, small_i.at[0], sems.at[6]))
     copies.append(pltpu.make_async_copy(partner, small_i.at[1], sems.at[7]))
@@ -102,7 +101,7 @@
                         at = (base + 4 + p) % LANES
                         square[pl.ds(at, 1), pl.ds(0, ny)] = mons[f, 1, c, p, pl.ds(x, 1), :]
         message[pl.ds(ROW_MON + 32 * half, ny), :] = jnp.transpose(square[...])[:ny]
-    own_eps = [(x * 16 + f * 8, eps_out[x]) for x in range(nx) for f in range(2)]
+    own_eps = [(x * 16 + f * 8, eps_in[x]) for x in range(nx) for f in range(2)]
     square[...] = jnp.zeros_like(square)
     for p in range(PLANES):
         square[pl.ds(p * nx, nx), pl.ds(0, ny)] = CONTRAST * small_i[0, p].astype(F32)
@@ -148,7 +147,7 @@
     return jnp.transpose(square[...])[:ny]
 
 
-def coef_kernel(eps, mine, theirs, fields, coef, mirror_coef, y_up, y_down, table, lines, square):
+def coef_kernel(eps, mine, theirs, ef, hf, ea, ha, coef, mirror_coef, y_up, y_down, table, lines, square):
     nx = eps.shape[0]
     ny = END - TOP
     weight, density, partner = small_parts(mine)
@@ -172,7 +171,7 @@
             for k in range(2):
                 for c in range(3):
                     for x in range(nx):
-                        out[pl.ds(at, 2), :] = fields[f, k, c, x, pl.ds(first, 2), :]
+                        out[pl.ds(at, 2), :] = ((ef, hf), (ea, ha))[f][k][c, x, pl.ds(first, 2), :]
                         at += 2
         for x in range(nx):
             out[pl.ds(at, 2), :] = coef[x, pl.ds(first, 2), :]
@@ -192,9 +191,52 @@
     return jnp.concatenate([tops[i], middle, ends[i]], 0)
 
 
-def edges_kernel(fields, coef, mirror_coef, theirs, y_low, y_high,
+def edge_planes(part, ks, nx, mark):
+    up, down = [], []
+    last = nx - 1
+    for f in range(2):
+        e = lambda c, x: part(f, 0, c, x)
+        h = lambda c, x: part(f, 1, c, x)
+        k = ks[last]
+        ex, ey, ez = e(0, last), e(1, last), e(2, last)
+        ex_b, ey_b, ez_b = e(0, last - 1), e(1, last - 1), e(2, last - 1)
+        hy_b = mark(h(1, last - 1) - COURANT * ((up_z(ex_b) - ex_b) - (ez - ez_b)), last - 1)
+        hz_b = mark(h(2, last - 1) - COURANT * ((ey - ey_b) - (up_y(ex_b) - ex_b)), last - 1)
+        hx = mark(h(0, last) - COURANT * ((up_y(ez) - ez) - (up_z(ey) - ey)), last)
+        hy = mark(h(1, last) - COURANT * ((up_z(ex) - ex) + ez), last)
+        hz = mark(h(2, last) - COURANT * (-ey - (up_y(ex) - ex)), last)
+        ex = ex + k * ((hz - down_y(hz)) - (hy - down_z(hy)))
+        ey = ey + k * ((hx - down_z(hx)) - (hz - hz_b))
+        ez = ez + k * ((hy - hy_b) - (hx - down_y(hx)))
+        up += [hy, hz, mark(hy - COURANT * ((up_z(ex) - ex) + ez), last),
+               mark(hz - COURANT * (-ey - (up_y(ex) - ex)), last)]
+        k = ks[0]
+        ex, ey, ez = e(0, 0), e(1, 0), e(2, 0)
+        hx = mark(h(0, 0) - COURANT * ((up_y(ez) - ez) - (up_z(ey) - ey)), 0)
+        hy = mark(h(1, 0) - COURANT * ((up_z(ex) - ex) - (e(2, 1) - ez)), 0)
+        hz = mark(h(2, 0) - COURANT * ((e(1, 1) - ey) - (up_y(ex) - ex)), 0)
+        down += [ey, ez, ey + k * ((hx - down_z(hx)) - hz), ez + k * (hy - (hx - down_y(hx)))]
+    return up + [ks[last]], down + [ks[0]]
+
+
+LATER = (2, 3, 6, 7, 8)
+SLIM = 6
+
+
+def bulk_kernel(ef, hf, ea, ha, eps, x_up, x_down):
+    nx, ny = eps.shape[0], eps.shape[1]
+    fields = ((ef, hf), (ea, ha))
+    ks = [COURANT / eps[x] if x in (0, nx - 1) else None for x in range(nx)]
+    up, down = edge_planes(lambda f, k, c, x: fields[f][k][c, x], ks, nx, lambda v, x: v)
+    for out, planes in ((x_up, up), (x_down, down)):
+        for i, plane in enumerate(planes):
+            out[pl.ds(i * ny, ny), :] = plane
+
+
+def edges_kernel(ef, hf, ea, ha, coef, mirror_coef, theirs, y_low, y_high,
                  tops, ends, mirror, x_up, x_down):
     nx, ny = coef.shape[0], coef.shape[1]
+    fields = ((ef, hf), (ea, ha))
     tops[...] = jnp.zeros_like(tops)
     ends[...] = jnp.zeros_like(ends)
     mirror[...] = jnp.zeros_like(mirror)
@@ -208,54 +250,32 @@
             row = TOP - 2 if out is tops else END
             mirror[c, pl.ds(row, 2), :] = source[pl.ds(26 * nx + 2 * c, 2), pl.ds(0, LANES)]
 
-    def put(out, plane, value):
-        out[pl.ds(plane * ny, ny), :] = value[TOP:END]
-        out[pl.ds(10 * ny + 4 * plane, 2), :] = value[TOP - 2:TOP]
-        out[pl.ds(10 * ny + 4 * plane + 2, 2), :] = value[END:END + 2]
-
     def part(f, k, c, x):
-        return framed(fields[f, k, c, x], tops, ends, plane_index(f, k, c, x, nx))
+        return framed(fields[f][k][c, x], tops, ends, plane_index(f, k, c, x, nx))
 
     ks = [framed(coef[x], tops, ends, 12 * nx + x) for x in range(nx)]
-    last = nx - 1
-    for f in range(2):
-        e = lambda c, x: part(f, 0, c, x)
-        h = lambda c, x: part(f, 1, c, x)
-        k, before = ks[last], ks[last - 1] > 0
-        inside = k > 0
-        ex, ey, ez = e(0, last), e(1, last), e(2, last)
-        ex_b, ey_b, ez_b = e(0, last - 1), e(1, last - 1), e(2, last - 1)
-        hy_b = jnp.where(before, h(1, last - 1) - COURANT * ((up_z(ex_b) - ex_b) - (ez - ez_b)), 0.0)
-        hz_b = jnp.where(before, h(2, last - 1) - COURANT * ((ey - ey_b) - (up_y(ex_b) - ex_b)), 0.0)
-        hx = jnp.where(inside, h(0, last) - COURANT * ((up_y(ez) - ez) - (up_z(ey) - ey)), 0.0)
-        hy = jnp.where(inside, h(1, last) - COURANT * ((up_z(ex) - ex) + ez), 0.0)
-        hz = jnp.where(inside, h(2, last) - COURANT * (-ey - (up_y(ex) - ex)), 0.0)
-        ex = ex + k * ((hz - down_y(hz)) - (hy - down_z(hy)))
-        ey = ey + k * ((hx - down_z(hx)) - (hz - hz_b))
-        ez = ez + k * ((hy - hy_b) - (hx - down_y(hx)))
-        put(x_up, 4 * f, hy)
-        put(x_up, 4 * f + 1, hz)
-        put(x_up, 4 * f + 2, jnp.where(inside, hy - COURANT * ((up_z(ex) - ex) + ez), 0.0))
-        put(x_up, 4 * f + 3, jnp.where(inside, hz - COURANT * (-ey - (up_y(ex) - ex)), 0.0))
-        k = ks[0]
-        inside = k > 0
-        ex, ey, ez = e(0, 0), e(1, 0), e(2, 0)
-        hx = jnp.where(inside, h(0, 0) - COURANT * ((up_y(ez) - ez) - (up_z(ey) - ey)), 0.0)
-        hy = jnp.where(inside, h(1, 0) - COURANT * ((up_z(ex) - ex) - (e(2, 1) - ez)), 0.0)
-        hz = jnp.where(inside, h(2, 0) - COURANT * ((e(1, 1) - ey) - (up_y(ex) - ex)), 0.0)
-        put(x_down, 4 * f, ey)
-        put(x_down, 4 * f + 1, ez)
-        put(x_down, 4 * f + 2, ey + k * ((hx - down_z(hx)) - hz))
-        put(x_down, 4 * f + 3, ez + k * (hy - (hx - down_y(hx))))
-    put(x_up, 8, ks[last])
-    put(x_down, 8, ks[0])
+    up, down = edge_planes(part, ks, nx, lambda v, x: jnp.where(ks[x] > 0, v, 0.0))
     m = [mirror[c] for c in range(3)]
     km = mirror[3]
-    first = lane_of(km.shape) % 64 < 32
-    put(x_up, 9, jnp.concatenate([jnp.where(first, m[0], turn(m[1], 32)),
-                                  jnp.where(first, m[2], turn(km, 32))], 1))
-    put(x_down, 9, jnp.concatenate([jnp.where(first, turn(m[1], -32), m[0]),
-                                    jnp.where(first, turn(km, -32), m[2])], 1))
+    lane = lane_of(km.shape)
+    first = lane % 64 < 32
+    up_m = [jnp.where(first, m[0], turn(m[1], 32)), jnp.where(first, m[2], turn(km, 32))]
+    down_m = [jnp.where(first, turn(m[1], -32), m[0]), jnp.where(first, turn(km, -32), m[2])]
+    for out, planes, window, base in ((x_up, up, up_m, 96), (x_down, down, down_m, 64)):
+        for i, plane in enumerate(planes):
+            out[pl.ds(8 * i, 4), :] = plane[TOP - 2:TOP + 2]
+            out[pl.ds(8 * i + 4, 4), :] = plane[END - 2:END + 2]
+        side = window[1]
+        for i, plane in enumerate(LATER):
+            plane = planes[plane]
+            near = jnp.where(lane >= LANES // 2, plane[:, :LANES], plane[:, LANES:])
+            part_in = turn(near, SHIFT + base + SLIM * i - 1)
+            inside = (lane >= base + SLIM * i) & (lane < base + SLIM * (i + 1))
+            side = jnp.where(inside, part_in, side)
+        value = jnp.concatenate([window[0], side], 1)
+        out[pl.ds(72, ny), :] = value[TOP:END]
+        out[pl.ds(72 + ny, 2), :] = value[TOP - 2:TOP]
+        out[pl.ds(74 + ny, 2), :] = value[END:END + 2]
 
 
 def slab_gradient(message, first, second, ny):
@@ -278,25 +298,38 @@
             out[pl.ds(p * nx + x, 1), :] = square[pl.ds(x * 16 + 2 + p, 1), :]
 
 
-def step_kernel(fields, coef, tops, ends, mirror, x_low, x_high, mine, theirs,
+def step_kernel(ef_in, hf_in, ea_in, ha_in, coef, tops, ends, mirror, bulk_low, bulk_high,
+                x_low, x_high, mine, theirs,
                 ef_out, hf_out, ea_out, ha_out, grad,
                 ee, hh, halo, square, table, lines, sems):
     nx, ny, nz = coef.shape
 
-    def take(source, plane, slot):
-        halo[slot, pl.ds(0, TOP), :] = jnp.zeros((TOP, nz), F32)
-        halo[slot, pl.ds(END, TOP), :] = jnp.zeros((TOP, nz), F32)
-        halo[slot, pl.ds(TOP, ny), :] = source[pl.ds(plane * ny, ny), :]
-        halo[slot, pl.ds(TOP - 2, 2), :] = source[pl.ds(10 * ny + 4 * plane, 2), :]
-        halo[slot, pl.ds(END, 2), :] = source[pl.ds(10 * ny + 4 * plane + 2, 2), :]
-
-    for plane in range(10):
-        take(x_low, plane, plane)
-        take(x_high, plane, 10 + plane)
+    fields = ((ef_in, hf_in), (ea_in, ha_in))
+    lane = lane_of((ny, LANES))
+    for bulk, source, slot, base in ((bulk_low, x_low, 0, 96), (bulk_high, x_high, 10, 64)):
+        halo[slot + 9, pl.ds(0, TOP), :] = jnp.zeros((TOP, nz), F32)
+        halo[slot + 9, pl.ds(END, TOP), :] = jnp.zeros((TOP, nz), F32)
+        halo[slot + 9, pl.ds(TOP, ny), :] = source[pl.ds(72, ny), :]
+        halo[slot + 9, pl.ds(TOP - 2, 2), :] = source[pl.ds(72 + ny, 2), :]
+        halo[slot + 9, pl.ds(END, 2), :] = source[pl.ds(74 + ny, 2), :]
+        side = source[pl.ds(72, ny), pl.ds(LANES, LANES)]
+        for plane in range(9):
+            at = slot + plane
+            halo[at, pl.ds(0, TOP), :] = jnp.zeros((TOP, nz), F32)
+            halo[at, pl.ds(END, TOP), :] = jnp.zeros((TOP, nz), F32)
+            value = bulk[pl.ds(plane * ny, ny), :]
+            if plane in LATER:
+                near = turn(side, 1 - SHIFT - base - SLIM * LATER.index(plane))
+                value = jnp.concatenate(
+                    [jnp.where(lane >= Z0 - 1, near, value[:, :LANES]),
+                     jnp.where(lane < Z0 + PLANES + 1 - LANES, near, value[:, LANES:])], 1)
+            halo[at, pl.ds(TOP, ny), :] = value
+            halo[at, pl.ds(TOP - 2, 4), :] = source[pl.ds(8 * plane, 4), :]
+            halo[at, pl.ds(END - 2, 4), :] = source[pl.ds(8 * plane + 4, 4), :]
     k_low, k_high = halo[8], halo[18]
 
     def part(f, k, c, x):
-        return framed(fields[f, k, c, x], tops, ends, plane_index(f, k, c, x, nx))
+        return framed(fields[f][k][c, x], tops, ends, plane_index(f, k, c, x, nx))
 
     def inverse(x):
         return framed(coef[x], tops, ends, 12 * nx + x)
@@ -418,7 +451,7 @@
         in_specs=spaces(len(args), len(args) if any_in else 0),
         out_specs=spaces(len(outs), any_out),
         scratch_shapes=list(scratch),
-        compiler_params=pltpu.CompilerParams(vmem_limit_bytes=VMEM_LIMIT),
+        compiler_params=pltpu.CompilerParams(vmem_limit_bytes=FAR_LIMIT if any_in else VMEM_LIMIT),
         cost_estimate=pl.CostEstimate(flops=4_000_000, bytes_accessed=4_000_000, transcendentals=0),
         name=name,
     )(*args)
@@ -440,29 +473,33 @@
     vmem = lambda *dims: pltpu.VMEM(dims, F32)
     square = vmem(LANES, LANES)
     lines = vmem(PLANES * nx, LANES)
-    fields_shape = shape(2, 2, 3, nx, ny, nz)
     block = shape(nx, ny, nz)
-
-    mine, fields, eps = call(
-        load_kernel, [shape(MESSAGE, LANES), fields_shape, block],
-        [e_fwd, h_fwd, e_adj, h_adj, eps_back, density, design_mask, partner_map, mon_fwd, mon_adj],
-        [vmem(*density.shape), pltpu.VMEM((2,) + density.shape, jnp.int32), vmem(2, *mon_fwd.shape),
-         square, pltpu.SemaphoreType.DMA((10,))], name="load", any_in=True)
+    fields = [e_fwd, h_fwd, e_adj, h_adj]
+
+    mine, = call(
+        message_kernel, [shape(MESSAGE, LANES)],
+        fields + [eps_back, density, design_mask, partner_map, mon_fwd, mon_adj],
+        [vmem(2, 2, 3, nx, ny, nz), vmem(nx, ny, nz), vmem(*density.shape),
+         pltpu.VMEM((2,) + density.shape, jnp.int32), vmem(2, *mon_fwd.shape),
+         square, pltpu.SemaphoreType.DMA((10,))], name="message", any_in=True)
     theirs = mirrored(mine, "gx")
+    bulk_shape = shape(9 * ny, nz)
+    bulk_up, bulk_down = call(bulk_kernel, [bulk_shape, bulk_shape], fields + [eps_back], name="bulk")
+    bulk_low, bulk_high = shifted(bulk_up, "gx", 1), shifted(bulk_down, "gx", -1)
     y_shape = shape(2 * (13 * nx) + 8, nz)
     coef, mirror_coef, y_up, y_down = call(
-        coef_kernel, [block, shape(ny, LANES), y_shape, y_shape], [eps, mine, theirs, fields],
+        coef_kernel, [block, shape(ny, LANES), y_shape, y_shape], [eps_back, mine, theirs] + fields,
         [lines, lines, square], name="coefficient")
     y_low, y_high = shifted(y_up, "gy", 1), shifted(y_down, "gy", -1)
-    x_shape = shape(10 * (ny + 4), nz)
+    x_shape = shape(9 * 8 + ny + 4, nz)
     tile = shape(13 * nx, 8, nz)
     tops, ends, mirror, x_up, x_down = call(
         edges_kernel, [tile, tile, shape(4, FRAME, LANES), x_shape, x_shape],
-        [fields, coef, mirror_coef, theirs, y_low, y_high], name="edges")
+        fields + [coef, mirror_coef, theirs, y_low, y_high], name="edges")
     x_low, x_high = shifted(x_up, "gx", 1), shifted(x_down, "gx", -1)
     ef, hf, ea, ha, grad = call(
         step_kernel, [shape(*e_fwd.shape)] * 4 + [shape(*density.shape)],
-        [fields, coef, tops, ends, mirror, x_low, x_high, mine, theirs],
+        fields + [coef, tops, ends, mirror, bulk_low, bulk_high, x_low, x_high, mine, theirs],
         [vmem(2, 3, nx + 1, FRAME, nz), vmem(2, 3, nx + 1, FRAME, nz), vmem(20, FRAME, nz),
          square, lines, lines, pltpu.SemaphoreType.DMA((4,))], name="steps", any_out=4)
     return ef, hf, ea, ha, grad

time: 68.7 us -> 55.2 us (0.80)
  the two profiles are of different devices: /device:TPU:37 before, /device:TPU:15 now
where the time goes in v3:
time: 55.2 us; the launch traced here: 54.9 us
  starting transfers between devices  32.8 us (59%)
  waiting for transfers between devices  13.2 us (24%)
  Pallas kernels  8.05 us (15%)
  between operations  0.83 us (2%)
    ppermute x6, starting transfers between devices, shifted(): lax.ppermute(block, axis, [(i - distance, i) for i in devices if i - dist...  21.6 us
    ppermute x1, starting transfers between devices, mirrored(): return lax.ppermute(block, axis, [(i, size - 1 - i) for i in range(size)])  11.1 us
    ppermute x6, waiting for transfers between devices, shifted(): lax.ppermute(block, axis, [(i - distance, i) for i in devices if i - dist...  10.7 us
    pallas_call x5, Pallas kernels, call(): pl.pallas_call(kernel, out_shape=outs, in_specs=spaces(len(args), len(arg...  8.05 us
    ppermute x1, waiting for transfers between devices, mirrored(): return lax.ppermute(block, axis, [(i, size - 1 - i) for i in range(size)])  2.48 us
  transfers between devices with their start and end apart: 7, of which 3 were waited for; matrix products, arithmetic and copies ran while one was open for 0% of the time, Pallas kernels for 3%

profile of v3, /device:TPU:15, one launch (start us, length us, event | category | flops | bytes accessed | tf_op | source)
XLA Modules:
  0.0 54.9 jit_solution(7955476798647701844)
XLA Ops:
  0.6 0.0 copy-start.3
  0.6 0.0 copy-start.2
  0.7 0.0 copy-start.1
  0.7 0.0 copy-start
  0.7 0.0 copy-start.4
  0.7 2.7 %message.1.mine = f32[192,128]{1,0:T(8,128)} custom-call(f32[3,4,32,256]{3,2,1,0:T(8,128)} %ef_in.1, f32[3,4,32,256]{3,2,1,0:T(8,128)} %hf_in.1, f32[3,4,32,256]{3,2,1,0:T(8,128)} %ea_in.1, f32[3,4,32,256]{3,2,1,0:T(8,128)} %ha_in.1, f32[4,32,256]{2,1,0:T(8,128)} %eps.5, f32[4,4,32]{2,1,0:T(4,128)} %density.1, s32[4,4,32]{2,1,0:T(4,128)} %mask.1, ...), custom_call_target="tpu_custom_call" | custom-call | flops 4000000 | bytes 4000000 | tf_op jit(solution)/shard_map/message/pallas_call | solution.py:448
  3.4 0.0 copy-start.5
  3.5 11.1 %collective-permute-start = (f32[192,128]{1,0:T(8,128)}, f32[192,128]{1,0:T(8,128)S(1)}, u32[]{:S(2)}, u32[]{:S(2)}) collective-permute-start(f32[192,128]{1,0:T(8,128)} %message.1.mine), channel_id=1, source_target_pairs={{0,496},{16,480},{32,464},{48,448},{64,432},{80,416},{96,400},{112... | collective-permute-start | bytes 294920 | tf_op jit(solution)/shard_map/ppermute | solution.py:467
  14.6 0.0 copy-done.3
  14.6 0.0 copy-done.2
  14.6 0.0 copy-done.1
  14.6 0.0 copy-done
  14.6 0.0 copy-done.4
  14.7 0.3 bulk.1
  15.0 4.5 %collective-permute-start.3 = (f32[288,256]{1,0:T(8,128)S(1)}, f32[288,256]{1,0:T(8,128)S(1)}, u32[]{:S(2)}, u32[]{:S(2)}) collective-permute-start(f32[288,256]{1,0:T(8,128)S(1)} %get-tuple-element.23), channel_id=1, source_target_pairs={{0,16},{16,32},{32,48},{48,64},{64,80},{80,96},{96,112},{112,128},... | collective-permute-start | bytes 884744 | tf_op jit(solution)/shard_map/ppermute | solution.py:462
  19.5 1.9 %collective-permute-start.4 = (f32[288,256]{1,0:T(8,128)S(1)}, f32[288,256]{1,0:T(8,128)S(1)}, u32[]{:S(2)}, u32[]{:S(2)}) collective-permute-start(f32[288,256]{1,0:T(8,128)S(1)} %get-tuple-element.24), channel_id=1, source_target_pairs={{16,0},{32,16},{48,32},{64,48},{80,64},{96,80},{112,96},{128,112},... | collective-permute-start | bytes 884744 | tf_op jit(solution)/shard_map/ppermute | solution.py:462
  21.5 2.5 %collective-permute-done.theirs = f32[192,128]{1,0:T(8,128)S(1)} collective-permute-done((f32[192,128]{1,0:T(8,128)}, f32[192,128]{1,0:T(8,128)S(1)}, u32[]{:S(2)}, u32[]{:S(2)}) %collective-permute-start) | collective-permute-done | bytes 98336 | tf_op jit(solution)/shard_map/ppermute | solution.py:467
  24.0 0.0 copy-done.5
  24.0 0.5 coefficient.1
  24.4 5.1 %collective-permute-start.1 = (f32[112,256]{1,0:T(8,128)S(1)}, f32[112,256]{1,0:T(8,128)S(1)}, u32[]{:S(2)}, u32[]{:S(2)}) collective-permute-start(f32[112,256]{1,0:T(8,128)S(1)} %get-tuple-element.18), channel_id=1, source_target_pairs={{0,1},{1,2},{2,3},{3,4},{4,5},{5,6},{6,7},{7,8},{8,9},{9,10},{10,1... | collective-permute-start | bytes 344072 | tf_op jit(solution)/shard_map/ppermute | solution.py:462
  29.5 1.9 %collective-permute-start.2 = (f32[112,256]{1,0:T(8,128)S(1)}, f32[112,256]{1,0:T(8,128)S(1)}, u32[]{:S(2)}, u32[]{:S(2)}) collective-permute-start(f32[112,256]{1,0:T(8,128)S(1)} %get-tuple-element.19), channel_id=1, source_target_pairs={{1,0},{2,1},{3,2},{4,3},{5,4},{6,5},{7,6},{8,7},{9,8},{10,9},{11,1... | collective-permute-start | bytes 344072 | tf_op jit(solution)/shard_map/ppermute | solution.py:462
  31.5 0.0 collective-permute-done.1.y_low
  31.5 5.7 %collective-permute-done.2.y_high = f32[112,256]{1,0:T(8,128)S(1)} collective-permute-done((f32[112,256]{1,0:T(8,128)S(1)}, f32[112,256]{1,0:T(8,128)S(1)}, u32[]{:S(2)}, u32[]{:S(2)}) %collective-permute-start.2) | collective-permute-done | bytes 114720 | tf_op jit(solution)/shard_map/ppermute | solution.py:462
  37.2 0.7 %edges.1 = (f32[52,8,256]{2,1,0:T(8,128)S(1)}, f32[52,8,256]{2,1,0:T(8,128)S(1)}, f32[4,48,128]{2,1,0:T(8,128)S(1)}, f32[108,256]{1,0:T(8,128)S(1)}, f32[108,256]{1,0:T(8,128)S(1)}) custom-call(f32[3,4,32,256]{3,2,1,0:T(8,128)S(1)} %copy-done, f32[3,4,32,256]{3,2,1,0:T(8,128)S(1)} %copy-done.1, f32[3,4,32,256]{3,2,1,0:T(8,128)S(1)} %copy-done.2, ...), custom_call_target="tpu_custom_call" | custom-call | flops 4000000 | bytes 4000000 | tf_op jit(solution)/shard_map/edges/pallas_call | solution.py:448
  37.9 6.2 %collective-permute-start.5 = (f32[108,256]{1,0:T(8,128)S(1)}, f32[108,256]{1,0:T(8,128)S(1)}, u32[]{:S(2)}, u32[]{:S(2)}) collective-permute-start(f32[108,256]{1,0:T(8,128)S(1)} %get-tuple-element.25), channel_id=1, source_target_pairs={{0,16},{16,32},{32,48},{48,64},{64,80},{80,96},{96,112},{112,128},... | collective-permute-start | bytes 331784 | tf_op jit(solution)/shard_map/ppermute | solution.py:462
  44.1 1.9 %collective-permute-start.6 = (f32[108,256]{1,0:T(8,128)S(1)}, f32[108,256]{1,0:T(8,128)S(1)}, u32[]{:S(2)}, u32[]{:S(2)}) collective-permute-start(f32[108,256]{1,0:T(8,128)S(1)} %get-tuple-element.26), channel_id=1, source_target_pairs={{16,0},{32,16},{48,32},{64,48},{80,64},{96,80},{112,96},{128,112},... | collective-permute-start | bytes 331784 | tf_op jit(solution)/shard_map/ppermute | solution.py:462
  46.0 0.0 collective-permute-done.3.bulk_low
  46.0 0.0 collective-permute-done.4.bulk_high
  46.1 0.0 collective-permute-done.5.x_low
  46.1 5.1 %collective-permute-done.6.x_high = f32[108,256]{1,0:T(8,128)S(1)} collective-permute-done((f32[108,256]{1,0:T(8,128)S(1)}, f32[108,256]{1,0:T(8,128)S(1)}, u32[]{:S(2)}, u32[]{:S(2)}) %collective-permute-start.6) | collective-permute-done | bytes 110624 | tf_op jit(solution)/shard_map/ppermute | solution.py:462
  51.1 3.8 %steps.1 = (f32[3,4,32,256]{3,2,1,0:T(8,128)}, f32[3,4,32,256]{3,2,1,0:T(8,128)}, f32[3,4,32,256]{3,2,1,0:T(8,128)}, f32[3,4,32,256]{3,2,1,0:T(8,128)}, f32[4,4,32]{2,1,0:T(4,128)}) custom-call(f32[3,4,32,256]{3,2,1,0:T(8,128)S(1)} %copy-done, f32[3,4,32,256]{3,2,1,0:T(8,128)S(1)} %copy-done.1, f32[3,4,32,256]{3,2,1,0:T(8,128)S(1)} %copy-done.2, ...), custom_call_target="tpu_custom_call" | custom-call | flops 4000000 | bytes 4000000 | tf_op jit(solution)/shard_map/steps/pallas_call | solution.py:448
Async XLA Ops:
  0.6 14.0 %copy-start.3 = (f32[3,4,32,256]{3,2,1,0:T(8,128)S(1)}, f32[3,4,32,256]{3,2,1,0:T(8,128)}, u32[]{:S(2)}) copy-start(f32[3,4,32,256]{3,2,1,0:T(8,128)} %ha_in.1) | copy-start | bytes 1179652
  0.6 14.0 %copy-start.2 = (f32[3,4,32,256]{3,2,1,0:T(8,128)S(1)}, f32[3,4,32,256]{3,2,1,0:T(8,128)}, u32[]{:S(2)}) copy-start(f32[3,4,32,256]{3,2,1,0:T(8,128)} %ea_in.1) | copy-start | bytes 1179652
  0.7 14.0 %copy-start.1 = (f32[3,4,32,256]{3,2,1,0:T(8,128)S(1)}, f32[3,4,32,256]{3,2,1,0:T(8,128)}, u32[]{:S(2)}) copy-start(f32[3,4,32,256]{3,2,1,0:T(8,128)} %hf_in.1) | copy-start | bytes 1179652
  0.7 14.0 %copy-start = (f32[3,4,32,256]{3,2,1,0:T(8,128)S(1)}, f32[3,4,32,256]{3,2,1,0:T(8,128)}, u32[]{:S(2)}) copy-start(f32[3,4,32,256]{3,2,1,0:T(8,128)} %ef_in.1) | copy-start | bytes 1179652
  0.7 14.0 %copy-start.4 = (f32[4,32,256]{2,1,0:T(8,128)S(1)}, f32[4,32,256]{2,1,0:T(8,128)}, u32[]{:S(2)}) copy-start(f32[4,32,256]{2,1,0:T(8,128)} %eps.5) | copy-start | bytes 393220
  3.4 20.5 %copy-start.5 = (f32[192,128]{1,0:T(8,128)S(1)}, f32[192,128]{1,0:T(8,128)}, u32[]{:S(2)}) copy-start(f32[192,128]{1,0:T(8,128)} %message.1.mine) | copy-start | bytes 294916
  3.5 20.5 %collective-permute-start = (f32[192,128]{1,0:T(8,128)}, f32[192,128]{1,0:T(8,128)S(1)}, u32[]{:S(2)}, u32[]{:S(2)}) collective-permute-start(f32[192,128]{1,0:T(8,128)} %message.1.mine), channel_id=1, source_target_pairs={{0,496},{16,480},{32,464},{48,448},{64,432},{80,416},{96,400},{112... | collective-permute-start | bytes 294920 | tf_op jit(solution)/shard_map/ppermute | solution.py:467
  15.0 31.1 %collective-permute-start.3 = (f32[288,256]{1,0:T(8,128)S(1)}, f32[288,256]{1,0:T(8,128)S(1)}, u32[]{:S(2)}, u32[]{:S(2)}) collective-permute-start(f32[288,256]{1,0:T(8,128)S(1)} %get-tuple-element.23), channel_id=1, source_target_pairs={{0,16},{16,32},{32,48},{48,64},{64,80},{80,96},{96,112},{112,128},... | collective-permute-start | bytes 884744 | tf_op jit(solution)/shard_map/ppermute | solution.py:462
  19.5 26.5 %collective-permute-start.4 = (f32[288,256]{1,0:T(8,128)S(1)}, f32[288,256]{1,0:T(8,128)S(1)}, u32[]{:S(2)}, u32[]{:S(2)}) collective-permute-start(f32[288,256]{1,0:T(8,128)S(1)} %get-tuple-element.24), channel_id=1, source_target_pairs={{16,0},{32,16},{48,32},{64,48},{80,64},{96,80},{112,96},{128,112},... | collective-permute-start | bytes 884744 | tf_op jit(solution)/shard_map/ppermute | solution.py:462
  24.4 7.1 %collective-permute-start.1 = (f32[112,256]{1,0:T(8,128)S(1)}, f32[112,256]{1,0:T(8,128)S(1)}, u32[]{:S(2)}, u32[]{:S(2)}) collective-permute-start(f32[112,256]{1,0:T(8,128)S(1)} %get-tuple-element.18), channel_id=1, source_target_pairs={{0,1},{1,2},{2,3},{3,4},{4,5},{5,6},{6,7},{7,8},{8,9},{9,10},{10,1... | collective-permute-start | bytes 344072 | tf_op jit(solution)/shard_map/ppermute | solution.py:462
  29.5 7.6 %collective-permute-start.2 = (f32[112,256]{1,0:T(8,128)S(1)}, f32[112,256]{1,0:T(8,128)S(1)}, u32[]{:S(2)}, u32[]{:S(2)}) collective-permute-start(f32[112,256]{1,0:T(8,128)S(1)} %get-tuple-element.19), channel_id=1, source_target_pairs={{1,0},{2,1},{3,2},{4,3},{5,4},{6,5},{7,6},{8,7},{9,8},{10,9},{11,1... | collective-permute-start | bytes 344072 | tf_op jit(solution)/shard_map/ppermute | solution.py:462
  37.9 8.2 %collective-permute-start.5 = (f32[108,256]{1,0:T(8,128)S(1)}, f32[108,256]{1,0:T(8,128)S(1)}, u32[]{:S(2)}, u32[]{:S(2)}) collective-permute-start(f32[108,256]{1,0:T(8,128)S(1)} %get-tuple-element.25), channel_id=1, source_target_pairs={{0,16},{16,32},{32,48},{48,64},{64,80},{80,96},{96,112},{112,128},... | collective-permute-start | bytes 331784 | tf_op jit(solution)/shard_map/ppermute | solution.py:462
  44.1 7.0 %collective-permute-start.6 = (f32[108,256]{1,0:T(8,128)S(1)}, f32[108,256]{1,0:T(8,128)S(1)}, u32[]{:S(2)}, u32[]{:S(2)}) collective-permute-start(f32[108,256]{1,0:T(8,128)S(1)} %get-tuple-element.26), channel_id=1, source_target_pairs={{16,0},{32,16},{48,32},{64,48},{80,64},{96,80},{112,96},{128,112},... | collective-permute-start | bytes 331784 | tf_op jit(solution)/shard_map/ppermute | solution.py:462

commit v4 on v3

--- a/solution.py
+++ b/solution.py
@@ -52,6 +52,14 @@
 
 def down_z(a):
     return jnp.where(lane_of(a.shape) == 0, 0.0, pltpu.roll(a, 1, 1))
+
+
+def is_odd(axis):
+    return lax.axis_index(axis) % 2 == 1
+
+
+def ordered(odd, up, down):
+    return jnp.where(odd, up, down), jnp.where(odd, down, up)
 
 
 def pack_planes(planes):
@@ -147,7 +155,7 @@
     return jnp.transpose(square[...])[:ny]
 
 
-def coef_kernel(eps, mine, theirs, ef, hf, ea, ha, coef, mirror_coef, y_up, y_down, table, lines, square):
+def coef_kernel(eps, mine, theirs, ef, hf, ea, ha, coef, mirror_coef, y_far, y_near, table, lines, square):
     nx = eps.shape[0]
     ny = END - TOP
     weight, density, partner = small_parts(mine)
@@ -165,22 +173,26 @@
         coef[x] = COURANT / (eps[x] + jnp.concatenate([low, high], 1))
     packed = theirs[pl.ds(ROW_EPS, ny), :] + spread_slab(extra_m, lines, square, nx, ny)
     mirror_coef[...] = jnp.where(lane < 64, COURANT / jnp.where(lane < 64, packed, 1.0), 0.0)
-    for out, first in ((y_up, ny - 2), (y_down, 0)):
-        at = 0
-        for f in range(2):
-            for k in range(2):
-                for c in range(3):
-                    for x in range(nx):
-                        out[pl.ds(at, 2), :] = ((ef, hf), (ea, ha))[f][k][c, x, pl.ds(first, 2), :]
-                        at += 2
-        for x in range(nx):
-            out[pl.ds(at, 2), :] = coef[x, pl.ds(first, 2), :]
-            at += 2
-        out[pl.ds(at, 8), :] = jnp.zeros((8, out.shape[1]), F32)
-        for c in range(3):
-            out[pl.ds(at, 2), pl.ds(0, LANES)] = theirs[pl.ds(c * 32 + first, 2), :]
-            at += 2
-        out[pl.ds(at, 2), pl.ds(0, LANES)] = mirror_coef[pl.ds(first, 2), :]
+    odd = is_odd("gy")
+
+    def put(at, ref, lanes):
+        far, near = ordered(odd, ref[pl.ds(ny - 2, 2), :], ref[pl.ds(0, 2), :])
+        y_far[pl.ds(at, 2), pl.ds(0, lanes)] = far
+        y_near[pl.ds(at, 2), pl.ds(0, lanes)] = near
+
+    for f, pair in enumerate(((ef, hf), (ea, ha))):
+        for k, field in enumerate(pair):
+            for c in range(3):
+                for x in range(nx):
+                    put(2 * plane_index(f, k, c, x, nx), field.at[c, x], y_far.shape[1])
+    for x in range(nx):
+        put(24 * nx + 2 * x, coef.at[x], y_far.shape[1])
+    rest = jnp.zeros((8, y_far.shape[1]), F32)
+    y_far[pl.ds(26 * nx, 8), :] = rest
+    y_near[pl.ds(26 * nx, 8), :] = rest
+    for c in range(3):
+        put(26 * nx + 2 * c, theirs.at[pl.ds(c * 32, ny), :], LANES)
+    put(26 * nx + 6, mirror_coef, LANES)
 
 
 def plane_index(f, k, c, x, nx):
@@ -223,18 +235,20 @@
 SLIM = 6
 
 
-def bulk_kernel(ef, hf, ea, ha, eps, x_up, x_down):
+def bulk_kernel(ef, hf, ea, ha, eps, x_far, x_near):
     nx, ny = eps.shape[0], eps.shape[1]
     fields = ((ef, hf), (ea, ha))
     ks = [COURANT / eps[x] if x in (0, nx - 1) else None for x in range(nx)]
     up, down = edge_planes(lambda f, k, c, x: fields[f][k][c, x], ks, nx, lambda v, x: v)
-    for out, planes in ((x_up, up), (x_down, down)):
-        for i, plane in enumerate(planes):
-            out[pl.ds(i * ny, ny), :] = plane
-
-
-def edges_kernel(ef, hf, ea, ha, coef, mirror_coef, theirs, y_low, y_high,
-                 tops, ends, mirror, x_up, x_down):
+    odd = is_odd("gx")
+    for i, planes in enumerate(zip(up, down)):
+        far, near = ordered(odd, *planes)
+        x_far[pl.ds(i * ny, ny), :] = far
+        x_near[pl.ds(i * ny, ny), :] = near
+
+
+def edges_kernel(ef, hf, ea, ha, coef, mirror_coef, theirs, y_far, y_near,
+                 tops, ends, mirror, x_far, x_near, x_up, x_down):
     nx, ny = coef.shape[0], coef.shape[1]
     fields = ((ef, hf), (ea, ha))
     tops[...] = jnp.zeros_like(tops)
@@ -243,12 +257,20 @@
     for c in range(3):
         mirror[c, pl.ds(TOP, ny), :] = theirs[pl.ds(c * 32, ny), :]
     mirror[3, pl.ds(TOP, ny), :] = mirror_coef[...]
-    for source, out, first in ((y_low, tops, TOP - 2), (y_high, ends, 0)):
-        for i in range(13 * nx):
-            out[i, pl.ds(first, 2), :] = source[pl.ds(2 * i, 2), :]
-        for c in range(4):
-            row = TOP - 2 if out is tops else END
-            mirror[c, pl.ds(row, 2), :] = source[pl.ds(26 * nx + 2 * c, 2), pl.ds(0, LANES)]
+    odd = is_odd("gy")
+
+    def came(at, lanes):
+        high, low = ordered(odd, y_far[pl.ds(at, 2), pl.ds(0, lanes)], y_near[pl.ds(at, 2), pl.ds(0, lanes)])
+        return low, high
+
+    for i in range(13 * nx):
+        low, high = came(2 * i, y_far.shape[1])
+        tops[i, pl.ds(TOP - 2, 2), :] = low
+        ends[i, pl.ds(0, 2), :] = high
+    for c in range(4):
+        low, high = came(26 * nx + 2 * c, LANES)
+        mirror[c, pl.ds(TOP - 2, 2), :] = low
+        mirror[c, pl.ds(END, 2), :] = high
 
     def part(f, k, c, x):
         return framed(fields[f][k][c, x], tops, ends, plane_index(f, k, c, x, nx))
@@ -276,6 +298,7 @@
         out[pl.ds(72, ny), :] = value[TOP:END]
         out[pl.ds(72 + ny, 2), :] = value[TOP - 2:TOP]
         out[pl.ds(74 + ny, 2), :] = value[END:END + 2]
+    x_far[...], x_near[...] = ordered(is_odd("gx"), x_up[...], x_down[...])
 
 
 def slab_gradient(message, first, second, ny):
@@ -298,34 +321,44 @@
             out[pl.ds(p * nx + x, 1), :] = square[pl.ds(x * 16 + 2 + p, 1), :]
 
 
-def step_kernel(ef_in, hf_in, ea_in, ha_in, coef, tops, ends, mirror, bulk_low, bulk_high,
-                x_low, x_high, mine, theirs,
+def step_kernel(ef_in, hf_in, ea_in, ha_in, coef, tops, ends, mirror, bulk_far, bulk_near,
+                x_far, x_near, mine, theirs,
                 ef_out, hf_out, ea_out, ha_out, grad,
                 ee, hh, halo, square, table, lines, sems):
     nx, ny, nz = coef.shape
 
     fields = ((ef_in, hf_in), (ea_in, ha_in))
     lane = lane_of((ny, LANES))
-    for bulk, source, slot, base in ((bulk_low, x_low, 0, 96), (bulk_high, x_high, 10, 64)):
+    odd = is_odd("gx")
+    for slot, base in ((0, 96), (10, 64)):
+        def source_at(row, rows, slot=slot):
+            pair = (x_near, x_far) if slot == 0 else (x_far, x_near)
+            return jnp.where(odd, pair[0][pl.ds(row, rows), :], pair[1][pl.ds(row, rows), :])
+
+        def bulk_at(row, rows, slot=slot):
+            pair = (bulk_near, bulk_far) if slot == 0 else (bulk_far, bulk_near)
+            return jnp.where(odd, pair[0][pl.ds(row, rows), :], pair[1][pl.ds(row, rows), :])
+
         halo[slot + 9, pl.ds(0, TOP), :] = jnp.zeros((TOP, nz), F32)
         halo[slot + 9, pl.ds(END, TOP), :] = jnp.zeros((TOP, nz), F32)
-        halo[slot + 9, pl.ds(TOP, ny), :] = source[pl.ds(72, ny), :]
-        halo[slot + 9, pl.ds(TOP - 2, 2), :] = source[pl.ds(72 + ny, 2), :]
-        halo[slot + 9, pl.ds(END, 2), :] = source[pl.ds(74 + ny, 2), :]
-        side = source[pl.ds(72, ny), pl.ds(LANES, LANES)]
+        window = source_at(72, ny)
+        halo[slot + 9, pl.ds(TOP, ny), :] = window
+        halo[slot + 9, pl.ds(TOP - 2, 2), :] = source_at(72 + ny, 2)
+        halo[slot + 9, pl.ds(END, 2), :] = source_at(74 + ny, 2)
+        side = window[:, LANES:]
         for plane in range(9):
             at = slot + plane
             halo[at, pl.ds(0, TOP), :] = jnp.zeros((TOP, nz), F32)
             halo[at, pl.ds(END, TOP), :] = jnp.zeros((TOP, nz), F32)
-            value = bulk[pl.ds(plane * ny, ny), :]
+            value = bulk_at(plane * ny, ny)
             if plane in LATER:
                 near = turn(side, 1 - SHIFT - base - SLIM * LATER.index(plane))
                 value = jnp.concatenate(
                     [jnp.where(lane >= Z0 - 1, near, value[:, :LANES]),
                      jnp.where(lane < Z0 + PLANES + 1 - LANES, near, value[:, LANES:])], 1)
             halo[at, pl.ds(TOP, ny), :] = value
-            halo[at, pl.ds(TOP - 2, 4), :] = source[pl.ds(8 * plane, 4), :]
-            halo[at, pl.ds(END - 2, 4), :] = source[pl.ds(8 * plane + 4, 4), :]
+            halo[at, pl.ds(TOP - 2, 4), :] = source_at(8 * plane, 4)
+            halo[at, pl.ds(END - 2, 4), :] = source_at(8 * plane + 4, 4)
     k_low, k_high = halo[8], halo[18]
 
     def part(f, k, c, x):
@@ -457,9 +490,12 @@
     )(*args)
 
 
-def shifted(block, axis, distance):
-    devices = range(lax.axis_size(axis))
-    return lax.ppermute(block, axis, [(i - distance, i) for i in devices if i - distance in devices])
+def swapped(far, near, axis):
+    def pairs(first):
+        lows = range(first, lax.axis_size(axis) - 1, 2)
+        return [(i, i + 1) for i in lows] + [(i + 1, i) for i in lows]
+
+    return lax.ppermute(far, axis, pairs(1)), lax.ppermute(near, axis, pairs(0))
 
 
 def mirrored(block, axis):
@@ -484,22 +520,23 @@
          square, pltpu.SemaphoreType.DMA((10,))], name="message", any_in=True)
     theirs = mirrored(mine, "gx")
     bulk_shape = shape(9 * ny, nz)
-    bulk_up, bulk_down = call(bulk_kernel, [bulk_shape, bulk_shape], fields + [eps_back], name="bulk")
-    bulk_low, bulk_high = shifted(bulk_up, "gx", 1), shifted(bulk_down, "gx", -1)
+    bulk = call(bulk_kernel, [bulk_shape, bulk_shape], fields + [eps_back], name="bulk")
+    bulk_far, bulk_near = swapped(*bulk, "gx")
     y_shape = shape(2 * (13 * nx) + 8, nz)
-    coef, mirror_coef, y_up, y_down = call(
+    coef, mirror_coef, y_far, y_near = call(
         coef_kernel, [block, shape(ny, LANES), y_shape, y_shape], [eps_back, mine, theirs] + fields,
         [lines, lines, square], name="coefficient")
-    y_low, y_high = shifted(y_up, "gy", 1), shifted(y_down, "gy", -1)
+    y_far, y_near = swapped(y_far, y_near, "gy")
     x_shape = shape(9 * 8 + ny + 4, nz)
     tile = shape(13 * nx, 8, nz)
-    tops, ends, mirror, x_up, x_down = call(
+    tops, ends, mirror, x_far, x_near = call(
         edges_kernel, [tile, tile, shape(4, FRAME, LANES), x_shape, x_shape],
-        fields + [coef, mirror_coef, theirs, y_low, y_high], name="edges")
-    x_low, x_high = shifted(x_up, "gx", 1), shifted(x_down, "gx", -1)
+        fields + [coef, mirror_coef, theirs, y_far, y_near],
+        [vmem(*x_shape.shape)] * 2, name="edges")
+    x_far, x_near = swapped(x_far, x_near, "gx")
     ef, hf, ea, ha, grad = call(
         step_kernel, [shape(*e_fwd.shape)] * 4 + [shape(*density.shape)],
-        fields + [coef, tops, ends, mirror, bulk_low, bulk_high, x_low, x_high, mine, theirs],
+        fields + [coef, tops, ends, mirror, bulk_far, bulk_near, x_far, x_near, mine, theirs],
         [vmem(2, 3, nx + 1, FRAME, nz), vmem(2, 3, nx + 1, FRAME, nz), vmem(20, FRAME, nz),
          square, lines, lines, pltpu.SemaphoreType.DMA((4,))], name="steps", any_out=4)
     return ef, hf, ea, ha, grad

time: 55.2 us -> 56.2 us (1.018)
  starting transfers between devices: 32.8 us -> 38 us
  waiting for transfers between devices: 13.2 us -> 8.82 us
    ppermute x6, starting transfers between devices: 21.6 us -> 26.8 us  [the longest x3 21.1 us: swapped(): lax.ppermute(far, axis, pairs(1))]
    ppermute x6, waiting for transfers between devices: 10.7 us -> 6.37 us  [the longest x3 3.37 us: swapped(): lax.ppermute(near, axis, pairs(0))]
  transfers between devices with their start and end apart: 7 -> 7, of which waited for: 3 -> 4; matrix products, arithmetic and copies ran while one was open for 0% -> 0% of each run, Pallas kernels for 3% -> 3%
where the time goes in v4:
time: 56.2 us; the launch traced here: 55.9 us
  starting transfers between devices  38 us (68%)
  waiting for transfers between devices  8.82 us (16%)
  Pallas kernels  8.25 us (15%)
  between operations  0.82 us (1%)
    ppermute x3, starting transfers between devices, swapped(): lax.ppermute(far, axis, pairs(1))  21.1 us
    ppermute x1, starting transfers between devices, mirrored(): return lax.ppermute(block, axis, [(i, size - 1 - i) for i in range(size)])  11.1 us
    pallas_call x5, Pallas kernels, call(): pl.pallas_call(kernel, out_shape=outs, in_specs=spaces(len(args), len(arg...  8.25 us
    ppermute x3, starting transfers between devices, swapped(): lax.ppermute(near, axis, pairs(0))  5.76 us
    ppermute x3, waiting for transfers between devices, swapped(): lax.ppermute(near, axis, pairs(0))  3.37 us
    ppermute x3, waiting for transfers between devices, swapped(): lax.ppermute(far, axis, pairs(1))  3 us
    ppermute x1, waiting for transfers between devices, mirrored(): return lax.ppermute(block, axis, [(i, size - 1 - i) for i in range(size)])  2.45 us
  transfers between devices with their start and end apart: 7, of which 4 were waited for; matrix products, arithmetic and copies ran while one was open for 0% of the time, Pallas kernels for 3%

profile of v4, /device:TPU:15, one launch (start us, length us, event | category | flops | bytes accessed | tf_op | source)
XLA Modules:
  0.0 55.9 jit_solution(17168480786849771981)
XLA Ops:
  0.6 0.0 copy-start.3
  0.6 0.0 copy-start.2
  0.7 0.0 copy-start.1
  0.7 0.0 copy-start
  0.7 0.0 copy-start.4
  0.7 2.7 %message.1.mine = f32[192,128]{1,0:T(8,128)} custom-call(f32[3,4,32,256]{3,2,1,0:T(8,128)} %ef_in.1, f32[3,4,32,256]{3,2,1,0:T(8,128)} %hf_in.1, f32[3,4,32,256]{3,2,1,0:T(8,128)} %ea_in.1, f32[3,4,32,256]{3,2,1,0:T(8,128)} %ha_in.1, f32[4,32,256]{2,1,0:T(8,128)} %eps.5, f32[4,4,32]{2,1,0:T(4,128)} %density.1, s32[4,4,32]{2,1,0:T(4,128)} %mask.1, ...), custom_call_target="tpu_custom_call" | custom-call | flops 4000000 | bytes 4000000 | tf_op jit(solution)/shard_map/message/pallas_call | solution.py:481
  3.4 0.0 copy-start.5
  3.5 11.1 %collective-permute-start = (f32[192,128]{1,0:T(8,128)}, f32[192,128]{1,0:T(8,128)S(1)}, u32[]{:S(2)}, u32[]{:S(2)}) collective-permute-start(f32[192,128]{1,0:T(8,128)} %message.1.mine), channel_id=1, source_target_pairs={{0,496},{16,480},{32,464},{48,448},{64,432},{80,416},{96,400},{112... | collective-permute-start | bytes 294920 | tf_op jit(solution)/shard_map/ppermute | solution.py:503
  14.6 0.0 copy-done.3
  14.6 0.0 copy-done.2
  14.6 0.0 copy-done.1
  14.6 0.0 copy-done
  14.6 0.0 copy-done.4
  14.7 0.4 bulk.1
  15.0 4.5 %collective-permute-start.3 = (f32[288,256]{1,0:T(8,128)S(1)}, f32[288,256]{1,0:T(8,128)S(1)}, u32[]{:S(2)}, u32[]{:S(2)}) collective-permute-start(f32[288,256]{1,0:T(8,128)S(1)} %get-tuple-element.23), channel_id=1, source_target_pairs={{16,32},{48,64},{80,96},{112,128},{144,160},{176,192},{208,224},{2... | collective-permute-start | bytes 884744 | tf_op jit(solution)/shard_map/ppermute | solution.py:498
  19.6 1.9 %collective-permute-start.4 = (f32[288,256]{1,0:T(8,128)S(1)}, f32[288,256]{1,0:T(8,128)S(1)}, u32[]{:S(2)}, u32[]{:S(2)}) collective-permute-start(f32[288,256]{1,0:T(8,128)S(1)} %get-tuple-element.24), channel_id=1, source_target_pairs={{0,16},{32,48},{64,80},{96,112},{128,144},{160,176},{192,208},{224... | collective-permute-start | bytes 884744 | tf_op jit(solution)/shard_map/ppermute | solution.py:498
  21.5 2.5 %collective-permute-done.theirs = f32[192,128]{1,0:T(8,128)S(1)} collective-permute-done((f32[192,128]{1,0:T(8,128)}, f32[192,128]{1,0:T(8,128)S(1)}, u32[]{:S(2)}, u32[]{:S(2)}) %collective-permute-start) | collective-permute-done | bytes 98336 | tf_op jit(solution)/shard_map/ppermute | solution.py:503
  24.0 0.0 copy-done.5
  24.0 0.5 coefficient.1
  24.4 5.4 %collective-permute-start.1 = (f32[112,256]{1,0:T(8,128)S(1)}, f32[112,256]{1,0:T(8,128)S(1)}, u32[]{:S(2)}, u32[]{:S(2)}) collective-permute-start(f32[112,256]{1,0:T(8,128)S(1)} %get-tuple-element.18), channel_id=1, source_target_pairs={{1,2},{3,4},{5,6},{7,8},{9,10},{11,12},{13,14},{2,1},{4,3},{6,5},{... | collective-permute-start | bytes 344072 | tf_op jit(solution)/shard_map/ppermute | solution.py:498
  29.9 1.9 %collective-permute-start.2 = (f32[112,256]{1,0:T(8,128)S(1)}, f32[112,256]{1,0:T(8,128)S(1)}, u32[]{:S(2)}, u32[]{:S(2)}) collective-permute-start(f32[112,256]{1,0:T(8,128)S(1)} %get-tuple-element.19), channel_id=1, source_target_pairs={{0,1},{2,3},{4,5},{6,7},{8,9},{10,11},{12,13},{14,15},{1,0},{3,2},... | collective-permute-start | bytes 344072 | tf_op jit(solution)/shard_map/ppermute | solution.py:498
  31.8 2.8 %collective-permute-done.1.y_far = f32[112,256]{1,0:T(8,128)S(1)} collective-permute-done((f32[112,256]{1,0:T(8,128)S(1)}, f32[112,256]{1,0:T(8,128)S(1)}, u32[]{:S(2)}, u32[]{:S(2)}) %collective-permute-start.1) | collective-permute-done | bytes 114720 | tf_op jit(solution)/shard_map/ppermute | solution.py:498
  34.6 0.0 collective-permute-done.2.y_near
  34.6 0.8 %edges.1 = (f32[52,8,256]{2,1,0:T(8,128)S(1)}, f32[52,8,256]{2,1,0:T(8,128)S(1)}, f32[4,48,128]{2,1,0:T(8,128)S(1)}, f32[108,256]{1,0:T(8,128)S(1)}, f32[108,256]{1,0:T(8,128)S(1)}) custom-call(f32[3,4,32,256]{3,2,1,0:T(8,128)S(1)} %copy-done, f32[3,4,32,256]{3,2,1,0:T(8,128)S(1)} %copy-done.1, f32[3,4,32,256]{3,2,1,0:T(8,128)S(1)} %copy-done.2, ...), custom_call_target="tpu_custom_call" | custom-call | flops 4000000 | bytes 4000000 | tf_op jit(solution)/shard_map/edges/pallas_call | solution.py:481
  35.4 11.1 %collective-permute-start.5 = (f32[108,256]{1,0:T(8,128)S(1)}, f32[108,256]{1,0:T(8,128)S(1)}, u32[]{:S(2)}, u32[]{:S(2)}) collective-permute-start(f32[108,256]{1,0:T(8,128)S(1)} %get-tuple-element.25), channel_id=1, source_target_pairs={{16,32},{48,64},{80,96},{112,128},{144,160},{176,192},{208,224},{2... | collective-permute-start | bytes 331784 | tf_op jit(solution)/shard_map/ppermute | solution.py:498
  46.5 1.9 %collective-permute-start.6 = (f32[108,256]{1,0:T(8,128)S(1)}, f32[108,256]{1,0:T(8,128)S(1)}, u32[]{:S(2)}, u32[]{:S(2)}) collective-permute-start(f32[108,256]{1,0:T(8,128)S(1)} %get-tuple-element.26), channel_id=1, source_target_pairs={{0,16},{32,48},{64,80},{96,112},{128,144},{160,176},{192,208},{224... | collective-permute-start | bytes 331784 | tf_op jit(solution)/shard_map/ppermute | solution.py:498
  48.4 0.0 collective-permute-done.3.bulk_far
  48.4 0.0 collective-permute-done.4.bulk_near
  48.4 0.2 collective-permute-done.5.x_far
  48.6 3.4 %collective-permute-done.6.x_near = f32[108,256]{1,0:T(8,128)S(1)} collective-permute-done((f32[108,256]{1,0:T(8,128)S(1)}, f32[108,256]{1,0:T(8,128)S(1)}, u32[]{:S(2)}, u32[]{:S(2)}) %collective-permute-start.6) | collective-permute-done | bytes 110624 | tf_op jit(solution)/shard_map/ppermute | solution.py:498
  52.0 3.9 %steps.1 = (f32[3,4,32,256]{3,2,1,0:T(8,128)}, f32[3,4,32,256]{3,2,1,0:T(8,128)}, f32[3,4,32,256]{3,2,1,0:T(8,128)}, f32[3,4,32,256]{3,2,1,0:T(8,128)}, f32[4,4,32]{2,1,0:T(4,128)}) custom-call(f32[3,4,32,256]{3,2,1,0:T(8,128)S(1)} %copy-done, f32[3,4,32,256]{3,2,1,0:T(8,128)S(1)} %copy-done.1, f32[3,4,32,256]{3,2,1,0:T(8,128)S(1)} %copy-done.2, ...), custom_call_target="tpu_custom_call" | custom-call | flops 4000000 | bytes 4000000 | tf_op jit(solution)/shard_map/steps/pallas_call | solution.py:481
Async XLA Ops:
  0.6 14.0 %copy-start.3 = (f32[3,4,32,256]{3,2,1,0:T(8,128)S(1)}, f32[3,4,32,256]{3,2,1,0:T(8,128)}, u32[]{:S(2)}) copy-start(f32[3,4,32,256]{3,2,1,0:T(8,128)} %ha_in.1) | copy-start | bytes 1179652
  0.6 14.0 %copy-start.2 = (f32[3,4,32,256]{3,2,1,0:T(8,128)S(1)}, f32[3,4,32,256]{3,2,1,0:T(8,128)}, u32[]{:S(2)}) copy-start(f32[3,4,32,256]{3,2,1,0:T(8,128)} %ea_in.1) | copy-start | bytes 1179652
  0.7 14.0 %copy-start.1 = (f32[3,4,32,256]{3,2,1,0:T(8,128)S(1)}, f32[3,4,32,256]{3,2,1,0:T(8,128)}, u32[]{:S(2)}) copy-start(f32[3,4,32,256]{3,2,1,0:T(8,128)} %hf_in.1) | copy-start | bytes 1179652
  0.7 14.0 %copy-start = (f32[3,4,32,256]{3,2,1,0:T(8,128)S(1)}, f32[3,4,32,256]{3,2,1,0:T(8,128)}, u32[]{:S(2)}) copy-start(f32[3,4,32,256]{3,2,1,0:T(8,128)} %ef_in.1) | copy-start | bytes 1179652
  0.7 14.0 %copy-start.4 = (f32[4,32,256]{2,1,0:T(8,128)S(1)}, f32[4,32,256]{2,1,0:T(8,128)}, u32[]{:S(2)}) copy-start(f32[4,32,256]{2,1,0:T(8,128)} %eps.5) | copy-start | bytes 393220
  3.4 20.5 %copy-start.5 = (f32[192,128]{1,0:T(8,128)S(1)}, f32[192,128]{1,0:T(8,128)}, u32[]{:S(2)}) copy-start(f32[192,128]{1,0:T(8,128)} %message.1.mine) | copy-start | bytes 294916
  3.5 20.5 %collective-permute-start = (f32[192,128]{1,0:T(8,128)}, f32[192,128]{1,0:T(8,128)S(1)}, u32[]{:S(2)}, u32[]{:S(2)}) collective-permute-start(f32[192,128]{1,0:T(8,128)} %message.1.mine), channel_id=1, source_target_pairs={{0,496},{16,480},{32,464},{48,448},{64,432},{80,416},{96,400},{112... | collective-permute-start | bytes 294920 | tf_op jit(solution)/shard_map/ppermute | solution.py:503
  15.0 33.4 %collective-permute-start.3 = (f32[288,256]{1,0:T(8,128)S(1)}, f32[288,256]{1,0:T(8,128)S(1)}, u32[]{:S(2)}, u32[]{:S(2)}) collective-permute-start(f32[288,256]{1,0:T(8,128)S(1)} %get-tuple-element.23), channel_id=1, source_target_pairs={{16,32},{48,64},{80,96},{112,128},{144,160},{176,192},{208,224},{2... | collective-permute-start | bytes 884744 | tf_op jit(solution)/shard_map/ppermute | solution.py:498
  19.6 28.8 %collective-permute-start.4 = (f32[288,256]{1,0:T(8,128)S(1)}, f32[288,256]{1,0:T(8,128)S(1)}, u32[]{:S(2)}, u32[]{:S(2)}) collective-permute-start(f32[288,256]{1,0:T(8,128)S(1)} %get-tuple-element.24), channel_id=1, source_target_pairs={{0,16},{32,48},{64,80},{96,112},{128,144},{160,176},{192,208},{224... | collective-permute-start | bytes 884744 | tf_op jit(solution)/shard_map/ppermute | solution.py:498
  24.4 10.1 %collective-permute-start.1 = (f32[112,256]{1,0:T(8,128)S(1)}, f32[112,256]{1,0:T(8,128)S(1)}, u32[]{:S(2)}, u32[]{:S(2)}) collective-permute-start(f32[112,256]{1,0:T(8,128)S(1)} %get-tuple-element.18), channel_id=1, source_target_pairs={{1,2},{3,4},{5,6},{7,8},{9,10},{11,12},{13,14},{2,1},{4,3},{6,5},{... | collective-permute-start | bytes 344072 | tf_op jit(solution)/shard_map/ppermute | solution.py:498
  29.9 4.7 %collective-permute-start.2 = (f32[112,256]{1,0:T(8,128)S(1)}, f32[112,256]{1,0:T(8,128)S(1)}, u32[]{:S(2)}, u32[]{:S(2)}) collective-permute-start(f32[112,256]{1,0:T(8,128)S(1)} %get-tuple-element.19), channel_id=1, source_target_pairs={{0,1},{2,3},{4,5},{6,7},{8,9},{10,11},{12,13},{14,15},{1,0},{3,2},... | collective-permute-start | bytes 344072 | tf_op jit(solution)/shard_map/ppermute | solution.py:498
  35.4 13.3 %collective-permute-start.5 = (f32[108,256]{1,0:T(8,128)S(1)}, f32[108,256]{1,0:T(8,128)S(1)}, u32[]{:S(2)}, u32[]{:S(2)}) collective-permute-start(f32[108,256]{1,0:T(8,128)S(1)} %get-tuple-element.25), channel_id=1, source_target_pairs={{16,32},{48,64},{80,96},{112,128},{144,160},{176,192},{208,224},{2... | collective-permute-start | bytes 331784 | tf_op jit(solution)/shard_map/ppermute | solution.py:498
  46.5 5.5 %collective-permute-start.6 = (f32[108,256]{1,0:T(8,128)S(1)}, f32[108,256]{1,0:T(8,128)S(1)}, u32[]{:S(2)}, u32[]{:S(2)}) collective-permute-start(f32[108,256]{1,0:T(8,128)S(1)} %get-tuple-element.26), channel_id=1, source_target_pairs={{0,16},{32,48},{64,80},{96,112},{128,144},{160,176},{192,208},{224... | collective-permute-start | bytes 331784 | tf_op jit(solution)/shard_map/ppermute | solution.py:498

commit v5 on v4

--- a/solution.py
+++ b/solution.py
@@ -155,7 +155,8 @@
     return jnp.transpose(square[...])[:ny]
 
 
-def coef_kernel(eps, mine, theirs, ef, hf, ea, ha, coef, mirror_coef, y_far, y_near, table, lines, square):
+def coef_kernel(bulk_far, bulk_near, eps, mine, theirs, ef, hf, ea, ha, coef, mirror_coef, y_far, y_near, table, lines, square):
+    del bulk_far, bulk_near
     nx = eps.shape[0]
     ny = END - TOP
     weight, density, partner = small_parts(mine)
@@ -235,7 +236,8 @@
 SLIM = 6
 
 
-def bulk_kernel(ef, hf, ea, ha, eps, x_far, x_near):
+def bulk_kernel(ef, hf, ea, ha, eps, message, x_far, x_near):
+    del message
     nx, ny = eps.shape[0], eps.shape[1]
     fields = ((ef, hf), (ea, ha))
     ks = [COURANT / eps[x] if x in (0, nx - 1) else None for x in range(nx)]
@@ -321,7 +323,7 @@
             out[pl.ds(p * nx + x, 1), :] = square[pl.ds(x * 16 + 2 + p, 1), :]
 
 
-def step_kernel(ef_in, hf_in, ea_in, ha_in, coef, tops, ends, mirror, bulk_far, bulk_near,
+def step_kernel(ef_in, hf_in, ea_in, ha_in, coef, tops, ends, mirror, bulk_far_1, bulk_near_1, bulk_far_2, bulk_near_2,
                 x_far, x_near, mine, theirs,
                 ef_out, hf_out, ea_out, ha_out, grad,
                 ee, hh, halo, square, table, lines, sems):
@@ -336,8 +338,9 @@
             return jnp.where(odd, pair[0][pl.ds(row, rows), :], pair[1][pl.ds(row, rows), :])
 
         def bulk_at(row, rows, slot=slot):
-            pair = (bulk_near, bulk_far) if slot == 0 else (bulk_far, bulk_near)
-            return jnp.where(odd, pair[0][pl.ds(row, rows), :], pair[1][pl.ds(row, rows), :])
+            far = bulk_far_1[pl.ds(row, rows), :] + bulk_far_2[pl.ds(row, rows), :]
+            near = bulk_near_1[pl.ds(row, rows), :] + bulk_near_2[pl.ds(row, rows), :]
+            return jnp.where(odd, near, far) if slot == 0 else jnp.where(odd, far, near)
 
         halo[slot + 9, pl.ds(0, TOP), :] = jnp.zeros((TOP, nz), F32)
         halo[slot + 9, pl.ds(END, TOP), :] = jnp.zeros((TOP, nz), F32)
@@ -490,9 +493,11 @@
     )(*args)
 
 
-def swapped(far, near, axis):
+def swapped(far, near, axis, start=0, stop=None):
+    size = lax.axis_size(axis)
+
     def pairs(first):
-        lows = range(first, lax.axis_size(axis) - 1, 2)
+        lows = [i for i in range(first, size - 1, 2) if start <= i < (size if stop is None else stop)]
         return [(i, i + 1) for i in lows] + [(i + 1, i) for i in lows]
 
     return lax.ppermute(far, axis, pairs(1)), lax.ppermute(near, axis, pairs(0))
@@ -520,11 +525,13 @@
          square, pltpu.SemaphoreType.DMA((10,))], name="message", any_in=True)
     theirs = mirrored(mine, "gx")
     bulk_shape = shape(9 * ny, nz)
-    bulk = call(bulk_kernel, [bulk_shape, bulk_shape], fields + [eps_back], name="bulk")
-    bulk_far, bulk_near = swapped(*bulk, "gx")
+    bulk = call(bulk_kernel, [bulk_shape, bulk_shape], fields + [eps_back, mine], name="bulk")
+    half = lax.axis_size("gx") // 2
+    bulk_lower = swapped(*bulk, "gx", stop=half)
+    bulk_upper = swapped(*bulk, "gx", start=half)
     y_shape = shape(2 * (13 * nx) + 8, nz)
     coef, mirror_coef, y_far, y_near = call(
-        coef_kernel, [block, shape(ny, LANES), y_shape, y_shape], [eps_back, mine, theirs] + fields,
+        coef_kernel, [block, shape(ny, LANES), y_shape, y_shape], [*bulk_lower, eps_back, mine, theirs] + fields,
         [lines, lines, square], name="coefficient")
     y_far, y_near = swapped(y_far, y_near, "gy")
     x_shape = shape(9 * 8 + ny + 4, nz)
@@ -536,7 +543,7 @@
     x_far, x_near = swapped(x_far, x_near, "gx")
     ef, hf, ea, ha, grad = call(
         step_kernel, [shape(*e_fwd.shape)] * 4 + [shape(*density.shape)],
-        fields + [coef, tops, ends, mirror, bulk_far, bulk_near, x_far, x_near, mine, theirs],
+        fields + [coef, tops, ends, mirror, *bulk_lower, *bulk_upper, x_far, x_near, mine, theirs],
         [vmem(2, 3, nx + 1, FRAME, nz), vmem(2, 3, nx + 1, FRAME, nz), vmem(20, FRAME, nz),
          square, lines, lines, pltpu.SemaphoreType.DMA((4,))], name="steps", any_out=4)
     return ef, hf, ea, ha, grad

time: 56.2 us -> 56.5 us (level)
  the two profiles are of different devices: /device:TPU:15 before, /device:TPU:239 now
where the time goes in v5:
time: 56.5 us; the launch traced here: 56.2 us
  starting transfers between devices  29.2 us (52%)
  waiting for transfers between devices  17 us (30%)
  Pallas kernels  8.27 us (15%)
  local copies, waits for them, and re-layouts  0.91 us (2%)
  between operations  0.84 us (1%)
    ppermute x4, starting transfers between devices, swapped(): lax.ppermute(far, axis, pairs(1))  20.5 us
    ppermute x1, waiting for transfers between devices, mirrored(): return lax.ppermute(block, axis, [(i, size - 1 - i) for i in range(size)])  11.2 us
    pallas_call x5, Pallas kernels, call(): pl.pallas_call(kernel, out_shape=outs, in_specs=spaces(len(args), len(arg...  8.27 us
    ppermute x4, starting transfers between devices, swapped(): lax.ppermute(near, axis, pairs(0))  6.72 us
    ppermute x4, waiting for transfers between devices, swapped(): lax.ppermute(near, axis, pairs(0))  3.38 us
    ppermute x4, waiting for transfers between devices, swapped(): lax.ppermute(far, axis, pairs(1))  2.37 us
    ppermute x1, starting transfers between devices, mirrored(): return lax.ppermute(block, axis, [(i, size - 1 - i) for i in range(size)])  1.92 us
  transfers between devices with their start and end apart: 9, of which 4 were waited for; matrix products, arithmetic and copies ran while one was open for 0% of the time, Pallas kernels for 2%

profile of v5, /device:TPU:239, one launch (start us, length us, event | category | flops | bytes accessed | tf_op | source)
XLA Modules:
  0.0 56.2 jit_solution(17760576335775925414)
XLA Ops:
  0.6 0.0 copy-start.3
  0.6 0.0 copy-start.2
  0.7 0.0 copy-start.1
  0.7 0.0 copy-start
  0.7 0.0 copy-start.6
  0.7 2.7 %message.1.mine = f32[192,128]{1,0:T(8,128)} custom-call(f32[3,4,32,256]{3,2,1,0:T(8,128)} %ef_in.1, f32[3,4,32,256]{3,2,1,0:T(8,128)} %hf_in.1, f32[3,4,32,256]{3,2,1,0:T(8,128)} %ea_in.1, f32[3,4,32,256]{3,2,1,0:T(8,128)} %ha_in.1, f32[4,32,256]{2,1,0:T(8,128)} %eps.5, f32[4,4,32]{2,1,0:T(4,128)} %density.1, s32[4,4,32]{2,1,0:T(4,128)} %mask.1, ...), custom_call_target="tpu_custom_call" | custom-call | flops 4000000 | bytes 4000000 | tf_op jit(solution)/shard_map/message/pallas_call | solution.py:484
  3.4 0.0 copy-done.3
  3.5 0.0 copy-done.2
  3.5 0.0 copy-done.1
  3.5 0.0 copy-done
  3.5 0.0 copy-done.6
  3.5 0.0 copy-start.4
  3.5 0.9 %copy-done.4 = f32[192,128]{1,0:T(8,128)S(1)} copy-done((f32[192,128]{1,0:T(8,128)S(1)}, f32[192,128]{1,0:T(8,128)}, u32[]{:S(2)}) %copy-start.4) | copy-done | bytes 98328
  4.4 0.4 bulk.1
  4.8 4.6 %collective-permute-start = (f32[288,256]{1,0:T(8,128)S(1)}, f32[288,256]{1,0:T(8,128)S(1)}, u32[]{:S(2)}, u32[]{:S(2)}) collective-permute-start(f32[288,256]{1,0:T(8,128)S(1)} %get-tuple-element.16), channel_id=1, source_target_pairs={{16,32},{48,64},{80,96},{112,128},{144,160},{176,192},{208,224},{2... | collective-permute-start | bytes 884744 | tf_op jit(solution)/shard_map/ppermute | solution.py:503
  9.4 1.9 %collective-permute-start.1 = (f32[288,256]{1,0:T(8,128)S(1)}, f32[288,256]{1,0:T(8,128)S(1)}, u32[]{:S(2)}, u32[]{:S(2)}) collective-permute-start(f32[288,256]{1,0:T(8,128)S(1)} %get-tuple-element.17), channel_id=1, source_target_pairs={{0,16},{32,48},{64,80},{96,112},{128,144},{160,176},{192,208},{224... | collective-permute-start | bytes 884744 | tf_op jit(solution)/shard_map/ppermute | solution.py:503
  11.3 1.9 %collective-permute-start.2 = (f32[192,128]{1,0:T(8,128)S(1)}, f32[192,128]{1,0:T(8,128)S(1)}, u32[]{:S(2)}, u32[]{:S(2)}) collective-permute-start(f32[192,128]{1,0:T(8,128)S(1)} %copy-done.4), channel_id=1, source_target_pairs={{0,496},{16,480},{32,464},{48,448},{64,432},{80,416},{96,400},{112... | collective-permute-start | bytes 294920 | tf_op jit(solution)/shard_map/ppermute | solution.py:508
  13.3 0.7 %collective-permute-start.5 = (f32[288,256]{1,0:T(8,128)S(1)}, f32[288,256]{1,0:T(8,128)S(1)}, u32[]{:S(2)}, u32[]{:S(2)}) collective-permute-start(f32[288,256]{1,0:T(8,128)S(1)} %get-tuple-element.16), channel_id=1, source_target_pairs={{272,288},{304,320},{336,352},{368,384},{400,416},{432,448},{464,4... | collective-permute-start | bytes 884744 | tf_op jit(solution)/shard_map/ppermute | solution.py:503
  13.9 0.7 %collective-permute-start.6 = (f32[288,256]{1,0:T(8,128)S(1)}, f32[288,256]{1,0:T(8,128)S(1)}, u32[]{:S(2)}, u32[]{:S(2)}) collective-permute-start(f32[288,256]{1,0:T(8,128)S(1)} %get-tuple-element.17), channel_id=1, source_target_pairs={{256,272},{288,304},{320,336},{352,368},{384,400},{416,432},{448,4... | collective-permute-start | bytes 884744 | tf_op jit(solution)/shard_map/ppermute | solution.py:503
  14.6 11.2 %collective-permute-done.2.theirs = f32[192,128]{1,0:T(8,128)S(1)} collective-permute-done((f32[192,128]{1,0:T(8,128)S(1)}, f32[192,128]{1,0:T(8,128)S(1)}, u32[]{:S(2)}, u32[]{:S(2)}) %collective-permute-start.2) | collective-permute-done | bytes 98336 | tf_op jit(solution)/shard_map/ppermute | solution.py:508
  25.9 0.0 collective-permute-done.bulk_far.bulk_far_1
  25.9 0.0 collective-permute-done.1.bulk_near.bulk_near_1
  25.9 0.5 coefficient.1
  26.4 4.6 %collective-permute-start.3 = (f32[112,256]{1,0:T(8,128)S(1)}, f32[112,256]{1,0:T(8,128)S(1)}, u32[]{:S(2)}, u32[]{:S(2)}) collective-permute-start(f32[112,256]{1,0:T(8,128)S(1)} %get-tuple-element.20), channel_id=1, source_target_pairs={{1,2},{3,4},{5,6},{7,8},{9,10},{11,12},{13,14},{2,1},{4,3},{6,5},{... | collective-permute-start | bytes 344072 | tf_op jit(solution)/shard_map/ppermute | solution.py:503
  31.0 2.2 %collective-permute-start.4 = (f32[112,256]{1,0:T(8,128)S(1)}, f32[112,256]{1,0:T(8,128)S(1)}, u32[]{:S(2)}, u32[]{:S(2)}) collective-permute-start(f32[112,256]{1,0:T(8,128)S(1)} %get-tuple-element.21), channel_id=1, source_target_pairs={{0,1},{2,3},{4,5},{6,7},{8,9},{10,11},{12,13},{14,15},{1,0},{3,2},... | collective-permute-start | bytes 344072 | tf_op jit(solution)/shard_map/ppermute | solution.py:503
  33.2 2.1 %collective-permute-done.3.y_far = f32[112,256]{1,0:T(8,128)S(1)} collective-permute-done((f32[112,256]{1,0:T(8,128)S(1)}, f32[112,256]{1,0:T(8,128)S(1)}, u32[]{:S(2)}, u32[]{:S(2)}) %collective-permute-start.3) | collective-permute-done | bytes 114720 | tf_op jit(solution)/shard_map/ppermute | solution.py:503
  35.3 0.0 collective-permute-done.4.y_near
  35.3 0.0 copy-start.5
  35.3 0.8 %edges.1 = (f32[52,8,256]{2,1,0:T(8,128)S(1)}, f32[52,8,256]{2,1,0:T(8,128)S(1)}, f32[4,48,128]{2,1,0:T(8,128)S(1)}, f32[108,256]{1,0:T(8,128)S(1)}, f32[108,256]{1,0:T(8,128)S(1)}) custom-call(f32[3,4,32,256]{3,2,1,0:T(8,128)S(1)} %copy-done, f32[3,4,32,256]{3,2,1,0:T(8,128)S(1)} %copy-done.1, f32[3,4,32,256]{3,2,1,0:T(8,128)S(1)} %copy-done.2, ...), custom_call_target="tpu_custom_call" | custom-call | flops 4000000 | bytes 4000000 | tf_op jit(solution)/shard_map/edges/pallas_call | solution.py:484
  36.1 10.6 %collective-permute-start.7 = (f32[108,256]{1,0:T(8,128)S(1)}, f32[108,256]{1,0:T(8,128)S(1)}, u32[]{:S(2)}, u32[]{:S(2)}) collective-permute-start(f32[108,256]{1,0:T(8,128)S(1)} %get-tuple-element.25), channel_id=1, source_target_pairs={{16,32},{48,64},{80,96},{112,128},{144,160},{176,192},{208,224},{2... | collective-permute-start | bytes 331784 | tf_op jit(solution)/shard_map/ppermute | solution.py:503
  46.7 1.9 %collective-permute-start.8 = (f32[108,256]{1,0:T(8,128)S(1)}, f32[108,256]{1,0:T(8,128)S(1)}, u32[]{:S(2)}, u32[]{:S(2)}) collective-permute-start(f32[108,256]{1,0:T(8,128)S(1)} %get-tuple-element.26), channel_id=1, source_target_pairs={{0,16},{32,48},{64,80},{96,112},{128,144},{160,176},{192,208},{224... | collective-permute-start | bytes 331784 | tf_op jit(solution)/shard_map/ppermute | solution.py:503
  48.7 0.0 collective-permute-done.5.bulk_far_2
  48.7 0.0 collective-permute-done.6.bulk_near_2
  48.7 0.2 collective-permute-done.7.x_far
  48.9 3.4 %collective-permute-done.8.x_near = f32[108,256]{1,0:T(8,128)S(1)} collective-permute-done((f32[108,256]{1,0:T(8,128)S(1)}, f32[108,256]{1,0:T(8,128)S(1)}, u32[]{:S(2)}, u32[]{:S(2)}) %collective-permute-start.8) | collective-permute-done | bytes 110624 | tf_op jit(solution)/shard_map/ppermute | solution.py:503
  52.3 0.0 copy-done.5
  52.3 3.9 %steps.1 = (f32[3,4,32,256]{3,2,1,0:T(8,128)}, f32[3,4,32,256]{3,2,1,0:T(8,128)}, f32[3,4,32,256]{3,2,1,0:T(8,128)}, f32[3,4,32,256]{3,2,1,0:T(8,128)}, f32[4,4,32]{2,1,0:T(4,128)}) custom-call(f32[3,4,32,256]{3,2,1,0:T(8,128)S(1)} %copy-done, f32[3,4,32,256]{3,2,1,0:T(8,128)S(1)} %copy-done.1, f32[3,4,32,256]{3,2,1,0:T(8,128)S(1)} %copy-done.2, ...), custom_call_target="tpu_custom_call" | custom-call | flops 4000000 | bytes 4000000 | tf_op jit(solution)/shard_map/steps/pallas_call | solution.py:484
Async XLA Ops:
  0.6 2.8 %copy-start.3 = (f32[3,4,32,256]{3,2,1,0:T(8,128)S(1)}, f32[3,4,32,256]{3,2,1,0:T(8,128)}, u32[]{:S(2)}) copy-start(f32[3,4,32,256]{3,2,1,0:T(8,128)} %ha_in.1) | copy-start | bytes 1179652
  0.6 2.8 %copy-start.2 = (f32[3,4,32,256]{3,2,1,0:T(8,128)S(1)}, f32[3,4,32,256]{3,2,1,0:T(8,128)}, u32[]{:S(2)}) copy-start(f32[3,4,32,256]{3,2,1,0:T(8,128)} %ea_in.1) | copy-start | bytes 1179652
  0.7 2.8 %copy-start.1 = (f32[3,4,32,256]{3,2,1,0:T(8,128)S(1)}, f32[3,4,32,256]{3,2,1,0:T(8,128)}, u32[]{:S(2)}) copy-start(f32[3,4,32,256]{3,2,1,0:T(8,128)} %hf_in.1) | copy-start | bytes 1179652
  0.7 2.8 %copy-start = (f32[3,4,32,256]{3,2,1,0:T(8,128)S(1)}, f32[3,4,32,256]{3,2,1,0:T(8,128)}, u32[]{:S(2)}) copy-start(f32[3,4,32,256]{3,2,1,0:T(8,128)} %ef_in.1) | copy-start | bytes 1179652
  0.7 2.8 %copy-start.6 = (f32[4,32,256]{2,1,0:T(8,128)S(1)}, f32[4,32,256]{2,1,0:T(8,128)}, u32[]{:S(2)}) copy-start(f32[4,32,256]{2,1,0:T(8,128)} %eps.5) | copy-start | bytes 393220
  3.5 0.9 %copy-start.4 = (f32[192,128]{1,0:T(8,128)S(1)}, f32[192,128]{1,0:T(8,128)}, u32[]{:S(2)}) copy-start(f32[192,128]{1,0:T(8,128)} %message.1.mine) | copy-start | bytes 294916
  4.8 21.1 %collective-permute-start = (f32[288,256]{1,0:T(8,128)S(1)}, f32[288,256]{1,0:T(8,128)S(1)}, u32[]{:S(2)}, u32[]{:S(2)}) collective-permute-start(f32[288,256]{1,0:T(8,128)S(1)} %get-tuple-element.16), channel_id=1, source_target_pairs={{16,32},{48,64},{80,96},{112,128},{144,160},{176,192},{208,224},{2... | collective-permute-start | bytes 884744 | tf_op jit(solution)/shard_map/ppermute | solution.py:503
  9.4 16.5 %collective-permute-start.1 = (f32[288,256]{1,0:T(8,128)S(1)}, f32[288,256]{1,0:T(8,128)S(1)}, u32[]{:S(2)}, u32[]{:S(2)}) collective-permute-start(f32[288,256]{1,0:T(8,128)S(1)} %get-tuple-element.17), channel_id=1, source_target_pairs={{0,16},{32,48},{64,80},{96,112},{128,144},{160,176},{192,208},{224... | collective-permute-start | bytes 884744 | tf_op jit(solution)/shard_map/ppermute | solution.py:503
  11.3 14.5 %collective-permute-start.2 = (f32[192,128]{1,0:T(8,128)S(1)}, f32[192,128]{1,0:T(8,128)S(1)}, u32[]{:S(2)}, u32[]{:S(2)}) collective-permute-start(f32[192,128]{1,0:T(8,128)S(1)} %copy-done.4), channel_id=1, source_target_pairs={{0,496},{16,480},{32,464},{48,448},{64,432},{80,416},{96,400},{112... | collective-permute-start | bytes 294920 | tf_op jit(solution)/shard_map/ppermute | solution.py:508
  13.3 35.4 %collective-permute-start.5 = (f32[288,256]{1,0:T(8,128)S(1)}, f32[288,256]{1,0:T(8,128)S(1)}, u32[]{:S(2)}, u32[]{:S(2)}) collective-permute-start(f32[288,256]{1,0:T(8,128)S(1)} %get-tuple-element.16), channel_id=1, source_target_pairs={{272,288},{304,320},{336,352},{368,384},{400,416},{432,448},{464,4... | collective-permute-start | bytes 884744 | tf_op jit(solution)/shard_map/ppermute | solution.py:503
  13.9 34.7 %collective-permute-start.6 = (f32[288,256]{1,0:T(8,128)S(1)}, f32[288,256]{1,0:T(8,128)S(1)}, u32[]{:S(2)}, u32[]{:S(2)}) collective-permute-start(f32[288,256]{1,0:T(8,128)S(1)} %get-tuple-element.17), channel_id=1, source_target_pairs={{256,272},{288,304},{320,336},{352,368},{384,400},{416,432},{448,4... | collective-permute-start | bytes 884744 | tf_op jit(solution)/shard_map/ppermute | solution.py:503
  26.4 8.9 %collective-permute-start.3 = (f32[112,256]{1,0:T(8,128)S(1)}, f32[112,256]{1,0:T(8,128)S(1)}, u32[]{:S(2)}, u32[]{:S(2)}) collective-permute-start(f32[112,256]{1,0:T(8,128)S(1)} %get-tuple-element.20), channel_id=1, source_target_pairs={{1,2},{3,4},{5,6},{7,8},{9,10},{11,12},{13,14},{2,1},{4,3},{6,5},{... | collective-permute-start | bytes 344072 | tf_op jit(solution)/shard_map/ppermute | solution.py:503
  31.0 4.4 %collective-permute-start.4 = (f32[112,256]{1,0:T(8,128)S(1)}, f32[112,256]{1,0:T(8,128)S(1)}, u32[]{:S(2)}, u32[]{:S(2)}) collective-permute-start(f32[112,256]{1,0:T(8,128)S(1)} %get-tuple-element.21), channel_id=1, source_target_pairs={{0,1},{2,3},{4,5},{6,7},{8,9},{10,11},{12,13},{14,15},{1,0},{3,2},... | collective-permute-start | bytes 344072 | tf_op jit(solution)/shard_map/ppermute | solution.py:503
  35.3 17.0 %copy-start.5 = (f32[192,128]{1,0:T(8,128)S(1)}, f32[192,128]{1,0:T(8,128)}, u32[]{:S(2)}) copy-start(f32[192,128]{1,0:T(8,128)} %message.1.mine) | copy-start | bytes 294916
  36.1 12.8 %collective-permute-start.7 = (f32[108,256]{1,0:T(8,128)S(1)}, f32[108,256]{1,0:T(8,128)S(1)}, u32[]{:S(2)}, u32[]{:S(2)}) collective-permute-start(f32[108,256]{1,0:T(8,128)S(1)} %get-tuple-element.25), channel_id=1, source_target_pairs={{16,32},{48,64},{80,96},{112,128},{144,160},{176,192},{208,224},{2... | collective-permute-start | bytes 331784 | tf_op jit(solution)/shard_map/ppermute | solution.py:503
  46.7 5.5 %collective-permute-start.8 = (f32[108,256]{1,0:T(8,128)S(1)}, f32[108,256]{1,0:T(8,128)S(1)}, u32[]{:S(2)}, u32[]{:S(2)}) collective-permute-start(f32[108,256]{1,0:T(8,128)S(1)} %get-tuple-element.26), channel_id=1, source_target_pairs={{0,16},{32,48},{64,80},{96,112},{128,144},{160,176},{192,208},{224... | collective-permute-start | bytes 331784 | tf_op jit(solution)/shard_map/ppermute | solution.py:503

commit v6 on v5

--- a/solution.py
+++ b/solution.py
@@ -80,8 +80,46 @@
     return jnp.transpose(square[...])
 
 
-def message_kernel(ef, hf, ea, ha, eps, density, mask, partner, mon_f, mon_a, message,
-                   fields, eps_in, small_f, small_i, mons, square, sems):
+def edge_planes(part, ks, nx, mark):
+    up, down = [], []
+    last = nx - 1
+    for f in range(2):
+        e = lambda c, x: part(f, 0, c, x)
+        h = lambda c, x: part(f, 1, c, x)
+        k = ks[last]
+        ex, ey, ez = e(0, last), e(1, last), e(2, last)
+        ex_b, ey_b, ez_b = e(0, last - 1), e(1, last - 1), e(2, last - 1)
+        hy_b = mark(h(1, last - 1) - COURANT * ((up_z(ex_b) - ex_b) - (ez - ez_b)), last - 1)
+        hz_b = mark(h(2, last - 1) - COURANT * ((ey - ey_b) - (up_y(ex_b) - ex_b)), last - 1)
+        hx = mark(h(0, last) - COURANT * ((up_y(ez) - ez) - (up_z(ey) - ey)), last)
+        hy = mark(h(1, last) - COURANT * ((up_z(ex) - ex) + ez), last)
+        hz = mark(h(2, last) - COURANT * (-ey - (up_y(ex) - ex)), last)
+        ex = ex + k * ((hz - down_y(hz)) - (hy - down_z(hy)))
+        ey = ey + k * ((hx - down_z(hx)) - (hz - hz_b))
+        ez = ez + k * ((hy - hy_b) - (hx - down_y(hx)))
+        up += [hy, hz, mark(hy - COURANT * ((up_z(ex) - ex) + ez), last),
+               mark(hz - COURANT * (-ey - (up_y(ex) - ex)), last)]
+        k = ks[0]
+        ex, ey, ez = e(0, 0), e(1, 0), e(2, 0)
+        hx = mark(h(0, 0) - COURANT * ((up_y(ez) - ez) - (up_z(ey) - ey)), 0)
+        hy = mark(h(1, 0) - COURANT * ((up_z(ex) - ex) - (e(2, 1) - ez)), 0)
+        hz = mark(h(2, 0) - COURANT * ((e(1, 1) - ey) - (up_y(ex) - ex)), 0)
+        down += [ey, ez, ey + k * ((hx - down_z(hx)) - hz), ez + k * (hy - (hx - down_y(hx)))]
+    return up + [ks[last]], down + [ks[0]]
+
+
+def write_bulk(part, eps, x_far, x_near):
+    nx, ny = eps.shape[0], eps.shape[1]
+    ks = [COURANT / eps[x] if x in (0, nx - 1) else None for x in range(nx)]
+    odd = is_odd("gx")
+    for i, planes in enumerate(zip(*edge_planes(part, ks, nx, lambda v, x: v))):
+        far, near = ordered(odd, *planes)
+        x_far[pl.ds(i * ny, ny), :] = far
+        x_near[pl.ds(i * ny, ny), :] = near
+
+
+def message_kernel(ef, hf, ea, ha, eps, density, mask, partner, mon_f, mon_a,
+                   message, fields, eps_in, small_f, small_i, mons, square, sems):
     nx, ny = ef.shape[1], ef.shape[2]
     copies = []
     for f, (e, h) in enumerate(((ef, hf), (ea, ha))):
@@ -126,6 +164,12 @@
              for k in range(2) for x in range(nx) for f in range(2)])
 
 
+def bulk_kernel(ef, hf, ea, ha, eps, message, x_far, x_near):
+    del message
+    fields = ((ef, hf), (ea, ha))
+    write_bulk(lambda f, k, c, x: fields[f][k][c, x], eps, x_far, x_near)
+
+
 def small_parts(message):
     weight = turn(message[pl.ds(ROW_EPS, 16), :], -64)
     density = turn(message[pl.ds(ROW_EPS + 16, 16), :], -64)
@@ -204,49 +248,11 @@
     return jnp.concatenate([tops[i], middle, ends[i]], 0)
 
 
-def edge_planes(part, ks, nx, mark):
-    up, down = [], []
-    last = nx - 1
-    for f in range(2):
-        e = lambda c, x: part(f, 0, c, x)
-        h = lambda c, x: part(f, 1, c, x)
-        k = ks[last]
-        ex, ey, ez = e(0, last), e(1, last), e(2, last)
-        ex_b, ey_b, ez_b = e(0, last - 1), e(1, last - 1), e(2, last - 1)
-        hy_b = mark(h(1, last - 1) - COURANT * ((up_z(ex_b) - ex_b) - (ez - ez_b)), last - 1)
-        hz_b = mark(h(2, last - 1) - COURANT * ((ey - ey_b) - (up_y(ex_b) - ex_b)), last - 1)
-        hx = mark(h(0, last) - COURANT * ((up_y(ez) - ez) - (up_z(ey) - ey)), last)
-        hy = mark(h(1, last) - COURANT * ((up_z(ex) - ex) + ez), last)
-        hz = mark(h(2, last) - COURANT * (-ey - (up_y(ex) - ex)), last)
-        ex = ex + k * ((hz - down_y(hz)) - (hy - down_z(hy)))
-        ey = ey + k * ((hx - down_z(hx)) - (hz - hz_b))
-        ez = ez + k * ((hy - hy_b) - (hx - down_y(hx)))
-        up += [hy, hz, mark(hy - COURANT * ((up_z(ex) - ex) + ez), last),
-               mark(hz - COURANT * (-ey - (up_y(ex) - ex)), last)]
-        k = ks[0]
-        ex, ey, ez = e(0, 0), e(1, 0), e(2, 0)
-        hx = mark(h(0, 0) - COURANT * ((up_y(ez) - ez) - (up_z(ey) - ey)), 0)
-        hy = mark(h(1, 0) - COURANT * ((up_z(ex) - ex) - (e(2, 1) - ez)), 0)
-        hz = mark(h(2, 0) - COURANT * ((e(1, 1) - ey) - (up_y(ex) - ex)), 0)
-        down += [ey, ez, ey + k * ((hx - down_z(hx)) - hz), ez + k * (hy - (hx - down_y(hx)))]
-    return up + [ks[last]], down + [ks[0]]
-
-
+ROWS_UP = ((7, 40), (7, 39), (8, 39), (8, 38, 39)) * 2 + ((7, 40),)
+ROWS_DOWN = ((6, 7, 40), (7, 40), (7, 39), (8, 39)) * 2 + ((7, 40),)
+FIXED = 20
 LATER = (2, 3, 6, 7, 8)
 SLIM = 6
-
-
-def bulk_kernel(ef, hf, ea, ha, eps, message, x_far, x_near):
-    del message
-    nx, ny = eps.shape[0], eps.shape[1]
-    fields = ((ef, hf), (ea, ha))
-    ks = [COURANT / eps[x] if x in (0, nx - 1) else None for x in range(nx)]
-    up, down = edge_planes(lambda f, k, c, x: fields[f][k][c, x], ks, nx, lambda v, x: v)
-    odd = is_odd("gx")
-    for i, planes in enumerate(zip(up, down)):
-        far, near = ordered(odd, *planes)
-        x_far[pl.ds(i * ny, ny), :] = far
-        x_near[pl.ds(i * ny, ny), :] = near
 
 
 def edges_kernel(ef, hf, ea, ha, coef, mirror_coef, theirs, y_far, y_near,
@@ -285,10 +291,13 @@
     first = lane % 64 < 32
     up_m = [jnp.where(first, m[0], turn(m[1], 32)), jnp.where(first, m[2], turn(km, 32))]
     down_m = [jnp.where(first, turn(m[1], -32), m[0]), jnp.where(first, turn(km, -32), m[2])]
-    for out, planes, window, base in ((x_up, up, up_m, 96), (x_down, down, down_m, 64)):
-        for i, plane in enumerate(planes):
-            out[pl.ds(8 * i, 4), :] = plane[TOP - 2:TOP + 2]
-            out[pl.ds(8 * i + 4, 4), :] = plane[END - 2:END + 2]
+    for out, planes, wanted, window, base in ((x_up, up, ROWS_UP, up_m, 96),
+                                              (x_down, down, ROWS_DOWN, down_m, 64)):
+        at = 0
+        for plane, rows in zip(planes, wanted):
+            for row in rows:
+                out[pl.ds(at, 1), :] = plane[row:row + 1]
+                at += 1
         side = window[1]
         for i, plane in enumerate(LATER):
             plane = planes[plane]
@@ -297,9 +306,9 @@
             inside = (lane >= base + SLIM * i) & (lane < base + SLIM * (i + 1))
             side = jnp.where(inside, part_in, side)
         value = jnp.concatenate([window[0], side], 1)
-        out[pl.ds(72, ny), :] = value[TOP:END]
-        out[pl.ds(72 + ny, 2), :] = value[TOP - 2:TOP]
-        out[pl.ds(74 + ny, 2), :] = value[END:END + 2]
+        out[pl.ds(FIXED, 2), :] = value[TOP - 2:TOP]
+        out[pl.ds(FIXED + 2, 2), :] = value[END:END + 2]
+        out[pl.ds(FIXED + 4, ny), :] = value[TOP:END]
     x_far[...], x_near[...] = ordered(is_odd("gx"), x_up[...], x_down[...])
 
 
@@ -344,12 +353,13 @@
 
         halo[slot + 9, pl.ds(0, TOP), :] = jnp.zeros((TOP, nz), F32)
         halo[slot + 9, pl.ds(END, TOP), :] = jnp.zeros((TOP, nz), F32)
-        window = source_at(72, ny)
+        window = source_at(FIXED + 4, ny)
         halo[slot + 9, pl.ds(TOP, ny), :] = window
-        halo[slot + 9, pl.ds(TOP - 2, 2), :] = source_at(72 + ny, 2)
-        halo[slot + 9, pl.ds(END, 2), :] = source_at(74 + ny, 2)
+        halo[slot + 9, pl.ds(TOP - 2, 2), :] = source_at(FIXED, 2)
+        halo[slot + 9, pl.ds(END, 2), :] = source_at(FIXED + 2, 2)
         side = window[:, LANES:]
-        for plane in range(9):
+        row_at = 0
+        for plane, rows in enumerate(ROWS_DOWN if slot else ROWS_UP):
             at = slot + plane
             halo[at, pl.ds(0, TOP), :] = jnp.zeros((TOP, nz), F32)
             halo[at, pl.ds(END, TOP), :] = jnp.zeros((TOP, nz), F32)
@@ -360,8 +370,9 @@
                     [jnp.where(lane >= Z0 - 1, near, value[:, :LANES]),
                      jnp.where(lane < Z0 + PLANES + 1 - LANES, near, value[:, LANES:])], 1)
             halo[at, pl.ds(TOP, ny), :] = value
-            halo[at, pl.ds(TOP - 2, 4), :] = source_at(8 * plane, 4)
-            halo[at, pl.ds(END - 2, 4), :] = source_at(8 * plane + 4, 4)
+            for row in rows:
+                halo[at, pl.ds(row, 1), :] = source_at(row_at, 1)
+                row_at += 1
     k_low, k_high = halo[8], halo[18]
 
     def part(f, k, c, x):
@@ -478,17 +489,17 @@
         copy.wait()
 
 
-def call(kernel, outs, args, scratch=(), name=None, any_in=False, any_out=0):
+def call(kernel, outs, args, scratch=(), name=None, any_in=False, any_out=0, work=4_000_000):
     spaces = lambda count, far: [pl.BlockSpec(memory_space=pltpu.HBM if i < far else pltpu.VMEM)
                                  for i in range(count)]
     return pl.pallas_call(
         kernel,
         out_shape=outs,
-        in_specs=spaces(len(args), len(args) if any_in else 0),
+        in_specs=[pl.BlockSpec(memory_space=pltpu.HBM if any_in else pltpu.VMEM)] * len(args),
         out_specs=spaces(len(outs), any_out),
         scratch_shapes=list(scratch),
         compiler_params=pltpu.CompilerParams(vmem_limit_bytes=FAR_LIMIT if any_in else VMEM_LIMIT),
-        cost_estimate=pl.CostEstimate(flops=4_000_000, bytes_accessed=4_000_000, transcendentals=0),
+        cost_estimate=pl.CostEstimate(flops=work, bytes_accessed=4_000_000, transcendentals=0),
         name=name,
     )(*args)
 
@@ -517,6 +528,7 @@
     block = shape(nx, ny, nz)
     fields = [e_fwd, h_fwd, e_adj, h_adj]
 
+    bulk_shape = shape(9 * ny, nz)
     mine, = call(
         message_kernel, [shape(MESSAGE, LANES)],
         fields + [eps_back, density, design_mask, partner_map, mon_fwd, mon_adj],
@@ -524,22 +536,21 @@
          pltpu.VMEM((2,) + density.shape, jnp.int32), vmem(2, *mon_fwd.shape),
          square, pltpu.SemaphoreType.DMA((10,))], name="message", any_in=True)
     theirs = mirrored(mine, "gx")
-    bulk_shape = shape(9 * ny, nz)
-    bulk = call(bulk_kernel, [bulk_shape, bulk_shape], fields + [eps_back, mine], name="bulk")
-    half = lax.axis_size("gx") // 2
-    bulk_lower = swapped(*bulk, "gx", stop=half)
-    bulk_upper = swapped(*bulk, "gx", start=half)
+    bulk = call(bulk_kernel, [bulk_shape, bulk_shape], [*fields, eps_back, mine], name="bulk")
+    early = lax.axis_size("gx") // 4
+    bulk_lower = swapped(*bulk, "gx", stop=early)
+    bulk_upper = swapped(*bulk, "gx", start=early)
     y_shape = shape(2 * (13 * nx) + 8, nz)
     coef, mirror_coef, y_far, y_near = call(
         coef_kernel, [block, shape(ny, LANES), y_shape, y_shape], [*bulk_lower, eps_back, mine, theirs] + fields,
         [lines, lines, square], name="coefficient")
     y_far, y_near = swapped(y_far, y_near, "gy")
-    x_shape = shape(9 * 8 + ny + 4, nz)
+    x_shape = shape(FIXED + 4 + ny, nz)
     tile = shape(13 * nx, 8, nz)
     tops, ends, mirror, x_far, x_near = call(
         edges_kernel, [tile, tile, shape(4, FRAME, LANES), x_shape, x_shape],
         fields + [coef, mirror_coef, theirs, y_far, y_near],
-        [vmem(*x_shape.shape)] * 2, name="edges")
+        [vmem(*x_shape.shape)] * 2, name="edges", work=1_000_000_000)
     x_far, x_near = swapped(x_far, x_near, "gx")
     ef, hf, ea, ha, grad = call(
         step_kernel, [shape(*e_fwd.shape)] * 4 + [shape(*density.shape)],

time: 56.5 us -> 54.4 us (0.963)
  the two profiles are of different devices: /device:TPU:239 before, /device:TPU:111 now
where the time goes in v6:
time: 54.4 us; the launch traced here: 54.1 us
  starting transfers between devices  30.9 us (57%)
  waiting for transfers between devices  13.2 us (24%)
  Pallas kernels  8.24 us (15%)
  local copies, waits for them, and re-layouts  0.91 us (2%)
  between operations  0.84 us (2%)
    ppermute x4, starting transfers between devices, swapped(): lax.ppermute(far, axis, pairs(1))  18.7 us
    pallas_call x5, Pallas kernels, call(): pl.pallas_call(kernel, out_shape=outs, in_specs=[pl.BlockSpec(memory_spac...  8.24 us
    ppermute x4, starting transfers between devices, swapped(): lax.ppermute(near, axis, pairs(0))  6.44 us
    ppermute x1, waiting for transfers between devices, mirrored(): return lax.ppermute(block, axis, [(i, size - 1 - i) for i in range(size)])  5.82 us
    ppermute x1, starting transfers between devices, mirrored(): return lax.ppermute(block, axis, [(i, size - 1 - i) for i in range(size)])  5.77 us
    ppermute x4, waiting for transfers between devices, swapped(): lax.ppermute(near, axis, pairs(0))  4.77 us
    ppermute x4, waiting for transfers between devices, swapped(): lax.ppermute(far, axis, pairs(1))  2.6 us
  transfers between devices with their start and end apart: 9, of which 4 were waited for; matrix products, arithmetic and copies ran while one was open for 0% of the time, Pallas kernels for 2%

profile of v6, /device:TPU:111, one launch (start us, length us, event | category | flops | bytes accessed | tf_op | source)
XLA Modules:
  0.0 54.1 jit_solution(316806802109369905)
XLA Ops:
  0.6 0.0 copy-start.3
  0.6 0.0 copy-start.2
  0.7 0.0 copy-start.1
  0.7 0.0 copy-start
  0.7 0.0 copy-start.6
  0.7 2.7 %message.1.mine = f32[192,128]{1,0:T(8,128)} custom-call(f32[3,4,32,256]{3,2,1,0:T(8,128)} %ef_in.1, f32[3,4,32,256]{3,2,1,0:T(8,128)} %hf_in.1, f32[3,4,32,256]{3,2,1,0:T(8,128)} %ea_in.1, f32[3,4,32,256]{3,2,1,0:T(8,128)} %ha_in.1, f32[4,32,256]{2,1,0:T(8,128)} %eps.5, f32[4,4,32]{2,1,0:T(4,128)} %density.1, s32[4,4,32]{2,1,0:T(4,128)} %mask.1, ...), custom_call_target="tpu_custom_call" | custom-call | flops 4000000 | bytes 4000000 | tf_op jit(solution)/shard_map/message/pallas_call | solution.py:495
  3.4 0.0 copy-done.3
  3.5 0.0 copy-done.2
  3.5 0.0 copy-done.1
  3.5 0.0 copy-done
  3.5 0.0 copy-done.6
  3.5 0.0 copy-start.4
  3.5 0.9 %copy-done.4 = f32[192,128]{1,0:T(8,128)S(1)} copy-done((f32[192,128]{1,0:T(8,128)S(1)}, f32[192,128]{1,0:T(8,128)}, u32[]{:S(2)}) %copy-start.4) | copy-done | bytes 98328
  4.4 0.4 bulk.1
  4.8 4.6 %collective-permute-start = (f32[288,256]{1,0:T(8,128)S(1)}, f32[288,256]{1,0:T(8,128)S(1)}, u32[]{:S(2)}, u32[]{:S(2)}) collective-permute-start(f32[288,256]{1,0:T(8,128)S(1)} %get-tuple-element.16), channel_id=1, source_target_pairs={{16,32},{48,64},{80,96},{112,128},{32,16},{64,48},{96,80},{128,112... | collective-permute-start | bytes 884744 | tf_op jit(solution)/shard_map/ppermute | solution.py:514
  9.4 1.9 %collective-permute-start.1 = (f32[288,256]{1,0:T(8,128)S(1)}, f32[288,256]{1,0:T(8,128)S(1)}, u32[]{:S(2)}, u32[]{:S(2)}) collective-permute-start(f32[288,256]{1,0:T(8,128)S(1)} %get-tuple-element.17), channel_id=1, source_target_pairs={{0,16},{32,48},{64,80},{96,112},{16,0},{48,32},{80,64},{112,96},{1... | collective-permute-start | bytes 884744 | tf_op jit(solution)/shard_map/ppermute | solution.py:514
  11.3 5.8 %collective-permute-start.2 = (f32[192,128]{1,0:T(8,128)S(1)}, f32[192,128]{1,0:T(8,128)S(1)}, u32[]{:S(2)}, u32[]{:S(2)}) collective-permute-start(f32[192,128]{1,0:T(8,128)S(1)} %copy-done.4), channel_id=1, source_target_pairs={{0,496},{16,480},{32,464},{48,448},{64,432},{80,416},{96,400},{112... | collective-permute-start | bytes 294920 | tf_op jit(solution)/shard_map/ppermute | solution.py:519
  17.1 0.7 %collective-permute-start.5 = (f32[288,256]{1,0:T(8,128)S(1)}, f32[288,256]{1,0:T(8,128)S(1)}, u32[]{:S(2)}, u32[]{:S(2)}) collective-permute-start(f32[288,256]{1,0:T(8,128)S(1)} %get-tuple-element.16), channel_id=1, source_target_pairs={{144,160},{176,192},{208,224},{240,256},{272,288},{304,320},{336,3... | collective-permute-start | bytes 884744 | tf_op jit(solution)/shard_map/ppermute | solution.py:514
  17.8 0.7 %collective-permute-start.6 = (f32[288,256]{1,0:T(8,128)S(1)}, f32[288,256]{1,0:T(8,128)S(1)}, u32[]{:S(2)}, u32[]{:S(2)}) collective-permute-start(f32[288,256]{1,0:T(8,128)S(1)} %get-tuple-element.17), channel_id=1, source_target_pairs={{128,144},{160,176},{192,208},{224,240},{256,272},{288,304},{320,3... | collective-permute-start | bytes 884744 | tf_op jit(solution)/shard_map/ppermute | solution.py:514
  18.5 5.8 %collective-permute-done.2.theirs = f32[192,128]{1,0:T(8,128)S(1)} collective-permute-done((f32[192,128]{1,0:T(8,128)S(1)}, f32[192,128]{1,0:T(8,128)S(1)}, u32[]{:S(2)}, u32[]{:S(2)}) %collective-permute-start.2) | collective-permute-done | bytes 98336 | tf_op jit(solution)/shard_map/ppermute | solution.py:519
  24.3 0.0 collective-permute-done.bulk_far.bulk_far_1
  24.3 1.8 %collective-permute-done.1.bulk_near.bulk_near_1 = f32[288,256]{1,0:T(8,128)S(1)} collective-permute-done((f32[288,256]{1,0:T(8,128)S(1)}, f32[288,256]{1,0:T(8,128)S(1)}, u32[]{:S(2)}, u32[]{:S(2)}) %collective-permute-start.1) | collective-permute-done | bytes 294944 | tf_op jit(solution)/shard_map/ppermute | solution.py:514
  26.1 0.5 coefficient.1
  26.6 4.3 %collective-permute-start.3 = (f32[112,256]{1,0:T(8,128)S(1)}, f32[112,256]{1,0:T(8,128)S(1)}, u32[]{:S(2)}, u32[]{:S(2)}) collective-permute-start(f32[112,256]{1,0:T(8,128)S(1)} %get-tuple-element.20), channel_id=1, source_target_pairs={{1,2},{3,4},{5,6},{7,8},{9,10},{11,12},{13,14},{2,1},{4,3},{6,5},{... | collective-permute-start | bytes 344072 | tf_op jit(solution)/shard_map/ppermute | solution.py:514
  30.9 1.9 %collective-permute-start.4 = (f32[112,256]{1,0:T(8,128)S(1)}, f32[112,256]{1,0:T(8,128)S(1)}, u32[]{:S(2)}, u32[]{:S(2)}) collective-permute-start(f32[112,256]{1,0:T(8,128)S(1)} %get-tuple-element.21), channel_id=1, source_target_pairs={{0,1},{2,3},{4,5},{6,7},{8,9},{10,11},{12,13},{14,15},{1,0},{3,2},... | collective-permute-start | bytes 344072 | tf_op jit(solution)/shard_map/ppermute | solution.py:514
  32.8 2.6 %collective-permute-done.3.y_far = f32[112,256]{1,0:T(8,128)S(1)} collective-permute-done((f32[112,256]{1,0:T(8,128)S(1)}, f32[112,256]{1,0:T(8,128)S(1)}, u32[]{:S(2)}, u32[]{:S(2)}) %collective-permute-start.3) | collective-permute-done | bytes 114720 | tf_op jit(solution)/shard_map/ppermute | solution.py:514
  35.4 0.0 collective-permute-done.4.y_near
  35.4 0.0 copy-start.5
  35.4 0.8 %edges.1 = (f32[52,8,256]{2,1,0:T(8,128)S(1)}, f32[52,8,256]{2,1,0:T(8,128)S(1)}, f32[4,48,128]{2,1,0:T(8,128)S(1)}, f32[56,256]{1,0:T(8,128)S(1)}, f32[56,256]{1,0:T(8,128)S(1)}) custom-call(f32[3,4,32,256]{3,2,1,0:T(8,128)S(1)} %copy-done, f32[3,4,32,256]{3,2,1,0:T(8,128)S(1)} %copy-done.1, f32[3,4,32,256]{3,2,1,0:T(8,128)S(1)} %copy-done.2, ...), custom_call_target="tpu_custom_call" | custom-call | flops 1000000000 | bytes 4000000 | tf_op jit(solution)/shard_map/edges/pallas_call | solution.py:495
  36.2 9.1 %collective-permute-start.7 = (f32[56,256]{1,0:T(8,128)S(1)}, f32[56,256]{1,0:T(8,128)S(1)}, u32[]{:S(2)}, u32[]{:S(2)}) collective-permute-start(f32[56,256]{1,0:T(8,128)S(1)} %get-tuple-element.25), channel_id=1, source_target_pairs={{16,32},{48,64},{80,96},{112,128},{144,160},{176,192},{208,224},{2... | collective-permute-start | bytes 172040 | tf_op jit(solution)/shard_map/ppermute | solution.py:514
  45.3 1.9 %collective-permute-start.8 = (f32[56,256]{1,0:T(8,128)S(1)}, f32[56,256]{1,0:T(8,128)S(1)}, u32[]{:S(2)}, u32[]{:S(2)}) collective-permute-start(f32[56,256]{1,0:T(8,128)S(1)} %get-tuple-element.26), channel_id=1, source_target_pairs={{0,16},{32,48},{64,80},{96,112},{128,144},{160,176},{192,208},{224... | collective-permute-start | bytes 172040 | tf_op jit(solution)/shard_map/ppermute | solution.py:514
  47.2 0.0 collective-permute-done.5.bulk_far_2
  47.2 0.0 collective-permute-done.6.bulk_near_2
  47.2 0.0 collective-permute-done.7.x_far
  47.2 3.0 %collective-permute-done.8.x_near = f32[56,256]{1,0:T(8,128)S(1)} collective-permute-done((f32[56,256]{1,0:T(8,128)S(1)}, f32[56,256]{1,0:T(8,128)S(1)}, u32[]{:S(2)}, u32[]{:S(2)}) %collective-permute-start.8) | collective-permute-done | bytes 57376 | tf_op jit(solution)/shard_map/ppermute | solution.py:514
  50.2 0.0 copy-done.5
  50.2 3.9 %steps.1 = (f32[3,4,32,256]{3,2,1,0:T(8,128)}, f32[3,4,32,256]{3,2,1,0:T(8,128)}, f32[3,4,32,256]{3,2,1,0:T(8,128)}, f32[3,4,32,256]{3,2,1,0:T(8,128)}, f32[4,4,32]{2,1,0:T(4,128)}) custom-call(f32[3,4,32,256]{3,2,1,0:T(8,128)S(1)} %copy-done, f32[3,4,32,256]{3,2,1,0:T(8,128)S(1)} %copy-done.1, f32[3,4,32,256]{3,2,1,0:T(8,128)S(1)} %copy-done.2, ...), custom_call_target="tpu_custom_call" | custom-call | flops 4000000 | bytes 4000000 | tf_op jit(solution)/shard_map/steps/pallas_call | solution.py:495
Async XLA Ops:
  0.6 2.8 %copy-start.3 = (f32[3,4,32,256]{3,2,1,0:T(8,128)S(1)}, f32[3,4,32,256]{3,2,1,0:T(8,128)}, u32[]{:S(2)}) copy-start(f32[3,4,32,256]{3,2,1,0:T(8,128)} %ha_in.1) | copy-start | bytes 1179652
  0.6 2.8 %copy-start.2 = (f32[3,4,32,256]{3,2,1,0:T(8,128)S(1)}, f32[3,4,32,256]{3,2,1,0:T(8,128)}, u32[]{:S(2)}) copy-start(f32[3,4,32,256]{3,2,1,0:T(8,128)} %ea_in.1) | copy-start | bytes 1179652
  0.7 2.8 %copy-start.1 = (f32[3,4,32,256]{3,2,1,0:T(8,128)S(1)}, f32[3,4,32,256]{3,2,1,0:T(8,128)}, u32[]{:S(2)}) copy-start(f32[3,4,32,256]{3,2,1,0:T(8,128)} %hf_in.1) | copy-start | bytes 1179652
  0.7 2.8 %copy-start = (f32[3,4,32,256]{3,2,1,0:T(8,128)S(1)}, f32[3,4,32,256]{3,2,1,0:T(8,128)}, u32[]{:S(2)}) copy-start(f32[3,4,32,256]{3,2,1,0:T(8,128)} %ef_in.1) | copy-start | bytes 1179652
  0.7 2.8 %copy-start.6 = (f32[4,32,256]{2,1,0:T(8,128)S(1)}, f32[4,32,256]{2,1,0:T(8,128)}, u32[]{:S(2)}) copy-start(f32[4,32,256]{2,1,0:T(8,128)} %eps.5) | copy-start | bytes 393220
  3.5 0.9 %copy-start.4 = (f32[192,128]{1,0:T(8,128)S(1)}, f32[192,128]{1,0:T(8,128)}, u32[]{:S(2)}) copy-start(f32[192,128]{1,0:T(8,128)} %message.1.mine) | copy-start | bytes 294916
  4.8 19.6 %collective-permute-start = (f32[288,256]{1,0:T(8,128)S(1)}, f32[288,256]{1,0:T(8,128)S(1)}, u32[]{:S(2)}, u32[]{:S(2)}) collective-permute-start(f32[288,256]{1,0:T(8,128)S(1)} %get-tuple-element.16), channel_id=1, source_target_pairs={{16,32},{48,64},{80,96},{112,128},{32,16},{64,48},{96,80},{128,112... | collective-permute-start | bytes 884744 | tf_op jit(solution)/shard_map/ppermute | solution.py:514
  9.4 16.7 %collective-permute-start.1 = (f32[288,256]{1,0:T(8,128)S(1)}, f32[288,256]{1,0:T(8,128)S(1)}, u32[]{:S(2)}, u32[]{:S(2)}) collective-permute-start(f32[288,256]{1,0:T(8,128)S(1)} %get-tuple-element.17), channel_id=1, source_target_pairs={{0,16},{32,48},{64,80},{96,112},{16,0},{48,32},{80,64},{112,96},{1... | collective-permute-start | bytes 884744 | tf_op jit(solution)/shard_map/ppermute | solution.py:514
  11.3 13.0 %collective-permute-start.2 = (f32[192,128]{1,0:T(8,128)S(1)}, f32[192,128]{1,0:T(8,128)S(1)}, u32[]{:S(2)}, u32[]{:S(2)}) collective-permute-start(f32[192,128]{1,0:T(8,128)S(1)} %copy-done.4), channel_id=1, source_target_pairs={{0,496},{16,480},{32,464},{48,448},{64,432},{80,416},{96,400},{112... | collective-permute-start | bytes 294920 | tf_op jit(solution)/shard_map/ppermute | solution.py:519
  17.1 30.1 %collective-permute-start.5 = (f32[288,256]{1,0:T(8,128)S(1)}, f32[288,256]{1,0:T(8,128)S(1)}, u32[]{:S(2)}, u32[]{:S(2)}) collective-permute-start(f32[288,256]{1,0:T(8,128)S(1)} %get-tuple-element.16), channel_id=1, source_target_pairs={{144,160},{176,192},{208,224},{240,256},{272,288},{304,320},{336,3... | collective-permute-start | bytes 884744 | tf_op jit(solution)/shard_map/ppermute | solution.py:514
  17.8 29.4 %collective-permute-start.6 = (f32[288,256]{1,0:T(8,128)S(1)}, f32[288,256]{1,0:T(8,128)S(1)}, u32[]{:S(2)}, u32[]{:S(2)}) collective-permute-start(f32[288,256]{1,0:T(8,128)S(1)} %get-tuple-element.17), channel_id=1, source_target_pairs={{128,144},{160,176},{192,208},{224,240},{256,272},{288,304},{320,3... | collective-permute-start | bytes 884744 | tf_op jit(solution)/shard_map/ppermute | solution.py:514
  26.6 8.8 %collective-permute-start.3 = (f32[112,256]{1,0:T(8,128)S(1)}, f32[112,256]{1,0:T(8,128)S(1)}, u32[]{:S(2)}, u32[]{:S(2)}) collective-permute-start(f32[112,256]{1,0:T(8,128)S(1)} %get-tuple-element.20), channel_id=1, source_target_pairs={{1,2},{3,4},{5,6},{7,8},{9,10},{11,12},{13,14},{2,1},{4,3},{6,5},{... | collective-permute-start | bytes 344072 | tf_op jit(solution)/shard_map/ppermute | solution.py:514
  30.9 4.5 %collective-permute-start.4 = (f32[112,256]{1,0:T(8,128)S(1)}, f32[112,256]{1,0:T(8,128)S(1)}, u32[]{:S(2)}, u32[]{:S(2)}) collective-permute-start(f32[112,256]{1,0:T(8,128)S(1)} %get-tuple-element.21), channel_id=1, source_target_pairs={{0,1},{2,3},{4,5},{6,7},{8,9},{10,11},{12,13},{14,15},{1,0},{3,2},... | collective-permute-start | bytes 344072 | tf_op jit(solution)/shard_map/ppermute | solution.py:514
  35.4 14.8 %copy-start.5 = (f32[192,128]{1,0:T(8,128)S(1)}, f32[192,128]{1,0:T(8,128)}, u32[]{:S(2)}) copy-start(f32[192,128]{1,0:T(8,128)} %message.1.mine) | copy-start | bytes 294916
  36.2 11.0 %collective-permute-start.7 = (f32[56,256]{1,0:T(8,128)S(1)}, f32[56,256]{1,0:T(8,128)S(1)}, u32[]{:S(2)}, u32[]{:S(2)}) collective-permute-start(f32[56,256]{1,0:T(8,128)S(1)} %get-tuple-element.25), channel_id=1, source_target_pairs={{16,32},{48,64},{80,96},{112,128},{144,160},{176,192},{208,224},{2... | collective-permute-start | bytes 172040 | tf_op jit(solution)/shard_map/ppermute | solution.py:514
  45.3 4.9 %collective-permute-start.8 = (f32[56,256]{1,0:T(8,128)S(1)}, f32[56,256]{1,0:T(8,128)S(1)}, u32[]{:S(2)}, u32[]{:S(2)}) collective-permute-start(f32[56,256]{1,0:T(8,128)S(1)} %get-tuple-element.26), channel_id=1, source_target_pairs={{0,16},{32,48},{64,80},{96,112},{128,144},{160,176},{192,208},{224... | collective-permute-start | bytes 172040 | tf_op jit(solution)/shard_map/ppermute | solution.py:514

commit v7 on v6

--- a/solution.py
+++ b/solution.py
@@ -550,7 +550,7 @@
     tops, ends, mirror, x_far, x_near = call(
         edges_kernel, [tile, tile, shape(4, FRAME, LANES), x_shape, x_shape],
         fields + [coef, mirror_coef, theirs, y_far, y_near],
-        [vmem(*x_shape.shape)] * 2, name="edges", work=1_000_000_000)
+        [vmem(*x_shape.shape)] * 2, name="edges", work=4_000_000_000)
     x_far, x_near = swapped(x_far, x_near, "gx")
     ef, hf, ea, ha, grad = call(
         step_kernel, [shape(*e_fwd.shape)] * 4 + [shape(*density.shape)],

time: 54.4 us -> 54.8 us (level)
  the two profiles are of different devices: /device:TPU:111 before, /device:TPU:261 now
where the time goes in v7:
time: 54.8 us; the launch traced here: 54.5 us
  starting transfers between devices  26.6 us (49%)
  waiting for transfers between devices  17.8 us (32%)
  Pallas kernels  8.24 us (15%)
  local copies, waits for them, and re-layouts  0.92 us (2%)
  between operations  0.84 us (2%)
    ppermute x4, starting transfers between devices, swapped(): lax.ppermute(far, axis, pairs(1))  15.8 us
    ppermute x4, waiting for transfers between devices, swapped(): lax.ppermute(near, axis, pairs(0))  9.55 us
    pallas_call x5, Pallas kernels, call(): pl.pallas_call(kernel, out_shape=outs, in_specs=[pl.BlockSpec(memory_spac...  8.24 us
    ppermute x1, waiting for transfers between devices, mirrored(): return lax.ppermute(block, axis, [(i, size - 1 - i) for i in range(size)])  8.21 us
    ppermute x4, starting transfers between devices, swapped(): lax.ppermute(near, axis, pairs(0))  8.05 us
    ppermute x1, starting transfers between devices, mirrored(): return lax.ppermute(block, axis, [(i, size - 1 - i) for i in range(size)])  2.75 us
  transfers between devices with their start and end apart: 9, of which 4 were waited for; matrix products, arithmetic and copies ran while one was open for 0% of the time, Pallas kernels for 1%

profile of v7, /device:TPU:261, one launch (start us, length us, event | category | flops | bytes accessed | tf_op | source)
XLA Modules:
  0.0 54.5 jit_solution(17531698540065716452)
XLA Ops:
  0.6 0.0 copy-start.3
  0.6 0.0 copy-start.2
  0.7 0.0 copy-start.1
  0.7 0.0 copy-start
  0.7 0.0 copy-start.6
  0.7 2.7 %message.1.mine = f32[192,128]{1,0:T(8,128)} custom-call(f32[3,4,32,256]{3,2,1,0:T(8,128)} %ef_in.1, f32[3,4,32,256]{3,2,1,0:T(8,128)} %hf_in.1, f32[3,4,32,256]{3,2,1,0:T(8,128)} %ea_in.1, f32[3,4,32,256]{3,2,1,0:T(8,128)} %ha_in.1, f32[4,32,256]{2,1,0:T(8,128)} %eps.5, f32[4,4,32]{2,1,0:T(4,128)} %density.1, s32[4,4,32]{2,1,0:T(4,128)} %mask.1, ...), custom_call_target="tpu_custom_call" | custom-call | flops 4000000 | bytes 4000000 | tf_op jit(solution)/shard_map/message/pallas_call | solution.py:495
  3.4 0.0 copy-done.3
  3.5 0.0 copy-done.2
  3.5 0.0 copy-done.1
  3.5 0.0 copy-done
  3.5 0.0 copy-done.6
  3.5 0.0 copy-start.4
  3.5 0.9 %copy-done.4 = f32[192,128]{1,0:T(8,128)S(1)} copy-done((f32[192,128]{1,0:T(8,128)S(1)}, f32[192,128]{1,0:T(8,128)}, u32[]{:S(2)}) %copy-start.4) | copy-done | bytes 98328
  4.4 0.4 bulk.1
  4.8 0.7 %collective-permute-start = (f32[288,256]{1,0:T(8,128)S(1)}, f32[288,256]{1,0:T(8,128)S(1)}, u32[]{:S(2)}, u32[]{:S(2)}) collective-permute-start(f32[288,256]{1,0:T(8,128)S(1)} %get-tuple-element.16), channel_id=1, source_target_pairs={{16,32},{48,64},{80,96},{112,128},{32,16},{64,48},{96,80},{128,112... | collective-permute-start | bytes 884744 | tf_op jit(solution)/shard_map/ppermute | solution.py:514
  5.4 0.7 %collective-permute-start.1 = (f32[288,256]{1,0:T(8,128)S(1)}, f32[288,256]{1,0:T(8,128)S(1)}, u32[]{:S(2)}, u32[]{:S(2)}) collective-permute-start(f32[288,256]{1,0:T(8,128)S(1)} %get-tuple-element.17), channel_id=1, source_target_pairs={{0,16},{32,48},{64,80},{96,112},{16,0},{48,32},{80,64},{112,96},{1... | collective-permute-start | bytes 884744 | tf_op jit(solution)/shard_map/ppermute | solution.py:514
  6.1 2.7 %collective-permute-start.2 = (f32[192,128]{1,0:T(8,128)S(1)}, f32[192,128]{1,0:T(8,128)S(1)}, u32[]{:S(2)}, u32[]{:S(2)}) collective-permute-start(f32[192,128]{1,0:T(8,128)S(1)} %copy-done.4), channel_id=1, source_target_pairs={{0,496},{16,480},{32,464},{48,448},{64,432},{80,416},{96,400},{112... | collective-permute-start | bytes 294920 | tf_op jit(solution)/shard_map/ppermute | solution.py:519
  8.9 8.2 %collective-permute-done.2.theirs = f32[192,128]{1,0:T(8,128)S(1)} collective-permute-done((f32[192,128]{1,0:T(8,128)S(1)}, f32[192,128]{1,0:T(8,128)S(1)}, u32[]{:S(2)}, u32[]{:S(2)}) %collective-permute-start.2) | collective-permute-done | bytes 98336 | tf_op jit(solution)/shard_map/ppermute | solution.py:519
  17.1 0.0 collective-permute-done.bulk_far.bulk_far_1
  17.1 0.0 collective-permute-done.1.bulk_near.bulk_near_1
  17.1 0.5 coefficient.1
  17.6 9.4 %collective-permute-start.3 = (f32[112,256]{1,0:T(8,128)S(1)}, f32[112,256]{1,0:T(8,128)S(1)}, u32[]{:S(2)}, u32[]{:S(2)}) collective-permute-start(f32[112,256]{1,0:T(8,128)S(1)} %get-tuple-element.20), channel_id=1, source_target_pairs={{1,2},{3,4},{5,6},{7,8},{9,10},{11,12},{13,14},{2,1},{4,3},{6,5},{... | collective-permute-start | bytes 344072 | tf_op jit(solution)/shard_map/ppermute | solution.py:514
  27.0 1.9 %collective-permute-start.4 = (f32[112,256]{1,0:T(8,128)S(1)}, f32[112,256]{1,0:T(8,128)S(1)}, u32[]{:S(2)}, u32[]{:S(2)}) collective-permute-start(f32[112,256]{1,0:T(8,128)S(1)} %get-tuple-element.21), channel_id=1, source_target_pairs={{0,1},{2,3},{4,5},{6,7},{8,9},{10,11},{12,13},{14,15},{1,0},{3,2},... | collective-permute-start | bytes 344072 | tf_op jit(solution)/shard_map/ppermute | solution.py:514
  28.9 1.9 %collective-permute-start.5 = (f32[288,256]{1,0:T(8,128)S(1)}, f32[288,256]{1,0:T(8,128)S(1)}, u32[]{:S(2)}, u32[]{:S(2)}) collective-permute-start(f32[288,256]{1,0:T(8,128)S(1)} %get-tuple-element.16), channel_id=1, source_target_pairs={{144,160},{176,192},{208,224},{240,256},{272,288},{304,320},{336,3... | collective-permute-start | bytes 884744 | tf_op jit(solution)/shard_map/ppermute | solution.py:514
  30.8 3.5 %collective-permute-start.6 = (f32[288,256]{1,0:T(8,128)S(1)}, f32[288,256]{1,0:T(8,128)S(1)}, u32[]{:S(2)}, u32[]{:S(2)}) collective-permute-start(f32[288,256]{1,0:T(8,128)S(1)} %get-tuple-element.17), channel_id=1, source_target_pairs={{128,144},{160,176},{192,208},{224,240},{256,272},{288,304},{320,3... | collective-permute-start | bytes 884744 | tf_op jit(solution)/shard_map/ppermute | solution.py:514
  34.3 0.0 collective-permute-done.3.y_far
  34.4 0.0 collective-permute-done.4.y_near
  34.4 0.0 copy-start.5
  34.4 0.8 %edges.1 = (f32[52,8,256]{2,1,0:T(8,128)S(1)}, f32[52,8,256]{2,1,0:T(8,128)S(1)}, f32[4,48,128]{2,1,0:T(8,128)S(1)}, f32[56,256]{1,0:T(8,128)S(1)}, f32[56,256]{1,0:T(8,128)S(1)}) custom-call(f32[3,4,32,256]{3,2,1,0:T(8,128)S(1)} %copy-done, f32[3,4,32,256]{3,2,1,0:T(8,128)S(1)} %copy-done.1, f32[3,4,32,256]{3,2,1,0:T(8,128)S(1)} %copy-done.2, ...), custom_call_target="tpu_custom_call" | custom-call | flops 4000000000 | bytes 4000000 | tf_op jit(solution)/shard_map/edges/pallas_call | solution.py:495
  35.1 3.9 %collective-permute-start.7 = (f32[56,256]{1,0:T(8,128)S(1)}, f32[56,256]{1,0:T(8,128)S(1)}, u32[]{:S(2)}, u32[]{:S(2)}) collective-permute-start(f32[56,256]{1,0:T(8,128)S(1)} %get-tuple-element.25), channel_id=1, source_target_pairs={{16,32},{48,64},{80,96},{112,128},{144,160},{176,192},{208,224},{2... | collective-permute-start | bytes 172040 | tf_op jit(solution)/shard_map/ppermute | solution.py:514
  39.0 1.9 %collective-permute-start.8 = (f32[56,256]{1,0:T(8,128)S(1)}, f32[56,256]{1,0:T(8,128)S(1)}, u32[]{:S(2)}, u32[]{:S(2)}) collective-permute-start(f32[56,256]{1,0:T(8,128)S(1)} %get-tuple-element.26), channel_id=1, source_target_pairs={{0,16},{32,48},{64,80},{96,112},{128,144},{160,176},{192,208},{224... | collective-permute-start | bytes 172040 | tf_op jit(solution)/shard_map/ppermute | solution.py:514
  40.9 0.1 collective-permute-done.5.bulk_far_2
  41.0 8.3 %collective-permute-done.6.bulk_near_2 = f32[288,256]{1,0:T(8,128)S(1)} collective-permute-done((f32[288,256]{1,0:T(8,128)S(1)}, f32[288,256]{1,0:T(8,128)S(1)}, u32[]{:S(2)}, u32[]{:S(2)}) %collective-permute-start.6) | collective-permute-done | bytes 294944 | tf_op jit(solution)/shard_map/ppermute | solution.py:514
  49.3 0.0 collective-permute-done.7.x_far
  49.3 1.2 %collective-permute-done.8.x_near = f32[56,256]{1,0:T(8,128)S(1)} collective-permute-done((f32[56,256]{1,0:T(8,128)S(1)}, f32[56,256]{1,0:T(8,128)S(1)}, u32[]{:S(2)}, u32[]{:S(2)}) %collective-permute-start.8) | collective-permute-done | bytes 57376 | tf_op jit(solution)/shard_map/ppermute | solution.py:514
  50.6 0.0 copy-done.5
  50.6 3.9 %steps.1 = (f32[3,4,32,256]{3,2,1,0:T(8,128)}, f32[3,4,32,256]{3,2,1,0:T(8,128)}, f32[3,4,32,256]{3,2,1,0:T(8,128)}, f32[3,4,32,256]{3,2,1,0:T(8,128)}, f32[4,4,32]{2,1,0:T(4,128)}) custom-call(f32[3,4,32,256]{3,2,1,0:T(8,128)S(1)} %copy-done, f32[3,4,32,256]{3,2,1,0:T(8,128)S(1)} %copy-done.1, f32[3,4,32,256]{3,2,1,0:T(8,128)S(1)} %copy-done.2, ...), custom_call_target="tpu_custom_call" | custom-call | flops 4000000 | bytes 4000000 | tf_op jit(solution)/shard_map/steps/pallas_call | solution.py:495
Async XLA Ops:
  0.6 2.8 %copy-start.3 = (f32[3,4,32,256]{3,2,1,0:T(8,128)S(1)}, f32[3,4,32,256]{3,2,1,0:T(8,128)}, u32[]{:S(2)}) copy-start(f32[3,4,32,256]{3,2,1,0:T(8,128)} %ha_in.1) | copy-start | bytes 1179652
  0.6 2.8 %copy-start.2 = (f32[3,4,32,256]{3,2,1,0:T(8,128)S(1)}, f32[3,4,32,256]{3,2,1,0:T(8,128)}, u32[]{:S(2)}) copy-start(f32[3,4,32,256]{3,2,1,0:T(8,128)} %ea_in.1) | copy-start | bytes 1179652
  0.7 2.8 %copy-start.1 = (f32[3,4,32,256]{3,2,1,0:T(8,128)S(1)}, f32[3,4,32,256]{3,2,1,0:T(8,128)}, u32[]{:S(2)}) copy-start(f32[3,4,32,256]{3,2,1,0:T(8,128)} %hf_in.1) | copy-start | bytes 1179652
  0.7 2.8 %copy-start = (f32[3,4,32,256]{3,2,1,0:T(8,128)S(1)}, f32[3,4,32,256]{3,2,1,0:T(8,128)}, u32[]{:S(2)}) copy-start(f32[3,4,32,256]{3,2,1,0:T(8,128)} %ef_in.1) | copy-start | bytes 1179652
  0.7 2.8 %copy-start.6 = (f32[4,32,256]{2,1,0:T(8,128)S(1)}, f32[4,32,256]{2,1,0:T(8,128)}, u32[]{:S(2)}) copy-start(f32[4,32,256]{2,1,0:T(8,128)} %eps.5) | copy-start | bytes 393220
  3.5 0.9 %copy-start.4 = (f32[192,128]{1,0:T(8,128)S(1)}, f32[192,128]{1,0:T(8,128)}, u32[]{:S(2)}) copy-start(f32[192,128]{1,0:T(8,128)} %message.1.mine) | copy-start | bytes 294916
  4.8 12.3 %collective-permute-start = (f32[288,256]{1,0:T(8,128)S(1)}, f32[288,256]{1,0:T(8,128)S(1)}, u32[]{:S(2)}, u32[]{:S(2)}) collective-permute-start(f32[288,256]{1,0:T(8,128)S(1)} %get-tuple-element.16), channel_id=1, source_target_pairs={{16,32},{48,64},{80,96},{112,128},{32,16},{64,48},{96,80},{128,112... | collective-permute-start | bytes 884744 | tf_op jit(solution)/shard_map/ppermute | solution.py:514
  5.4 11.7 %collective-permute-start.1 = (f32[288,256]{1,0:T(8,128)S(1)}, f32[288,256]{1,0:T(8,128)S(1)}, u32[]{:S(2)}, u32[]{:S(2)}) collective-permute-start(f32[288,256]{1,0:T(8,128)S(1)} %get-tuple-element.17), channel_id=1, source_target_pairs={{0,16},{32,48},{64,80},{96,112},{16,0},{48,32},{80,64},{112,96},{1... | collective-permute-start | bytes 884744 | tf_op jit(solution)/shard_map/ppermute | solution.py:514
  6.1 11.0 %collective-permute-start.2 = (f32[192,128]{1,0:T(8,128)S(1)}, f32[192,128]{1,0:T(8,128)S(1)}, u32[]{:S(2)}, u32[]{:S(2)}) collective-permute-start(f32[192,128]{1,0:T(8,128)S(1)} %copy-done.4), channel_id=1, source_target_pairs={{0,496},{16,480},{32,464},{48,448},{64,432},{80,416},{96,400},{112... | collective-permute-start | bytes 294920 | tf_op jit(solution)/shard_map/ppermute | solution.py:519
  17.6 16.8 %collective-permute-start.3 = (f32[112,256]{1,0:T(8,128)S(1)}, f32[112,256]{1,0:T(8,128)S(1)}, u32[]{:S(2)}, u32[]{:S(2)}) collective-permute-start(f32[112,256]{1,0:T(8,128)S(1)} %get-tuple-element.20), channel_id=1, source_target_pairs={{1,2},{3,4},{5,6},{7,8},{9,10},{11,12},{13,14},{2,1},{4,3},{6,5},{... | collective-permute-start | bytes 344072 | tf_op jit(solution)/shard_map/ppermute | solution.py:514
  27.0 7.4 %collective-permute-start.4 = (f32[112,256]{1,0:T(8,128)S(1)}, f32[112,256]{1,0:T(8,128)S(1)}, u32[]{:S(2)}, u32[]{:S(2)}) collective-permute-start(f32[112,256]{1,0:T(8,128)S(1)} %get-tuple-element.21), channel_id=1, source_target_pairs={{0,1},{2,3},{4,5},{6,7},{8,9},{10,11},{12,13},{14,15},{1,0},{3,2},... | collective-permute-start | bytes 344072 | tf_op jit(solution)/shard_map/ppermute | solution.py:514
  28.9 12.1 %collective-permute-start.5 = (f32[288,256]{1,0:T(8,128)S(1)}, f32[288,256]{1,0:T(8,128)S(1)}, u32[]{:S(2)}, u32[]{:S(2)}) collective-permute-start(f32[288,256]{1,0:T(8,128)S(1)} %get-tuple-element.16), channel_id=1, source_target_pairs={{144,160},{176,192},{208,224},{240,256},{272,288},{304,320},{336,3... | collective-permute-start | bytes 884744 | tf_op jit(solution)/shard_map/ppermute | solution.py:514
  30.8 18.5 %collective-permute-start.6 = (f32[288,256]{1,0:T(8,128)S(1)}, f32[288,256]{1,0:T(8,128)S(1)}, u32[]{:S(2)}, u32[]{:S(2)}) collective-permute-start(f32[288,256]{1,0:T(8,128)S(1)} %get-tuple-element.17), channel_id=1, source_target_pairs={{128,144},{160,176},{192,208},{224,240},{256,272},{288,304},{320,3... | collective-permute-start | bytes 884744 | tf_op jit(solution)/shard_map/ppermute | solution.py:514
  34.4 16.2 %copy-start.5 = (f32[192,128]{1,0:T(8,128)S(1)}, f32[192,128]{1,0:T(8,128)}, u32[]{:S(2)}) copy-start(f32[192,128]{1,0:T(8,128)} %message.1.mine) | copy-start | bytes 294916
  35.1 14.2 %collective-permute-start.7 = (f32[56,256]{1,0:T(8,128)S(1)}, f32[56,256]{1,0:T(8,128)S(1)}, u32[]{:S(2)}, u32[]{:S(2)}) collective-permute-start(f32[56,256]{1,0:T(8,128)S(1)} %get-tuple-element.25), channel_id=1, source_target_pairs={{16,32},{48,64},{80,96},{112,128},{144,160},{176,192},{208,224},{2... | collective-permute-start | bytes 172040 | tf_op jit(solution)/shard_map/ppermute | solution.py:514
  39.0 11.5 %collective-permute-start.8 = (f32[56,256]{1,0:T(8,128)S(1)}, f32[56,256]{1,0:T(8,128)S(1)}, u32[]{:S(2)}, u32[]{:S(2)}) collective-permute-start(f32[56,256]{1,0:T(8,128)S(1)} %get-tuple-element.26), channel_id=1, source_target_pairs={{0,16},{32,48},{64,80},{96,112},{128,144},{160,176},{192,208},{224... | collective-permute-start | bytes 172040 | tf_op jit(solution)/shard_map/ppermute | solution.py:514

commit v8 on v6

--- a/solution.py
+++ b/solution.py
@@ -537,7 +537,7 @@
          square, pltpu.SemaphoreType.DMA((10,))], name="message", any_in=True)
     theirs = mirrored(mine, "gx")
     bulk = call(bulk_kernel, [bulk_shape, bulk_shape], [*fields, eps_back, mine], name="bulk")
-    early = lax.axis_size("gx") // 4
+    early = 7 * lax.axis_size("gx") // 16
     bulk_lower = swapped(*bulk, "gx", stop=early)
     bulk_upper = swapped(*bulk, "gx", start=early)
     y_shape = shape(2 * (13 * nx) + 8, nz)

time: 54.4 us -> 53.6 us (0.985)
  the two profiles are of different devices: /device:TPU:111 before, /device:TPU:239 now
where the time goes in v8:
time: 53.6 us; the launch traced here: 53.3 us
  starting transfers between devices  34.8 us (65%)
  waiting for transfers between devices  8.49 us (16%)
  Pallas kernels  8.24 us (15%)
  local copies, waits for them, and re-layouts  0.91 us (2%)
  between operations  0.87 us (2%)
    ppermute x4, starting transfers between devices, swapped(): lax.ppermute(far, axis, pairs(1))  23.7 us
    pallas_call x5, Pallas kernels, call(): pl.pallas_call(kernel, out_shape=outs, in_specs=[pl.BlockSpec(memory_spac...  8.24 us
    ppermute x4, starting transfers between devices, swapped(): lax.ppermute(near, axis, pairs(0))  6.44 us
    ppermute x4, waiting for transfers between devices, swapped(): lax.ppermute(far, axis, pairs(1))  5.51 us
    ppermute x1, starting transfers between devices, mirrored(): return lax.ppermute(block, axis, [(i, size - 1 - i) for i in range(size)])  4.64 us
    ppermute x4, waiting for transfers between devices, swapped(): lax.ppermute(near, axis, pairs(0))  2.97 us
  transfers between devices with their start and end apart: 9, of which 2 were waited for; matrix products, arithmetic and copies ran while one was open for 0% of the time, Pallas kernels for 2%

profile of v8, /device:TPU:239, one launch (start us, length us, event | category | flops | bytes accessed | tf_op | source)
XLA Modules:
  0.0 53.3 jit_solution(3495698660059193992)
XLA Ops:
  0.6 0.0 copy-start.3
  0.6 0.0 copy-start.2
  0.7 0.0 copy-start.1
  0.7 0.0 copy-start
  0.7 0.0 copy-start.6
  0.7 2.7 %message.1.mine = f32[192,128]{1,0:T(8,128)} custom-call(f32[3,4,32,256]{3,2,1,0:T(8,128)} %ef_in.1, f32[3,4,32,256]{3,2,1,0:T(8,128)} %hf_in.1, f32[3,4,32,256]{3,2,1,0:T(8,128)} %ea_in.1, f32[3,4,32,256]{3,2,1,0:T(8,128)} %ha_in.1, f32[4,32,256]{2,1,0:T(8,128)} %eps.5, f32[4,4,32]{2,1,0:T(4,128)} %density.1, s32[4,4,32]{2,1,0:T(4,128)} %mask.1, ...), custom_call_target="tpu_custom_call" | custom-call | flops 4000000 | bytes 4000000 | tf_op jit(solution)/shard_map/message/pallas_call | solution.py:495
  3.4 0.0 copy-done.3
  3.5 0.0 copy-done.2
  3.5 0.0 copy-done.1
  3.5 0.0 copy-done
  3.5 0.0 copy-done.6
  3.5 0.0 copy-start.4
  3.5 0.9 %copy-done.4 = f32[192,128]{1,0:T(8,128)S(1)} copy-done((f32[192,128]{1,0:T(8,128)S(1)}, f32[192,128]{1,0:T(8,128)}, u32[]{:S(2)}) %copy-start.4) | copy-done | bytes 98328
  4.4 0.4 bulk.1
  4.8 0.7 %collective-permute-start = (f32[288,256]{1,0:T(8,128)S(1)}, f32[288,256]{1,0:T(8,128)S(1)}, u32[]{:S(2)}, u32[]{:S(2)}) collective-permute-start(f32[288,256]{1,0:T(8,128)S(1)} %get-tuple-element.16), channel_id=1, source_target_pairs={{16,32},{48,64},{80,96},{112,128},{144,160},{176,192},{208,224},{3... | collective-permute-start | bytes 884744 | tf_op jit(solution)/shard_map/ppermute | solution.py:514
  5.4 0.7 %collective-permute-start.1 = (f32[288,256]{1,0:T(8,128)S(1)}, f32[288,256]{1,0:T(8,128)S(1)}, u32[]{:S(2)}, u32[]{:S(2)}) collective-permute-start(f32[288,256]{1,0:T(8,128)S(1)} %get-tuple-element.17), channel_id=1, source_target_pairs={{0,16},{32,48},{64,80},{96,112},{128,144},{160,176},{192,208},{16,... | collective-permute-start | bytes 884744 | tf_op jit(solution)/shard_map/ppermute | solution.py:514
  6.1 4.6 %collective-permute-start.2 = (f32[192,128]{1,0:T(8,128)S(1)}, f32[192,128]{1,0:T(8,128)S(1)}, u32[]{:S(2)}, u32[]{:S(2)}) collective-permute-start(f32[192,128]{1,0:T(8,128)S(1)} %copy-done.4), channel_id=1, source_target_pairs={{0,496},{16,480},{32,464},{48,448},{64,432},{80,416},{96,400},{112... | collective-permute-start | bytes 294920 | tf_op jit(solution)/shard_map/ppermute | solution.py:519
  10.8 2.7 %collective-permute-start.5 = (f32[288,256]{1,0:T(8,128)S(1)}, f32[288,256]{1,0:T(8,128)S(1)}, u32[]{:S(2)}, u32[]{:S(2)}) collective-permute-start(f32[288,256]{1,0:T(8,128)S(1)} %get-tuple-element.16), channel_id=1, source_target_pairs={{240,256},{272,288},{304,320},{336,352},{368,384},{400,416},{432,4... | collective-permute-start | bytes 884744 | tf_op jit(solution)/shard_map/ppermute | solution.py:514
  13.5 1.9 %collective-permute-start.6 = (f32[288,256]{1,0:T(8,128)S(1)}, f32[288,256]{1,0:T(8,128)S(1)}, u32[]{:S(2)}, u32[]{:S(2)}) collective-permute-start(f32[288,256]{1,0:T(8,128)S(1)} %get-tuple-element.17), channel_id=1, source_target_pairs={{224,240},{256,272},{288,304},{320,336},{352,368},{384,400},{416,4... | collective-permute-start | bytes 884744 | tf_op jit(solution)/shard_map/ppermute | solution.py:514
  15.5 0.0 collective-permute-done.2.theirs
  15.5 0.0 collective-permute-done.bulk_far.bulk_far_1
  15.5 0.0 collective-permute-done.1.bulk_near.bulk_near_1
  15.5 0.5 coefficient.1
  16.0 5.0 %collective-permute-start.3 = (f32[112,256]{1,0:T(8,128)S(1)}, f32[112,256]{1,0:T(8,128)S(1)}, u32[]{:S(2)}, u32[]{:S(2)}) collective-permute-start(f32[112,256]{1,0:T(8,128)S(1)} %get-tuple-element.20), channel_id=1, source_target_pairs={{1,2},{3,4},{5,6},{7,8},{9,10},{11,12},{13,14},{2,1},{4,3},{6,5},{... | collective-permute-start | bytes 344072 | tf_op jit(solution)/shard_map/ppermute | solution.py:514
  21.0 1.9 %collective-permute-start.4 = (f32[112,256]{1,0:T(8,128)S(1)}, f32[112,256]{1,0:T(8,128)S(1)}, u32[]{:S(2)}, u32[]{:S(2)}) collective-permute-start(f32[112,256]{1,0:T(8,128)S(1)} %get-tuple-element.21), channel_id=1, source_target_pairs={{0,1},{2,3},{4,5},{6,7},{8,9},{10,11},{12,13},{14,15},{1,0},{3,2},... | collective-permute-start | bytes 344072 | tf_op jit(solution)/shard_map/ppermute | solution.py:514
  23.0 5.5 %collective-permute-done.3.y_far = f32[112,256]{1,0:T(8,128)S(1)} collective-permute-done((f32[112,256]{1,0:T(8,128)S(1)}, f32[112,256]{1,0:T(8,128)S(1)}, u32[]{:S(2)}, u32[]{:S(2)}) %collective-permute-start.3) | collective-permute-done | bytes 114720 | tf_op jit(solution)/shard_map/ppermute | solution.py:514
  28.5 0.0 collective-permute-done.4.y_near
  28.5 0.0 copy-start.5
  28.5 0.8 %edges.1 = (f32[52,8,256]{2,1,0:T(8,128)S(1)}, f32[52,8,256]{2,1,0:T(8,128)S(1)}, f32[4,48,128]{2,1,0:T(8,128)S(1)}, f32[56,256]{1,0:T(8,128)S(1)}, f32[56,256]{1,0:T(8,128)S(1)}) custom-call(f32[3,4,32,256]{3,2,1,0:T(8,128)S(1)} %copy-done, f32[3,4,32,256]{3,2,1,0:T(8,128)S(1)} %copy-done.1, f32[3,4,32,256]{3,2,1,0:T(8,128)S(1)} %copy-done.2, ...), custom_call_target="tpu_custom_call" | custom-call | flops 1000000000 | bytes 4000000 | tf_op jit(solution)/shard_map/edges/pallas_call | solution.py:495
  29.2 15.2 %collective-permute-start.7 = (f32[56,256]{1,0:T(8,128)S(1)}, f32[56,256]{1,0:T(8,128)S(1)}, u32[]{:S(2)}, u32[]{:S(2)}) collective-permute-start(f32[56,256]{1,0:T(8,128)S(1)} %get-tuple-element.25), channel_id=1, source_target_pairs={{16,32},{48,64},{80,96},{112,128},{144,160},{176,192},{208,224},{2... | collective-permute-start | bytes 172040 | tf_op jit(solution)/shard_map/ppermute | solution.py:514
  44.4 1.9 %collective-permute-start.8 = (f32[56,256]{1,0:T(8,128)S(1)}, f32[56,256]{1,0:T(8,128)S(1)}, u32[]{:S(2)}, u32[]{:S(2)}) collective-permute-start(f32[56,256]{1,0:T(8,128)S(1)} %get-tuple-element.26), channel_id=1, source_target_pairs={{0,16},{32,48},{64,80},{96,112},{128,144},{160,176},{192,208},{224... | collective-permute-start | bytes 172040 | tf_op jit(solution)/shard_map/ppermute | solution.py:514
  46.4 0.0 collective-permute-done.5.bulk_far_2
  46.4 0.0 collective-permute-done.6.bulk_near_2
  46.4 0.0 collective-permute-done.7.x_far
  46.4 3.0 %collective-permute-done.8.x_near = f32[56,256]{1,0:T(8,128)S(1)} collective-permute-done((f32[56,256]{1,0:T(8,128)S(1)}, f32[56,256]{1,0:T(8,128)S(1)}, u32[]{:S(2)}, u32[]{:S(2)}) %collective-permute-start.8) | collective-permute-done | bytes 57376 | tf_op jit(solution)/shard_map/ppermute | solution.py:514
  49.4 0.0 copy-done.5
  49.4 3.9 %steps.1 = (f32[3,4,32,256]{3,2,1,0:T(8,128)}, f32[3,4,32,256]{3,2,1,0:T(8,128)}, f32[3,4,32,256]{3,2,1,0:T(8,128)}, f32[3,4,32,256]{3,2,1,0:T(8,128)}, f32[4,4,32]{2,1,0:T(4,128)}) custom-call(f32[3,4,32,256]{3,2,1,0:T(8,128)S(1)} %copy-done, f32[3,4,32,256]{3,2,1,0:T(8,128)S(1)} %copy-done.1, f32[3,4,32,256]{3,2,1,0:T(8,128)S(1)} %copy-done.2, ...), custom_call_target="tpu_custom_call" | custom-call | flops 4000000 | bytes 4000000 | tf_op jit(solution)/shard_map/steps/pallas_call | solution.py:495
Async XLA Ops:
  0.6 2.8 %copy-start.3 = (f32[3,4,32,256]{3,2,1,0:T(8,128)S(1)}, f32[3,4,32,256]{3,2,1,0:T(8,128)}, u32[]{:S(2)}) copy-start(f32[3,4,32,256]{3,2,1,0:T(8,128)} %ha_in.1) | copy-start | bytes 1179652
  0.6 2.8 %copy-start.2 = (f32[3,4,32,256]{3,2,1,0:T(8,128)S(1)}, f32[3,4,32,256]{3,2,1,0:T(8,128)}, u32[]{:S(2)}) copy-start(f32[3,4,32,256]{3,2,1,0:T(8,128)} %ea_in.1) | copy-start | bytes 1179652
  0.7 2.8 %copy-start.1 = (f32[3,4,32,256]{3,2,1,0:T(8,128)S(1)}, f32[3,4,32,256]{3,2,1,0:T(8,128)}, u32[]{:S(2)}) copy-start(f32[3,4,32,256]{3,2,1,0:T(8,128)} %hf_in.1) | copy-start | bytes 1179652
  0.7 2.8 %copy-start = (f32[3,4,32,256]{3,2,1,0:T(8,128)S(1)}, f32[3,4,32,256]{3,2,1,0:T(8,128)}, u32[]{:S(2)}) copy-start(f32[3,4,32,256]{3,2,1,0:T(8,128)} %ef_in.1) | copy-start | bytes 1179652
  0.7 2.8 %copy-start.6 = (f32[4,32,256]{2,1,0:T(8,128)S(1)}, f32[4,32,256]{2,1,0:T(8,128)}, u32[]{:S(2)}) copy-start(f32[4,32,256]{2,1,0:T(8,128)} %eps.5) | copy-start | bytes 393220
  3.5 0.9 %copy-start.4 = (f32[192,128]{1,0:T(8,128)S(1)}, f32[192,128]{1,0:T(8,128)}, u32[]{:S(2)}) copy-start(f32[192,128]{1,0:T(8,128)} %message.1.mine) | copy-start | bytes 294916
  4.8 10.7 %collective-permute-start = (f32[288,256]{1,0:T(8,128)S(1)}, f32[288,256]{1,0:T(8,128)S(1)}, u32[]{:S(2)}, u32[]{:S(2)}) collective-permute-start(f32[288,256]{1,0:T(8,128)S(1)} %get-tuple-element.16), channel_id=1, source_target_pairs={{16,32},{48,64},{80,96},{112,128},{144,160},{176,192},{208,224},{3... | collective-permute-start | bytes 884744 | tf_op jit(solution)/shard_map/ppermute | solution.py:514
  5.4 10.0 %collective-permute-start.1 = (f32[288,256]{1,0:T(8,128)S(1)}, f32[288,256]{1,0:T(8,128)S(1)}, u32[]{:S(2)}, u32[]{:S(2)}) collective-permute-start(f32[288,256]{1,0:T(8,128)S(1)} %get-tuple-element.17), channel_id=1, source_target_pairs={{0,16},{32,48},{64,80},{96,112},{128,144},{160,176},{192,208},{16,... | collective-permute-start | bytes 884744 | tf_op jit(solution)/shard_map/ppermute | solution.py:514
  6.1 9.3 %collective-permute-start.2 = (f32[192,128]{1,0:T(8,128)S(1)}, f32[192,128]{1,0:T(8,128)S(1)}, u32[]{:S(2)}, u32[]{:S(2)}) collective-permute-start(f32[192,128]{1,0:T(8,128)S(1)} %copy-done.4), channel_id=1, source_target_pairs={{0,496},{16,480},{32,464},{48,448},{64,432},{80,416},{96,400},{112... | collective-permute-start | bytes 294920 | tf_op jit(solution)/shard_map/ppermute | solution.py:519
  10.8 35.6 %collective-permute-start.5 = (f32[288,256]{1,0:T(8,128)S(1)}, f32[288,256]{1,0:T(8,128)S(1)}, u32[]{:S(2)}, u32[]{:S(2)}) collective-permute-start(f32[288,256]{1,0:T(8,128)S(1)} %get-tuple-element.16), channel_id=1, source_target_pairs={{240,256},{272,288},{304,320},{336,352},{368,384},{400,416},{432,4... | collective-permute-start | bytes 884744 | tf_op jit(solution)/shard_map/ppermute | solution.py:514
  13.5 32.8 %collective-permute-start.6 = (f32[288,256]{1,0:T(8,128)S(1)}, f32[288,256]{1,0:T(8,128)S(1)}, u32[]{:S(2)}, u32[]{:S(2)}) collective-permute-start(f32[288,256]{1,0:T(8,128)S(1)} %get-tuple-element.17), channel_id=1, source_target_pairs={{224,240},{256,272},{288,304},{320,336},{352,368},{384,400},{416,4... | collective-permute-start | bytes 884744 | tf_op jit(solution)/shard_map/ppermute | solution.py:514
  16.0 12.5 %collective-permute-start.3 = (f32[112,256]{1,0:T(8,128)S(1)}, f32[112,256]{1,0:T(8,128)S(1)}, u32[]{:S(2)}, u32[]{:S(2)}) collective-permute-start(f32[112,256]{1,0:T(8,128)S(1)} %get-tuple-element.20), channel_id=1, source_target_pairs={{1,2},{3,4},{5,6},{7,8},{9,10},{11,12},{13,14},{2,1},{4,3},{6,5},{... | collective-permute-start | bytes 344072 | tf_op jit(solution)/shard_map/ppermute | solution.py:514
  21.0 7.4 %collective-permute-start.4 = (f32[112,256]{1,0:T(8,128)S(1)}, f32[112,256]{1,0:T(8,128)S(1)}, u32[]{:S(2)}, u32[]{:S(2)}) collective-permute-start(f32[112,256]{1,0:T(8,128)S(1)} %get-tuple-element.21), channel_id=1, source_target_pairs={{0,1},{2,3},{4,5},{6,7},{8,9},{10,11},{12,13},{14,15},{1,0},{3,2},... | collective-permute-start | bytes 344072 | tf_op jit(solution)/shard_map/ppermute | solution.py:514
  28.5 20.9 %copy-start.5 = (f32[192,128]{1,0:T(8,128)S(1)}, f32[192,128]{1,0:T(8,128)}, u32[]{:S(2)}) copy-start(f32[192,128]{1,0:T(8,128)} %message.1.mine) | copy-start | bytes 294916
  29.2 17.2 %collective-permute-start.7 = (f32[56,256]{1,0:T(8,128)S(1)}, f32[56,256]{1,0:T(8,128)S(1)}, u32[]{:S(2)}, u32[]{:S(2)}) collective-permute-start(f32[56,256]{1,0:T(8,128)S(1)} %get-tuple-element.25), channel_id=1, source_target_pairs={{16,32},{48,64},{80,96},{112,128},{144,160},{176,192},{208,224},{2... | collective-permute-start | bytes 172040 | tf_op jit(solution)/shard_map/ppermute | solution.py:514
  44.4 4.9 %collective-permute-start.8 = (f32[56,256]{1,0:T(8,128)S(1)}, f32[56,256]{1,0:T(8,128)S(1)}, u32[]{:S(2)}, u32[]{:S(2)}) collective-permute-start(f32[56,256]{1,0:T(8,128)S(1)} %get-tuple-element.26), channel_id=1, source_target_pairs={{0,16},{32,48},{64,80},{96,112},{128,144},{160,176},{192,208},{224... | collective-permute-start | bytes 172040 | tf_op jit(solution)/shard_map/ppermute | solution.py:514

commit v9 on v8

--- a/solution.py
+++ b/solution.py
@@ -255,8 +255,9 @@
 SLIM = 6
 
 
-def edges_kernel(ef, hf, ea, ha, coef, mirror_coef, theirs, y_far, y_near,
+def edges_kernel(bulk_far, ef, hf, ea, ha, coef, mirror_coef, theirs, y_far, y_near,
                  tops, ends, mirror, x_far, x_near, x_up, x_down):
+    del bulk_far
     nx, ny = coef.shape[0], coef.shape[1]
     fields = ((ef, hf), (ea, ha))
     tops[...] = jnp.zeros_like(tops)
@@ -543,14 +544,14 @@
     y_shape = shape(2 * (13 * nx) + 8, nz)
     coef, mirror_coef, y_far, y_near = call(
         coef_kernel, [block, shape(ny, LANES), y_shape, y_shape], [*bulk_lower, eps_back, mine, theirs] + fields,
-        [lines, lines, square], name="coefficient")
+        [lines, lines, square], name="coefficient", work=1_000_000_000)
     y_far, y_near = swapped(y_far, y_near, "gy")
     x_shape = shape(FIXED + 4 + ny, nz)
     tile = shape(13 * nx, 8, nz)
     tops, ends, mirror, x_far, x_near = call(
         edges_kernel, [tile, tile, shape(4, FRAME, LANES), x_shape, x_shape],
-        fields + [coef, mirror_coef, theirs, y_far, y_near],
-        [vmem(*x_shape.shape)] * 2, name="edges", work=1_000_000_000)
+        [bulk_upper[0], *fields, coef, mirror_coef, theirs, y_far, y_near],
+        [vmem(*x_shape.shape)] * 2, name="edges", work=4_000_000_000)
     x_far, x_near = swapped(x_far, x_near, "gx")
     ef, hf, ea, ha, grad = call(
         step_kernel, [shape(*e_fwd.shape)] * 4 + [shape(*density.shape)],

time: 53.6 us -> 51.9 us (0.968)
  the two profiles are of different devices: /device:TPU:239 before, /device:TPU:74 now
where the time goes in v9:
time: 51.9 us; the launch traced here: 51.6 us
  starting transfers between devices  29.1 us (56%)
  waiting for transfers between devices  12.4 us (24%)
  Pallas kernels  8.24 us (16%)
  local copies, waits for them, and re-layouts  0.91 us (2%)
  between operations  0.84 us (2%)
    ppermute x4, starting transfers between devices, swapped(): lax.ppermute(far, axis, pairs(1))  15.2 us
    pallas_call x5, Pallas kernels, call(): pl.pallas_call(kernel, out_shape=outs, in_specs=[pl.BlockSpec(memory_spac...  8.24 us
    ppermute x1, starting transfers between devices, mirrored(): return lax.ppermute(block, axis, [(i, size - 1 - i) for i in range(size)])  6.99 us
    ppermute x4, starting transfers between devices, swapped(): lax.ppermute(near, axis, pairs(0))  6.95 us
    ppermute x4, waiting for transfers between devices, swapped(): lax.ppermute(near, axis, pairs(0))  5.75 us
    ppermute x1, waiting for transfers between devices, mirrored(): return lax.ppermute(block, axis, [(i, size - 1 - i) for i in range(size)])  4.58 us
    ppermute x4, waiting for transfers between devices, swapped(): lax.ppermute(far, axis, pairs(1))  2.11 us
  transfers between devices with their start and end apart: 9, of which 5 were waited for; matrix products, arithmetic and copies ran while one was open for 0% of the time, Pallas kernels for 2%

profile of v9, /device:TPU:74, one launch (start us, length us, event | category | flops | bytes accessed | tf_op | source)
XLA Modules:
  0.0 51.6 jit_solution(6172337172035940076)
XLA Ops:
  0.6 0.0 copy-start.3
  0.6 0.0 copy-start.2
  0.7 0.0 copy-start.1
  0.7 0.0 copy-start
  0.7 0.0 copy-start.6
  0.7 2.7 %message.1.mine = f32[192,128]{1,0:T(8,128)} custom-call(f32[3,4,32,256]{3,2,1,0:T(8,128)} %ef_in.1, f32[3,4,32,256]{3,2,1,0:T(8,128)} %hf_in.1, f32[3,4,32,256]{3,2,1,0:T(8,128)} %ea_in.1, f32[3,4,32,256]{3,2,1,0:T(8,128)} %ha_in.1, f32[4,32,256]{2,1,0:T(8,128)} %eps.5, f32[4,4,32]{2,1,0:T(4,128)} %density.1, s32[4,4,32]{2,1,0:T(4,128)} %mask.1, ...), custom_call_target="tpu_custom_call" | custom-call | flops 4000000 | bytes 4000000 | tf_op jit(solution)/shard_map/message/pallas_call | solution.py:496
  3.4 0.0 copy-done.3
  3.5 0.0 copy-done.2
  3.5 0.0 copy-done.1
  3.5 0.0 copy-done
  3.5 0.0 copy-done.6
  3.5 0.0 copy-start.4
  3.5 0.9 %copy-done.4 = f32[192,128]{1,0:T(8,128)S(1)} copy-done((f32[192,128]{1,0:T(8,128)S(1)}, f32[192,128]{1,0:T(8,128)}, u32[]{:S(2)}) %copy-start.4) | copy-done | bytes 98328
  4.4 0.4 bulk.1
  4.8 3.7 %collective-permute-start = (f32[288,256]{1,0:T(8,128)S(1)}, f32[288,256]{1,0:T(8,128)S(1)}, u32[]{:S(2)}, u32[]{:S(2)}) collective-permute-start(f32[288,256]{1,0:T(8,128)S(1)} %get-tuple-element.16), channel_id=1, source_target_pairs={{16,32},{48,64},{80,96},{112,128},{144,160},{176,192},{208,224},{3... | collective-permute-start | bytes 884744 | tf_op jit(solution)/shard_map/ppermute | solution.py:515
  8.5 1.9 %collective-permute-start.1 = (f32[288,256]{1,0:T(8,128)S(1)}, f32[288,256]{1,0:T(8,128)S(1)}, u32[]{:S(2)}, u32[]{:S(2)}) collective-permute-start(f32[288,256]{1,0:T(8,128)S(1)} %get-tuple-element.17), channel_id=1, source_target_pairs={{0,16},{32,48},{64,80},{96,112},{128,144},{160,176},{192,208},{16,... | collective-permute-start | bytes 884744 | tf_op jit(solution)/shard_map/ppermute | solution.py:515
  10.4 7.0 %collective-permute-start.2 = (f32[192,128]{1,0:T(8,128)S(1)}, f32[192,128]{1,0:T(8,128)S(1)}, u32[]{:S(2)}, u32[]{:S(2)}) collective-permute-start(f32[192,128]{1,0:T(8,128)S(1)} %copy-done.4), channel_id=1, source_target_pairs={{0,496},{16,480},{32,464},{48,448},{64,432},{80,416},{96,400},{112... | collective-permute-start | bytes 294920 | tf_op jit(solution)/shard_map/ppermute | solution.py:520
  17.4 0.7 %collective-permute-start.3 = (f32[288,256]{1,0:T(8,128)S(1)}, f32[288,256]{1,0:T(8,128)S(1)}, u32[]{:S(2)}, u32[]{:S(2)}) collective-permute-start(f32[288,256]{1,0:T(8,128)S(1)} %get-tuple-element.16), channel_id=1, source_target_pairs={{240,256},{272,288},{304,320},{336,352},{368,384},{400,416},{432,4... | collective-permute-start | bytes 884744 | tf_op jit(solution)/shard_map/ppermute | solution.py:515
  18.1 4.6 %collective-permute-done.2.theirs = f32[192,128]{1,0:T(8,128)S(1)} collective-permute-done((f32[192,128]{1,0:T(8,128)S(1)}, f32[192,128]{1,0:T(8,128)S(1)}, u32[]{:S(2)}, u32[]{:S(2)}) %collective-permute-start.2) | collective-permute-done | bytes 98336 | tf_op jit(solution)/shard_map/ppermute | solution.py:520
  22.7 0.0 collective-permute-done.bulk_far.bulk_far_1
  22.7 2.0 %collective-permute-done.1.bulk_near.bulk_near_1 = f32[288,256]{1,0:T(8,128)S(1)} collective-permute-done((f32[288,256]{1,0:T(8,128)S(1)}, f32[288,256]{1,0:T(8,128)S(1)}, u32[]{:S(2)}, u32[]{:S(2)}) %collective-permute-start.1) | collective-permute-done | bytes 294944 | tf_op jit(solution)/shard_map/ppermute | solution.py:515
  24.7 0.5 coefficient.1
  25.2 3.8 %collective-permute-start.4 = (f32[112,256]{1,0:T(8,128)S(1)}, f32[112,256]{1,0:T(8,128)S(1)}, u32[]{:S(2)}, u32[]{:S(2)}) collective-permute-start(f32[112,256]{1,0:T(8,128)S(1)} %get-tuple-element.20), channel_id=1, source_target_pairs={{1,2},{3,4},{5,6},{7,8},{9,10},{11,12},{13,14},{2,1},{4,3},{6,5},{... | collective-permute-start | bytes 344072 | tf_op jit(solution)/shard_map/ppermute | solution.py:515
  29.0 2.4 %collective-permute-start.5 = (f32[112,256]{1,0:T(8,128)S(1)}, f32[112,256]{1,0:T(8,128)S(1)}, u32[]{:S(2)}, u32[]{:S(2)}) collective-permute-start(f32[112,256]{1,0:T(8,128)S(1)} %get-tuple-element.21), channel_id=1, source_target_pairs={{0,1},{2,3},{4,5},{6,7},{8,9},{10,11},{12,13},{14,15},{1,0},{3,2},... | collective-permute-start | bytes 344072 | tf_op jit(solution)/shard_map/ppermute | solution.py:515
  31.4 0.7 %collective-permute-start.6 = (f32[288,256]{1,0:T(8,128)S(1)}, f32[288,256]{1,0:T(8,128)S(1)}, u32[]{:S(2)}, u32[]{:S(2)}) collective-permute-start(f32[288,256]{1,0:T(8,128)S(1)} %get-tuple-element.17), channel_id=1, source_target_pairs={{224,240},{256,272},{288,304},{320,336},{352,368},{384,400},{416,4... | collective-permute-start | bytes 884744 | tf_op jit(solution)/shard_map/ppermute | solution.py:515
  32.1 0.0 collective-permute-done.3.bulk_far.bulk_far_2
  32.1 1.7 %collective-permute-done.4.y_far = f32[112,256]{1,0:T(8,128)S(1)} collective-permute-done((f32[112,256]{1,0:T(8,128)S(1)}, f32[112,256]{1,0:T(8,128)S(1)}, u32[]{:S(2)}, u32[]{:S(2)}) %collective-permute-start.4) | collective-permute-done | bytes 114720 | tf_op jit(solution)/shard_map/ppermute | solution.py:515
  33.8 0.0 collective-permute-done.5.y_near
  33.8 0.0 copy-start.5
  33.8 0.8 %edges.1 = (f32[52,8,256]{2,1,0:T(8,128)S(1)}, f32[52,8,256]{2,1,0:T(8,128)S(1)}, f32[4,48,128]{2,1,0:T(8,128)S(1)}, f32[56,256]{1,0:T(8,128)S(1)}, f32[56,256]{1,0:T(8,128)S(1)}) custom-call(f32[288,256]{1,0:T(8,128)S(1)} %collective-permute-done.3.bulk_far.bulk_far_2, f32[3,4,32,256]{3,2,1,0:T(8,128)S(1)} %copy-done, f32[3,4,32,256]{3,2,1,0:T(8,128)S(1)} %copy-done.1, ...), custom_call_target="tpu_custom_call" | custom-call | flops 4000000000 | bytes 4000000 | tf_op jit(solution)/shard_map/edges/pallas_call | solution.py:496
  34.6 7.0 %collective-permute-start.7 = (f32[56,256]{1,0:T(8,128)S(1)}, f32[56,256]{1,0:T(8,128)S(1)}, u32[]{:S(2)}, u32[]{:S(2)}) collective-permute-start(f32[56,256]{1,0:T(8,128)S(1)} %get-tuple-element.25), channel_id=1, source_target_pairs={{16,32},{48,64},{80,96},{112,128},{144,160},{176,192},{208,224},{2... | collective-permute-start | bytes 172040 | tf_op jit(solution)/shard_map/ppermute | solution.py:515
  41.6 1.9 %collective-permute-start.8 = (f32[56,256]{1,0:T(8,128)S(1)}, f32[56,256]{1,0:T(8,128)S(1)}, u32[]{:S(2)}, u32[]{:S(2)}) collective-permute-start(f32[56,256]{1,0:T(8,128)S(1)} %get-tuple-element.26), channel_id=1, source_target_pairs={{0,16},{32,48},{64,80},{96,112},{128,144},{160,176},{192,208},{224... | collective-permute-start | bytes 172040 | tf_op jit(solution)/shard_map/ppermute | solution.py:515
  43.5 0.0 collective-permute-done.6.bulk_near_2
  43.5 0.4 collective-permute-done.7.x_far
  44.0 3.7 %collective-permute-done.8.x_near = f32[56,256]{1,0:T(8,128)S(1)} collective-permute-done((f32[56,256]{1,0:T(8,128)S(1)}, f32[56,256]{1,0:T(8,128)S(1)}, u32[]{:S(2)}, u32[]{:S(2)}) %collective-permute-start.8) | collective-permute-done | bytes 57376 | tf_op jit(solution)/shard_map/ppermute | solution.py:515
  47.7 0.0 copy-done.5
  47.7 3.9 %steps.1 = (f32[3,4,32,256]{3,2,1,0:T(8,128)}, f32[3,4,32,256]{3,2,1,0:T(8,128)}, f32[3,4,32,256]{3,2,1,0:T(8,128)}, f32[3,4,32,256]{3,2,1,0:T(8,128)}, f32[4,4,32]{2,1,0:T(4,128)}) custom-call(f32[3,4,32,256]{3,2,1,0:T(8,128)S(1)} %copy-done, f32[3,4,32,256]{3,2,1,0:T(8,128)S(1)} %copy-done.1, f32[3,4,32,256]{3,2,1,0:T(8,128)S(1)} %copy-done.2, ...), custom_call_target="tpu_custom_call" | custom-call | flops 4000000 | bytes 4000000 | tf_op jit(solution)/shard_map/steps/pallas_call | solution.py:496
Async XLA Ops:
  0.6 2.8 %copy-start.3 = (f32[3,4,32,256]{3,2,1,0:T(8,128)S(1)}, f32[3,4,32,256]{3,2,1,0:T(8,128)}, u32[]{:S(2)}) copy-start(f32[3,4,32,256]{3,2,1,0:T(8,128)} %ha_in.1) | copy-start | bytes 1179652
  0.6 2.8 %copy-start.2 = (f32[3,4,32,256]{3,2,1,0:T(8,128)S(1)}, f32[3,4,32,256]{3,2,1,0:T(8,128)}, u32[]{:S(2)}) copy-start(f32[3,4,32,256]{3,2,1,0:T(8,128)} %ea_in.1) | copy-start | bytes 1179652
  0.7 2.8 %copy-start.1 = (f32[3,4,32,256]{3,2,1,0:T(8,128)S(1)}, f32[3,4,32,256]{3,2,1,0:T(8,128)}, u32[]{:S(2)}) copy-start(f32[3,4,32,256]{3,2,1,0:T(8,128)} %hf_in.1) | copy-start | bytes 1179652
  0.7 2.8 %copy-start = (f32[3,4,32,256]{3,2,1,0:T(8,128)S(1)}, f32[3,4,32,256]{3,2,1,0:T(8,128)}, u32[]{:S(2)}) copy-start(f32[3,4,32,256]{3,2,1,0:T(8,128)} %ef_in.1) | copy-start | bytes 1179652
  0.7 2.8 %copy-start.6 = (f32[4,32,256]{2,1,0:T(8,128)S(1)}, f32[4,32,256]{2,1,0:T(8,128)}, u32[]{:S(2)}) copy-start(f32[4,32,256]{2,1,0:T(8,128)} %eps.5) | copy-start | bytes 393220
  3.5 0.9 %copy-start.4 = (f32[192,128]{1,0:T(8,128)S(1)}, f32[192,128]{1,0:T(8,128)}, u32[]{:S(2)}) copy-start(f32[192,128]{1,0:T(8,128)} %message.1.mine) | copy-start | bytes 294916
  4.8 17.9 %collective-permute-start = (f32[288,256]{1,0:T(8,128)S(1)}, f32[288,256]{1,0:T(8,128)S(1)}, u32[]{:S(2)}, u32[]{:S(2)}) collective-permute-start(f32[288,256]{1,0:T(8,128)S(1)} %get-tuple-element.16), channel_id=1, source_target_pairs={{16,32},{48,64},{80,96},{112,128},{144,160},{176,192},{208,224},{3... | collective-permute-start | bytes 884744 | tf_op jit(solution)/shard_map/ppermute | solution.py:515
  8.5 16.2 %collective-permute-start.1 = (f32[288,256]{1,0:T(8,128)S(1)}, f32[288,256]{1,0:T(8,128)S(1)}, u32[]{:S(2)}, u32[]{:S(2)}) collective-permute-start(f32[288,256]{1,0:T(8,128)S(1)} %get-tuple-element.17), channel_id=1, source_target_pairs={{0,16},{32,48},{64,80},{96,112},{128,144},{160,176},{192,208},{16,... | collective-permute-start | bytes 884744 | tf_op jit(solution)/shard_map/ppermute | solution.py:515
  10.4 12.3 %collective-permute-start.2 = (f32[192,128]{1,0:T(8,128)S(1)}, f32[192,128]{1,0:T(8,128)S(1)}, u32[]{:S(2)}, u32[]{:S(2)}) collective-permute-start(f32[192,128]{1,0:T(8,128)S(1)} %copy-done.4), channel_id=1, source_target_pairs={{0,496},{16,480},{32,464},{48,448},{64,432},{80,416},{96,400},{112... | collective-permute-start | bytes 294920 | tf_op jit(solution)/shard_map/ppermute | solution.py:520
  17.4 14.7 %collective-permute-start.3 = (f32[288,256]{1,0:T(8,128)S(1)}, f32[288,256]{1,0:T(8,128)S(1)}, u32[]{:S(2)}, u32[]{:S(2)}) collective-permute-start(f32[288,256]{1,0:T(8,128)S(1)} %get-tuple-element.16), channel_id=1, source_target_pairs={{240,256},{272,288},{304,320},{336,352},{368,384},{400,416},{432,4... | collective-permute-start | bytes 884744 | tf_op jit(solution)/shard_map/ppermute | solution.py:515
  25.2 8.6 %collective-permute-start.4 = (f32[112,256]{1,0:T(8,128)S(1)}, f32[112,256]{1,0:T(8,128)S(1)}, u32[]{:S(2)}, u32[]{:S(2)}) collective-permute-start(f32[112,256]{1,0:T(8,128)S(1)} %get-tuple-element.20), channel_id=1, source_target_pairs={{1,2},{3,4},{5,6},{7,8},{9,10},{11,12},{13,14},{2,1},{4,3},{6,5},{... | collective-permute-start | bytes 344072 | tf_op jit(solution)/shard_map/ppermute | solution.py:515
  29.0 4.8 %collective-permute-start.5 = (f32[112,256]{1,0:T(8,128)S(1)}, f32[112,256]{1,0:T(8,128)S(1)}, u32[]{:S(2)}, u32[]{:S(2)}) collective-permute-start(f32[112,256]{1,0:T(8,128)S(1)} %get-tuple-element.21), channel_id=1, source_target_pairs={{0,1},{2,3},{4,5},{6,7},{8,9},{10,11},{12,13},{14,15},{1,0},{3,2},... | collective-permute-start | bytes 344072 | tf_op jit(solution)/shard_map/ppermute | solution.py:515
  31.4 12.1 %collective-permute-start.6 = (f32[288,256]{1,0:T(8,128)S(1)}, f32[288,256]{1,0:T(8,128)S(1)}, u32[]{:S(2)}, u32[]{:S(2)}) collective-permute-start(f32[288,256]{1,0:T(8,128)S(1)} %get-tuple-element.17), channel_id=1, source_target_pairs={{224,240},{256,272},{288,304},{320,336},{352,368},{384,400},{416,4... | collective-permute-start | bytes 884744 | tf_op jit(solution)/shard_map/ppermute | solution.py:515
  33.8 13.9 %copy-start.5 = (f32[192,128]{1,0:T(8,128)S(1)}, f32[192,128]{1,0:T(8,128)}, u32[]{:S(2)}) copy-start(f32[192,128]{1,0:T(8,128)} %message.1.mine) | copy-start | bytes 294916
  34.6 9.4 %collective-permute-start.7 = (f32[56,256]{1,0:T(8,128)S(1)}, f32[56,256]{1,0:T(8,128)S(1)}, u32[]{:S(2)}, u32[]{:S(2)}) collective-permute-start(f32[56,256]{1,0:T(8,128)S(1)} %get-tuple-element.25), channel_id=1, source_target_pairs={{16,32},{48,64},{80,96},{112,128},{144,160},{176,192},{208,224},{2... | collective-permute-start | bytes 172040 | tf_op jit(solution)/shard_map/ppermute | solution.py:515
  41.6 6.1 %collective-permute-start.8 = (f32[56,256]{1,0:T(8,128)S(1)}, f32[56,256]{1,0:T(8,128)S(1)}, u32[]{:S(2)}, u32[]{:S(2)}) collective-permute-start(f32[56,256]{1,0:T(8,128)S(1)} %get-tuple-element.26), channel_id=1, source_target_pairs={{0,16},{32,48},{64,80},{96,112},{128,144},{160,176},{192,208},{224... | collective-permute-start | bytes 172040 | tf_op jit(solution)/shard_map/ppermute | solution.py:515

commit v10 on v9

--- a/solution.py
+++ b/solution.py
@@ -333,7 +333,34 @@
             out[pl.ds(p * nx + x, 1), :] = square[pl.ds(x * 16 + 2 + p, 1), :]
 
 
-def step_kernel(ef_in, hf_in, ea_in, ha_in, coef, tops, ends, mirror, bulk_far_1, bulk_near_1, bulk_far_2, bulk_near_2,
+def first_kernel(ef, hf, ea, ha, coef, tops, ends, first_h, first_e):
+    nx = coef.shape[0]
+    fields = ((ef, hf), (ea, ha))
+
+    def part(f, k, c, x):
+        return framed(fields[f][k][c, x], tops, ends, plane_index(f, k, c, x, nx))
+
+    for f in range(2):
+        for x in range(nx):
+            inside = framed(coef[x], tops, ends, 12 * nx + x) > 0
+            ex, ey, ez = part(f, 0, 0, x), part(f, 0, 1, x), part(f, 0, 2, x)
+            ey_n = part(f, 0, 1, x + 1) if x + 1 < nx else 0.0
+            ez_n = part(f, 0, 2, x + 1) if x + 1 < nx else 0.0
+            hx, hy, hz = part(f, 1, 0, x), part(f, 1, 1, x), part(f, 1, 2, x)
+            first_h[f, 0, x] = jnp.where(inside, hx - COURANT * ((up_y(ez) - ez) - (up_z(ey) - ey)), 0.0)
+            first_h[f, 1, x] = jnp.where(inside, hy - COURANT * ((up_z(ex) - ex) - (ez_n - ez)), 0.0)
+            first_h[f, 2, x] = jnp.where(inside, hz - COURANT * ((ey_n - ey) - (up_y(ex) - ex)), 0.0)
+        for x in range(nx):
+            k = framed(coef[x], tops, ends, 12 * nx + x)
+            hx, hy, hz = first_h[f, 0, x], first_h[f, 1, x], first_h[f, 2, x]
+            hy_p = first_h[f, 1, x - 1] if x else 0.0
+            hz_p = first_h[f, 2, x - 1] if x else 0.0
+            first_e[f, 0, x] = part(f, 0, 0, x) + k * ((hz - down_y(hz)) - (hy - down_z(hy)))
+            first_e[f, 1, x] = part(f, 0, 1, x) + k * ((hx - down_z(hx)) - (hz - hz_p))
+            first_e[f, 2, x] = part(f, 0, 2, x) + k * ((hy - hy_p) - (hx - down_y(hx)))
+
+
+def step_kernel(ef_in, hf_in, ea_in, ha_in, coef, first_h, first_e, tops, ends, mirror, bulk_far_1, bulk_near_1, bulk_far_2, bulk_near_2,
                 x_far, x_near, mine, theirs,
                 ef_out, hf_out, ea_out, ha_out, grad,
                 ee, hh, halo, square, table, lines, sems):
@@ -382,6 +409,13 @@
     def inverse(x):
         return framed(coef[x], tops, ends, 12 * nx + x)
 
+    def e1(f, c, x):
+        edge = x >= nx - 1 or (x == 0 and c)
+        return ee[f, c, x] if edge else first_e[f, c, x]
+
+    def h1(f, c, x):
+        return hh[f, c, nx] if x == nx - 1 and c else first_h[f, c, x]
+
     copies = []
     first_slab, second_slab = [], []
     for f in range(2):
@@ -390,21 +424,19 @@
         dhz = jnp.where(k_low > 0, -COURANT * ey0, 0.0)
         hh[f, 1, 0] = halo[4 * f] + dhy
         hh[f, 2, 0] = halo[4 * f + 1] + dhz
-        for x in range(nx):
-            inside = inverse(x) > 0
-            ex, ey, ez = part(f, 0, 0, x), part(f, 0, 1, x), part(f, 0, 2, x)
-            ey_n = part(f, 0, 1, x + 1) if x + 1 < nx else halo[10 + 4 * f]
-            ez_n = part(f, 0, 2, x + 1) if x + 1 < nx else halo[10 + 4 * f + 1]
-            hx, hy, hz = part(f, 1, 0, x), part(f, 1, 1, x), part(f, 1, 2, x)
-            hh[f, 0, x + 1] = jnp.where(inside, hx - COURANT * ((up_y(ez) - ez) - (up_z(ey) - ey)), 0.0)
-            hh[f, 1, x + 1] = jnp.where(inside, hy - COURANT * ((up_z(ex) - ex) - (ez_n - ez)), 0.0)
-            hh[f, 2, x + 1] = jnp.where(inside, hz - COURANT * ((ey_n - ey) - (up_y(ex) - ex)), 0.0)
-        for x in range(nx):
-            k = inverse(x)
-            hx, hy, hz = hh[f, 0, x + 1], hh[f, 1, x + 1], hh[f, 2, x + 1]
-            ee[f, 0, x] = part(f, 0, 0, x) + k * ((hz - down_y(hz)) - (hy - down_z(hy)))
-            ee[f, 1, x] = part(f, 0, 1, x) + k * ((hx - down_z(hx)) - (hz - hh[f, 2, x]))
-            ee[f, 2, x] = part(f, 0, 2, x) + k * ((hy - hh[f, 1, x]) - (hx - down_y(hx)))
+        last = nx - 1
+        k = inverse(last)
+        inside = k > 0
+        dy = jnp.where(inside, COURANT * halo[10 + 4 * f + 1], 0.0)
+        dz = jnp.where(inside, -COURANT * halo[10 + 4 * f], 0.0)
+        hh[f, 1, nx] = first_h[f, 1, last] + dy
+        hh[f, 2, nx] = first_h[f, 2, last] + dz
+        ee[f, 0, last] = first_e[f, 0, last] + k * ((dz - down_y(dz)) - (dy - down_z(dy)))
+        ee[f, 1, last] = first_e[f, 1, last] - k * dz
+        ee[f, 2, last] = first_e[f, 2, last] + k * dy
+        k = inverse(0)
+        ee[f, 1, 0] = first_e[f, 1, 0] + k * hh[f, 2, 0]
+        ee[f, 2, 0] = first_e[f, 2, 0] - k * hh[f, 1, 0]
         ee[f, 1, nx] = halo[10 + 4 * f + 2] + k_high * hh[f, 2, nx]
         ee[f, 2, nx] = halo[10 + 4 * f + 3] - k_high * hh[f, 1, nx]
         dex = k_low * ((dhz - down_y(dhz)) - (dhy - down_z(dhy)))
@@ -416,26 +448,26 @@
             k_low > 0, halo[4 * f + 3] + dhz - COURANT * ((ee[f, 1, 0] - dey) - (up_y(dex) - dex)), 0.0)
         for x in range(nx):
             inside = inverse(x) > 0
-            ex, ey, ez = ee[f, 0, x], ee[f, 1, x], ee[f, 2, x]
+            ex, ey, ez = e1(f, 0, x), e1(f, 1, x), e1(f, 2, x)
             hh[f, 0, x + 1] = jnp.where(
-                inside, hh[f, 0, x + 1] - COURANT * ((up_y(ez) - ez) - (up_z(ey) - ey)), 0.0)
+                inside, h1(f, 0, x) - COURANT * ((up_y(ez) - ez) - (up_z(ey) - ey)), 0.0)
             hh[f, 1, x + 1] = jnp.where(
-                inside, hh[f, 1, x + 1] - COURANT * ((up_z(ex) - ex) - (ee[f, 2, x + 1] - ez)), 0.0)
+                inside, h1(f, 1, x) - COURANT * ((up_z(ex) - ex) - (e1(f, 2, x + 1) - ez)), 0.0)
             hh[f, 2, x + 1] = jnp.where(
-                inside, hh[f, 2, x + 1] - COURANT * ((ee[f, 1, x + 1] - ey) - (up_y(ex) - ex)), 0.0)
+                inside, h1(f, 2, x) - COURANT * ((e1(f, 1, x + 1) - ey) - (up_y(ex) - ex)), 0.0)
         copies.append(pltpu.make_async_copy(
             hh.at[f, :, pl.ds(1, nx), pl.ds(TOP, ny), :], (hf_out, ha_out)[f], sems.at[2 * f]))
         copies[-1].start()
     for c in range(3):
-        first_slab.append(pack_planes([(x * 16 + f * 8, ee[f, c, x, pl.ds(TOP, ny), :])
+        first_slab.append(pack_planes([(x * 16 + f * 8, e1(f, c, x)[TOP:END])
                                        for x in range(nx) for f in range(2)]))
     for f in range(2):
         for x in range(nx):
             k = inverse(x)
             hx, hy, hz = hh[f, 0, x + 1], hh[f, 1, x + 1], hh[f, 2, x + 1]
-            ee[f, 0, x] = ee[f, 0, x] + k * ((hz - down_y(hz)) - (hy - down_z(hy)))
-            ee[f, 1, x] = ee[f, 1, x] + k * ((hx - down_z(hx)) - (hz - hh[f, 2, x]))
-            ee[f, 2, x] = ee[f, 2, x] + k * ((hy - hh[f, 1, x]) - (hx - down_y(hx)))
+            ee[f, 0, x] = e1(f, 0, x) + k * ((hz - down_y(hz)) - (hy - down_z(hy)))
+            ee[f, 1, x] = e1(f, 1, x) + k * ((hx - down_z(hx)) - (hz - hh[f, 2, x]))
+            ee[f, 2, x] = e1(f, 2, x) + k * ((hy - hh[f, 1, x]) - (hx - down_y(hx)))
         copies.append(pltpu.make_async_copy(
             ee.at[f, :, pl.ds(0, nx), pl.ds(TOP, ny), :], (ef_out, ea_out)[f], sems.at[2 * f + 1]))
         copies[-1].start()
@@ -553,9 +585,11 @@
         [bulk_upper[0], *fields, coef, mirror_coef, theirs, y_far, y_near],
         [vmem(*x_shape.shape)] * 2, name="edges", work=4_000_000_000)
     x_far, x_near = swapped(x_far, x_near, "gx")
+    step = shape(2, 3, nx, FRAME, nz)
+    first_h, first_e = call(first_kernel, [step, step], [*fields, coef, tops, ends], name="first")
     ef, hf, ea, ha, grad = call(
         step_kernel, [shape(*e_fwd.shape)] * 4 + [shape(*density.shape)],
-        fields + [coef, tops, ends, mirror, *bulk_lower, *bulk_upper, x_far, x_near, mine, theirs],
+        fields + [coef, first_h, first_e, tops, ends, mirror, *bulk_lower, *bulk_upper, x_far, x_near, mine, theirs],
         [vmem(2, 3, nx + 1, FRAME, nz), vmem(2, 3, nx + 1, FRAME, nz), vmem(20, FRAME, nz),
          square, lines, lines, pltpu.SemaphoreType.DMA((4,))], name="steps", any_out=4)
     return ef, hf, ea, ha, grad

time: 51.9 us -> 51.3 us (0.988)
  waiting for transfers between devices: 12.4 us -> 11.7 us
    pallas_call x5 -> x6, Pallas kernels: 8.24 us -> 8.3 us  [call(): pl.pallas_call(kernel, out_shape=outs, in_specs=[pl.BlockSpec(memory_spac...]
  transfers between devices with their start and end apart: 9 -> 9, of which waited for: 5 -> 4; matrix products, arithmetic and copies ran while one was open for 0% -> 0% of each run, Pallas kernels for 2% -> 4%
where the time goes in v10:
time: 51.3 us; the launch traced here: 50.9 us
  starting transfers between devices  29.1 us (57%)
  waiting for transfers between devices  11.7 us (23%)
  Pallas kernels  8.3 us (16%)
  local copies, waits for them, and re-layouts  0.92 us (2%)
  between operations  0.86 us (2%)
    ppermute x4, starting transfers between devices, swapped(): lax.ppermute(far, axis, pairs(1))  15.2 us
    pallas_call x6, Pallas kernels, call(): pl.pallas_call(kernel, out_shape=outs, in_specs=[pl.BlockSpec(memory_spac...  8.3 us
    ppermute x1, starting transfers between devices, mirrored(): return lax.ppermute(block, axis, [(i, size - 1 - i) for i in range(size)])  6.99 us
    ppermute x4, starting transfers between devices, swapped(): lax.ppermute(near, axis, pairs(0))  6.95 us
    ppermute x4, waiting for transfers between devices, swapped(): lax.ppermute(near, axis, pairs(0))  5.45 us
    ppermute x1, waiting for transfers between devices, mirrored(): return lax.ppermute(block, axis, [(i, size - 1 - i) for i in range(size)])  4.58 us
    ppermute x4, waiting for transfers between devices, swapped(): lax.ppermute(far, axis, pairs(1))  1.68 us
  transfers between devices with their start and end apart: 9, of which 4 were waited for; matrix products, arithmetic and copies ran while one was open for 0% of the time, Pallas kernels for 4%

profile of v10, /device:TPU:74, one launch (start us, length us, event | category | flops | bytes accessed | tf_op | source)
XLA Modules:
  0.0 50.9 jit_solution(11130025243897705278)
XLA Ops:
  0.6 0.0 copy-start.3
  0.6 0.0 copy-start.2
  0.7 0.0 copy-start.1
  0.7 0.0 copy-start
  0.7 0.0 copy-start.6
  0.7 2.7 %message.1.mine = f32[192,128]{1,0:T(8,128)} custom-call(f32[3,4,32,256]{3,2,1,0:T(8,128)} %ef_in.1, f32[3,4,32,256]{3,2,1,0:T(8,128)} %hf_in.1, f32[3,4,32,256]{3,2,1,0:T(8,128)} %ea_in.1, f32[3,4,32,256]{3,2,1,0:T(8,128)} %ha_in.1, f32[4,32,256]{2,1,0:T(8,128)} %eps.5, f32[4,4,32]{2,1,0:T(4,128)} %density.1, s32[4,4,32]{2,1,0:T(4,128)} %mask.1, ...), custom_call_target="tpu_custom_call" | custom-call | flops 4000000 | bytes 4000000 | tf_op jit(solution)/shard_map/message/pallas_call | solution.py:528
  3.4 0.0 copy-done.3
  3.5 0.0 copy-done.2
  3.5 0.0 copy-done.1
  3.5 0.0 copy-done
  3.5 0.0 copy-done.6
  3.5 0.0 copy-start.4
  3.5 0.9 %copy-done.4 = f32[192,128]{1,0:T(8,128)S(1)} copy-done((f32[192,128]{1,0:T(8,128)S(1)}, f32[192,128]{1,0:T(8,128)}, u32[]{:S(2)}) %copy-start.4) | copy-done | bytes 98328
  4.4 0.4 bulk.1
  4.8 3.7 %collective-permute-start = (f32[288,256]{1,0:T(8,128)S(1)}, f32[288,256]{1,0:T(8,128)S(1)}, u32[]{:S(2)}, u32[]{:S(2)}) collective-permute-start(f32[288,256]{1,0:T(8,128)S(1)} %get-tuple-element.18), channel_id=1, source_target_pairs={{16,32},{48,64},{80,96},{112,128},{144,160},{176,192},{208,224},{3... | collective-permute-start | bytes 884744 | tf_op jit(solution)/shard_map/ppermute | solution.py:547
  8.5 1.9 %collective-permute-start.1 = (f32[288,256]{1,0:T(8,128)S(1)}, f32[288,256]{1,0:T(8,128)S(1)}, u32[]{:S(2)}, u32[]{:S(2)}) collective-permute-start(f32[288,256]{1,0:T(8,128)S(1)} %get-tuple-element.19), channel_id=1, source_target_pairs={{0,16},{32,48},{64,80},{96,112},{128,144},{160,176},{192,208},{16,... | collective-permute-start | bytes 884744 | tf_op jit(solution)/shard_map/ppermute | solution.py:547
  10.4 7.0 %collective-permute-start.2 = (f32[192,128]{1,0:T(8,128)S(1)}, f32[192,128]{1,0:T(8,128)S(1)}, u32[]{:S(2)}, u32[]{:S(2)}) collective-permute-start(f32[192,128]{1,0:T(8,128)S(1)} %copy-done.4), channel_id=1, source_target_pairs={{0,496},{16,480},{32,464},{48,448},{64,432},{80,416},{96,400},{112... | collective-permute-start | bytes 294920 | tf_op jit(solution)/shard_map/ppermute | solution.py:552
  17.4 0.7 %collective-permute-start.3 = (f32[288,256]{1,0:T(8,128)S(1)}, f32[288,256]{1,0:T(8,128)S(1)}, u32[]{:S(2)}, u32[]{:S(2)}) collective-permute-start(f32[288,256]{1,0:T(8,128)S(1)} %get-tuple-element.18), channel_id=1, source_target_pairs={{240,256},{272,288},{304,320},{336,352},{368,384},{400,416},{432,4... | collective-permute-start | bytes 884744 | tf_op jit(solution)/shard_map/ppermute | solution.py:547
  18.1 4.6 %collective-permute-done.2.theirs = f32[192,128]{1,0:T(8,128)S(1)} collective-permute-done((f32[192,128]{1,0:T(8,128)S(1)}, f32[192,128]{1,0:T(8,128)S(1)}, u32[]{:S(2)}, u32[]{:S(2)}) %collective-permute-start.2) | collective-permute-done | bytes 98336 | tf_op jit(solution)/shard_map/ppermute | solution.py:552
  22.7 0.0 collective-permute-done.bulk_far.bulk_far_1
  22.7 2.0 %collective-permute-done.1.bulk_near.bulk_near_1 = f32[288,256]{1,0:T(8,128)S(1)} collective-permute-done((f32[288,256]{1,0:T(8,128)S(1)}, f32[288,256]{1,0:T(8,128)S(1)}, u32[]{:S(2)}, u32[]{:S(2)}) %collective-permute-start.1) | collective-permute-done | bytes 294944 | tf_op jit(solution)/shard_map/ppermute | solution.py:547
  24.7 0.5 coefficient.1
  25.2 3.8 %collective-permute-start.4 = (f32[112,256]{1,0:T(8,128)S(1)}, f32[112,256]{1,0:T(8,128)S(1)}, u32[]{:S(2)}, u32[]{:S(2)}) collective-permute-start(f32[112,256]{1,0:T(8,128)S(1)} %get-tuple-element.22), channel_id=1, source_target_pairs={{1,2},{3,4},{5,6},{7,8},{9,10},{11,12},{13,14},{2,1},{4,3},{6,5},{... | collective-permute-start | bytes 344072 | tf_op jit(solution)/shard_map/ppermute | solution.py:547
  29.0 2.4 %collective-permute-start.5 = (f32[112,256]{1,0:T(8,128)S(1)}, f32[112,256]{1,0:T(8,128)S(1)}, u32[]{:S(2)}, u32[]{:S(2)}) collective-permute-start(f32[112,256]{1,0:T(8,128)S(1)} %get-tuple-element.23), channel_id=1, source_target_pairs={{0,1},{2,3},{4,5},{6,7},{8,9},{10,11},{12,13},{14,15},{1,0},{3,2},... | collective-permute-start | bytes 344072 | tf_op jit(solution)/shard_map/ppermute | solution.py:547
  31.4 0.7 %collective-permute-start.6 = (f32[288,256]{1,0:T(8,128)S(1)}, f32[288,256]{1,0:T(8,128)S(1)}, u32[]{:S(2)}, u32[]{:S(2)}) collective-permute-start(f32[288,256]{1,0:T(8,128)S(1)} %get-tuple-element.19), channel_id=1, source_target_pairs={{224,240},{256,272},{288,304},{320,336},{352,368},{384,400},{416,4... | collective-permute-start | bytes 884744 | tf_op jit(solution)/shard_map/ppermute | solution.py:547
  32.1 0.0 collective-permute-done.3.bulk_far.bulk_far_2
  32.1 1.7 %collective-permute-done.4.y_far = f32[112,256]{1,0:T(8,128)S(1)} collective-permute-done((f32[112,256]{1,0:T(8,128)S(1)}, f32[112,256]{1,0:T(8,128)S(1)}, u32[]{:S(2)}, u32[]{:S(2)}) %collective-permute-start.4) | collective-permute-done | bytes 114720 | tf_op jit(solution)/shard_map/ppermute | solution.py:547
  33.8 0.0 collective-permute-done.5.y_near
  33.8 0.8 %edges.1 = (f32[52,8,256]{2,1,0:T(8,128)S(1)}, f32[52,8,256]{2,1,0:T(8,128)S(1)}, f32[4,48,128]{2,1,0:T(8,128)S(1)}, f32[56,256]{1,0:T(8,128)S(1)}, f32[56,256]{1,0:T(8,128)S(1)}) custom-call(f32[288,256]{1,0:T(8,128)S(1)} %collective-permute-done.3.bulk_far.bulk_far_2, f32[3,4,32,256]{3,2,1,0:T(8,128)S(1)} %copy-done, f32[3,4,32,256]{3,2,1,0:T(8,128)S(1)} %copy-done.1, ...), custom_call_target="tpu_custom_call" | custom-call | flops 4000000000 | bytes 4000000 | tf_op jit(solution)/shard_map/edges/pallas_call | solution.py:528
  34.6 7.0 %collective-permute-start.7 = (f32[56,256]{1,0:T(8,128)S(1)}, f32[56,256]{1,0:T(8,128)S(1)}, u32[]{:S(2)}, u32[]{:S(2)}) collective-permute-start(f32[56,256]{1,0:T(8,128)S(1)} %get-tuple-element.29), channel_id=1, source_target_pairs={{16,32},{48,64},{80,96},{112,128},{144,160},{176,192},{208,224},{2... | collective-permute-start | bytes 172040 | tf_op jit(solution)/shard_map/ppermute | solution.py:547
  41.6 1.9 %collective-permute-start.8 = (f32[56,256]{1,0:T(8,128)S(1)}, f32[56,256]{1,0:T(8,128)S(1)}, u32[]{:S(2)}, u32[]{:S(2)}) collective-permute-start(f32[56,256]{1,0:T(8,128)S(1)} %get-tuple-element.30), channel_id=1, source_target_pairs={{0,16},{32,48},{64,80},{96,112},{128,144},{160,176},{192,208},{224... | collective-permute-start | bytes 172040 | tf_op jit(solution)/shard_map/ppermute | solution.py:547
  43.5 0.0 copy-start.5
  43.5 0.7 %first.1 = (f32[2,3,4,48,256]{4,3,2,1,0:T(8,128)S(1)}, f32[2,3,4,48,256]{4,3,2,1,0:T(8,128)S(1)}) custom-call(f32[3,4,32,256]{3,2,1,0:T(8,128)S(1)} %copy-done, f32[3,4,32,256]{3,2,1,0:T(8,128)S(1)} %copy-done.1, f32[3,4,32,256]{3,2,1,0:T(8,128)S(1)} %copy-done.2, f32[3,4,32,256]{3,2,1,0:T(8,128)S(1)} %copy-done.3, ...), custom_call_target="tpu_custom_call" | custom-call | flops 4000000 | bytes 4000000 | tf_op jit(solution)/shard_map/first/pallas_call | solution.py:528
  44.3 0.0 collective-permute-done.6.bulk_near_2
  44.3 0.0 collective-permute-done.7.x_far
  44.3 3.4 %collective-permute-done.8.x_near = f32[56,256]{1,0:T(8,128)S(1)} collective-permute-done((f32[56,256]{1,0:T(8,128)S(1)}, f32[56,256]{1,0:T(8,128)S(1)}, u32[]{:S(2)}, u32[]{:S(2)}) %collective-permute-start.8) | collective-permute-done | bytes 57376 | tf_op jit(solution)/shard_map/ppermute | solution.py:547
  47.7 0.0 copy-done.5
  47.7 3.3 %steps.1 = (f32[3,4,32,256]{3,2,1,0:T(8,128)}, f32[3,4,32,256]{3,2,1,0:T(8,128)}, f32[3,4,32,256]{3,2,1,0:T(8,128)}, f32[3,4,32,256]{3,2,1,0:T(8,128)}, f32[4,4,32]{2,1,0:T(4,128)}) custom-call(f32[3,4,32,256]{3,2,1,0:T(8,128)S(1)} %copy-done, f32[3,4,32,256]{3,2,1,0:T(8,128)S(1)} %copy-done.1, f32[3,4,32,256]{3,2,1,0:T(8,128)S(1)} %copy-done.2, ...), custom_call_target="tpu_custom_call" | custom-call | flops 4000000 | bytes 4000000 | tf_op jit(solution)/shard_map/steps/pallas_call | solution.py:528
Async XLA Ops:
  0.6 2.8 %copy-start.3 = (f32[3,4,32,256]{3,2,1,0:T(8,128)S(1)}, f32[3,4,32,256]{3,2,1,0:T(8,128)}, u32[]{:S(2)}) copy-start(f32[3,4,32,256]{3,2,1,0:T(8,128)} %ha_in.1) | copy-start | bytes 1179652
  0.6 2.8 %copy-start.2 = (f32[3,4,32,256]{3,2,1,0:T(8,128)S(1)}, f32[3,4,32,256]{3,2,1,0:T(8,128)}, u32[]{:S(2)}) copy-start(f32[3,4,32,256]{3,2,1,0:T(8,128)} %ea_in.1) | copy-start | bytes 1179652
  0.7 2.8 %copy-start.1 = (f32[3,4,32,256]{3,2,1,0:T(8,128)S(1)}, f32[3,4,32,256]{3,2,1,0:T(8,128)}, u32[]{:S(2)}) copy-start(f32[3,4,32,256]{3,2,1,0:T(8,128)} %hf_in.1) | copy-start | bytes 1179652
  0.7 2.8 %copy-start = (f32[3,4,32,256]{3,2,1,0:T(8,128)S(1)}, f32[3,4,32,256]{3,2,1,0:T(8,128)}, u32[]{:S(2)}) copy-start(f32[3,4,32,256]{3,2,1,0:T(8,128)} %ef_in.1) | copy-start | bytes 1179652
  0.7 2.8 %copy-start.6 = (f32[4,32,256]{2,1,0:T(8,128)S(1)}, f32[4,32,256]{2,1,0:T(8,128)}, u32[]{:S(2)}) copy-start(f32[4,32,256]{2,1,0:T(8,128)} %eps.5) | copy-start | bytes 393220
  3.5 0.9 %copy-start.4 = (f32[192,128]{1,0:T(8,128)S(1)}, f32[192,128]{1,0:T(8,128)}, u32[]{:S(2)}) copy-start(f32[192,128]{1,0:T(8,128)} %message.1.mine) | copy-start | bytes 294916
  4.8 17.9 %collective-permute-start = (f32[288,256]{1,0:T(8,128)S(1)}, f32[288,256]{1,0:T(8,128)S(1)}, u32[]{:S(2)}, u32[]{:S(2)}) collective-permute-start(f32[288,256]{1,0:T(8,128)S(1)} %get-tuple-element.18), channel_id=1, source_target_pairs={{16,32},{48,64},{80,96},{112,128},{144,160},{176,192},{208,224},{3... | collective-permute-start | bytes 884744 | tf_op jit(solution)/shard_map/ppermute | solution.py:547
  8.5 16.2 %collective-permute-start.1 = (f32[288,256]{1,0:T(8,128)S(1)}, f32[288,256]{1,0:T(8,128)S(1)}, u32[]{:S(2)}, u32[]{:S(2)}) collective-permute-start(f32[288,256]{1,0:T(8,128)S(1)} %get-tuple-element.19), channel_id=1, source_target_pairs={{0,16},{32,48},{64,80},{96,112},{128,144},{160,176},{192,208},{16,... | collective-permute-start | bytes 884744 | tf_op jit(solution)/shard_map/ppermute | solution.py:547
  10.4 12.3 %collective-permute-start.2 = (f32[192,128]{1,0:T(8,128)S(1)}, f32[192,128]{1,0:T(8,128)S(1)}, u32[]{:S(2)}, u32[]{:S(2)}) collective-permute-start(f32[192,128]{1,0:T(8,128)S(1)} %copy-done.4), channel_id=1, source_target_pairs={{0,496},{16,480},{32,464},{48,448},{64,432},{80,416},{96,400},{112... | collective-permute-start | bytes 294920 | tf_op jit(solution)/shard_map/ppermute | solution.py:552
  17.4 14.7 %collective-permute-start.3 = (f32[288,256]{1,0:T(8,128)S(1)}, f32[288,256]{1,0:T(8,128)S(1)}, u32[]{:S(2)}, u32[]{:S(2)}) collective-permute-start(f32[288,256]{1,0:T(8,128)S(1)} %get-tuple-element.18), channel_id=1, source_target_pairs={{240,256},{272,288},{304,320},{336,352},{368,384},{400,416},{432,4... | collective-permute-start | bytes 884744 | tf_op jit(solution)/shard_map/ppermute | solution.py:547
  25.2 8.6 %collective-permute-start.4 = (f32[112,256]{1,0:T(8,128)S(1)}, f32[112,256]{1,0:T(8,128)S(1)}, u32[]{:S(2)}, u32[]{:S(2)}) collective-permute-start(f32[112,256]{1,0:T(8,128)S(1)} %get-tuple-element.22), channel_id=1, source_target_pairs={{1,2},{3,4},{5,6},{7,8},{9,10},{11,12},{13,14},{2,1},{4,3},{6,5},{... | collective-permute-start | bytes 344072 | tf_op jit(solution)/shard_map/ppermute | solution.py:547
  29.0 4.8 %collective-permute-start.5 = (f32[112,256]{1,0:T(8,128)S(1)}, f32[112,256]{1,0:T(8,128)S(1)}, u32[]{:S(2)}, u32[]{:S(2)}) collective-permute-start(f32[112,256]{1,0:T(8,128)S(1)} %get-tuple-element.23), channel_id=1, source_target_pairs={{0,1},{2,3},{4,5},{6,7},{8,9},{10,11},{12,13},{14,15},{1,0},{3,2},... | collective-permute-start | bytes 344072 | tf_op jit(solution)/shard_map/ppermute | solution.py:547
  31.4 12.8 %collective-permute-start.6 = (f32[288,256]{1,0:T(8,128)S(1)}, f32[288,256]{1,0:T(8,128)S(1)}, u32[]{:S(2)}, u32[]{:S(2)}) collective-permute-start(f32[288,256]{1,0:T(8,128)S(1)} %get-tuple-element.19), channel_id=1, source_target_pairs={{224,240},{256,272},{288,304},{320,336},{352,368},{384,400},{416,4... | collective-permute-start | bytes 884744 | tf_op jit(solution)/shard_map/ppermute | solution.py:547
  34.6 9.7 %collective-permute-start.7 = (f32[56,256]{1,0:T(8,128)S(1)}, f32[56,256]{1,0:T(8,128)S(1)}, u32[]{:S(2)}, u32[]{:S(2)}) collective-permute-start(f32[56,256]{1,0:T(8,128)S(1)} %get-tuple-element.29), channel_id=1, source_target_pairs={{16,32},{48,64},{80,96},{112,128},{144,160},{176,192},{208,224},{2... | collective-permute-start | bytes 172040 | tf_op jit(solution)/shard_map/ppermute | solution.py:547
  41.6 6.1 %collective-permute-start.8 = (f32[56,256]{1,0:T(8,128)S(1)}, f32[56,256]{1,0:T(8,128)S(1)}, u32[]{:S(2)}, u32[]{:S(2)}) collective-permute-start(f32[56,256]{1,0:T(8,128)S(1)} %get-tuple-element.30), channel_id=1, source_target_pairs={{0,16},{32,48},{64,80},{96,112},{128,144},{160,176},{192,208},{224... | collective-permute-start | bytes 172040 | tf_op jit(solution)/shard_map/ppermute | solution.py:547
  43.5 4.1 %copy-start.5 = (f32[192,128]{1,0:T(8,128)S(1)}, f32[192,128]{1,0:T(8,128)}, u32[]{:S(2)}) copy-start(f32[192,128]{1,0:T(8,128)} %message.1.mine) | copy-start | bytes 294916

commit v11 on v10

--- a/solution.py
+++ b/solution.py
@@ -119,7 +119,7 @@
 
 
 def message_kernel(ef, hf, ea, ha, eps, density, mask, partner, mon_f, mon_a,
-                   message, fields, eps_in, small_f, small_i, mons, square, sems):
+                   message, x_far, x_near, fields, eps_in, small_f, small_i, mons, square, sems):
     nx, ny = ef.shape[1], ef.shape[2]
     copies = []
     for f, (e, h) in enumerate(((ef, hf), (ea, ha))):
@@ -162,12 +162,11 @@
         message[pl.ds(c * 32, ny), :] = pack_planes(
             [(k * 64 + x * 16 + f * 8, fields[f, k, c, x])
              for k in range(2) for x in range(nx) for f in range(2)])
-
-
-def bulk_kernel(ef, hf, ea, ha, eps, message, x_far, x_near):
-    del message
-    fields = ((ef, hf), (ea, ha))
-    write_bulk(lambda f, k, c, x: fields[f][k][c, x], eps, x_far, x_near)
+    write_bulk(lambda f, k, c, x: fields[f, k, c, x], eps_in, x_far, x_near)
+
+
+def keep_kernel(message, out):
+    out[...] = message[...]
 
 
 def small_parts(message):
@@ -562,14 +561,14 @@
     fields = [e_fwd, h_fwd, e_adj, h_adj]
 
     bulk_shape = shape(9 * ny, nz)
-    mine, = call(
-        message_kernel, [shape(MESSAGE, LANES)],
+    mine, *bulk = call(
+        message_kernel, [shape(MESSAGE, LANES), bulk_shape, bulk_shape],
         fields + [eps_back, density, design_mask, partner_map, mon_fwd, mon_adj],
         [vmem(2, 2, 3, nx, ny, nz), vmem(nx, ny, nz), vmem(*density.shape),
          pltpu.VMEM((2,) + density.shape, jnp.int32), vmem(2, *mon_fwd.shape),
          square, pltpu.SemaphoreType.DMA((10,))], name="message", any_in=True)
     theirs = mirrored(mine, "gx")
-    bulk = call(bulk_kernel, [bulk_shape, bulk_shape], [*fields, eps_back, mine], name="bulk")
+    mine, = call(keep_kernel, [shape(MESSAGE, LANES)], [mine], name="keep")
     early = 7 * lax.axis_size("gx") // 16
     bulk_lower = swapped(*bulk, "gx", stop=early)
     bulk_upper = swapped(*bulk, "gx", start=early)

time: 51.3 us -> 50.7 us (0.988)
  waiting for transfers between devices: 11.7 us -> 11 us
    ppermute x1, waiting for transfers between devices: 4.58 us -> 3.88 us  [mirrored(): return lax.ppermute(block, axis, [(i, size - 1 - i) for i in range(size)])]
where the time goes in v11:
time: 50.7 us; the launch traced here: 50.4 us
  starting transfers between devices  29.2 us (58%)
  waiting for transfers between devices  11 us (22%)
  Pallas kernels  8.49 us (17%)
  local copies, waits for them, and re-layouts  0.91 us (2%)
  between operations  0.84 us (2%)
    ppermute x4, starting transfers between devices, swapped(): lax.ppermute(far, axis, pairs(1))  15.2 us
    pallas_call x6, Pallas kernels, call(): pl.pallas_call(kernel, out_shape=outs, in_specs=[pl.BlockSpec(memory_spac...  8.49 us
    ppermute x1, starting transfers between devices, mirrored(): return lax.ppermute(block, axis, [(i, size - 1 - i) for i in range(size)])  6.99 us
    ppermute x4, starting transfers between devices, swapped(): lax.ppermute(near, axis, pairs(0))  6.95 us
    ppermute x4, waiting for transfers between devices, swapped(): lax.ppermute(near, axis, pairs(0))  5.46 us
    ppermute x1, waiting for transfers between devices, mirrored(): return lax.ppermute(block, axis, [(i, size - 1 - i) for i in range(size)])  3.88 us
    ppermute x4, waiting for transfers between devices, swapped(): lax.ppermute(far, axis, pairs(1))  1.67 us
  transfers between devices with their start and end apart: 9, of which 4 were waited for; matrix products, arithmetic and copies ran while one was open for 0% of the time, Pallas kernels for 4%

profile of v11, /device:TPU:74, one launch (start us, length us, event | category | flops | bytes accessed | tf_op | source)
XLA Modules:
  0.0 50.4 jit_solution(12826298758455024199)
XLA Ops:
  0.6 0.0 copy-start.3
  0.6 0.0 copy-start.2
  0.7 0.0 copy-start.1
  0.7 0.0 copy-start
  0.7 0.0 copy-start.4
  0.7 3.3 %message.1 = (f32[192,128]{1,0:T(8,128)}, f32[288,256]{1,0:T(8,128)}, f32[288,256]{1,0:T(8,128)}) custom-call(f32[3,4,32,256]{3,2,1,0:T(8,128)} %ef_in.1, f32[3,4,32,256]{3,2,1,0:T(8,128)} %hf_in.1, f32[3,4,32,256]{3,2,1,0:T(8,128)} %ea_in.1, f32[3,4,32,256]{3,2,1,0:T(8,128)} %ha_in.1, f32[4,32,256]{2,1,0:T(8,128)} %eps.3, f32[4,4,32]{2,1,0:T(4,128)} %density.1, ...), custom_call_target="tpu_custom_call" | custom-call | flops 4000000 | bytes 4000000 | tf_op jit(solution)/shard_map/message/pallas_call | solution.py:527
  4.0 3.7 %collective-permute-start = (f32[288,256]{1,0:T(8,128)}, f32[288,256]{1,0:T(8,128)S(1)}, u32[]{:S(2)}, u32[]{:S(2)}) collective-permute-start(f32[288,256]{1,0:T(8,128)} %get-tuple-element.19), channel_id=1, source_target_pairs={{16,32},{48,64},{80,96},{112,128},{144,160},{176,192},{208,224},{3... | collective-permute-start | bytes 884744 | tf_op jit(solution)/shard_map/ppermute | solution.py:546
  7.7 1.9 %collective-permute-start.1 = (f32[288,256]{1,0:T(8,128)}, f32[288,256]{1,0:T(8,128)S(1)}, u32[]{:S(2)}, u32[]{:S(2)}) collective-permute-start(f32[288,256]{1,0:T(8,128)} %get-tuple-element.20), channel_id=1, source_target_pairs={{0,16},{32,48},{64,80},{96,112},{128,144},{160,176},{192,208},{16,... | collective-permute-start | bytes 884744 | tf_op jit(solution)/shard_map/ppermute | solution.py:546
  9.6 7.0 %collective-permute-start.2 = (f32[192,128]{1,0:T(8,128)}, f32[192,128]{1,0:T(8,128)S(1)}, u32[]{:S(2)}, u32[]{:S(2)}) collective-permute-start(f32[192,128]{1,0:T(8,128)} %get-tuple-element.21.message), channel_id=1, source_target_pairs={{0,496},{16,480},{32,464},{48,448},{64,432},{80,416},{96,400},{112... | collective-permute-start | bytes 294920 | tf_op jit(solution)/shard_map/ppermute | solution.py:551
  16.6 0.7 %collective-permute-start.3 = (f32[288,256]{1,0:T(8,128)}, f32[288,256]{1,0:T(8,128)S(1)}, u32[]{:S(2)}, u32[]{:S(2)}) collective-permute-start(f32[288,256]{1,0:T(8,128)} %get-tuple-element.19), channel_id=1, source_target_pairs={{240,256},{272,288},{304,320},{336,352},{368,384},{400,416},{432,4... | collective-permute-start | bytes 884744 | tf_op jit(solution)/shard_map/ppermute | solution.py:546
  17.3 0.0 copy-start.5
  17.3 0.9 %copy-done.5 = f32[192,128]{1,0:T(8,128)S(1)} copy-done((f32[192,128]{1,0:T(8,128)S(1)}, f32[192,128]{1,0:T(8,128)}, u32[]{:S(2)}) %copy-start.5) | copy-done | bytes 98328
  18.2 0.0 copy-start.6
  18.2 3.9 %collective-permute-done.2.theirs = f32[192,128]{1,0:T(8,128)S(1)} collective-permute-done((f32[192,128]{1,0:T(8,128)}, f32[192,128]{1,0:T(8,128)S(1)}, u32[]{:S(2)}, u32[]{:S(2)}) %collective-permute-start.2) | collective-permute-done | bytes 98336 | tf_op jit(solution)/shard_map/ppermute | solution.py:551
  22.1 0.0 collective-permute-done.bulk_far.bulk_far_1
  22.1 2.0 %collective-permute-done.1.bulk_near.bulk_near_1 = f32[288,256]{1,0:T(8,128)S(1)} collective-permute-done((f32[288,256]{1,0:T(8,128)}, f32[288,256]{1,0:T(8,128)S(1)}, u32[]{:S(2)}, u32[]{:S(2)}) %collective-permute-start.1) | collective-permute-done | bytes 294944 | tf_op jit(solution)/shard_map/ppermute | solution.py:546
  24.1 0.0 copy-done.3
  24.2 0.0 copy-done.2
  24.2 0.0 copy-done.1
  24.2 0.0 copy-done
  24.2 0.0 copy-done.4
  24.2 0.5 coefficient.1
  24.7 3.8 %collective-permute-start.4 = (f32[112,256]{1,0:T(8,128)S(1)}, f32[112,256]{1,0:T(8,128)S(1)}, u32[]{:S(2)}, u32[]{:S(2)}) collective-permute-start(f32[112,256]{1,0:T(8,128)S(1)} %get-tuple-element.24), channel_id=1, source_target_pairs={{1,2},{3,4},{5,6},{7,8},{9,10},{11,12},{13,14},{2,1},{4,3},{6,5},{... | collective-permute-start | bytes 344072 | tf_op jit(solution)/shard_map/ppermute | solution.py:546
  28.5 2.4 %collective-permute-start.5 = (f32[112,256]{1,0:T(8,128)S(1)}, f32[112,256]{1,0:T(8,128)S(1)}, u32[]{:S(2)}, u32[]{:S(2)}) collective-permute-start(f32[112,256]{1,0:T(8,128)S(1)} %get-tuple-element.25), channel_id=1, source_target_pairs={{0,1},{2,3},{4,5},{6,7},{8,9},{10,11},{12,13},{14,15},{1,0},{3,2},... | collective-permute-start | bytes 344072 | tf_op jit(solution)/shard_map/ppermute | solution.py:546
  30.9 0.0 copy-done.6
  30.9 0.7 %collective-permute-start.6 = (f32[288,256]{1,0:T(8,128)S(1)}, f32[288,256]{1,0:T(8,128)S(1)}, u32[]{:S(2)}, u32[]{:S(2)}) collective-permute-start(f32[288,256]{1,0:T(8,128)S(1)} %copy-done.6), channel_id=1, source_target_pairs={{224,240},{256,272},{288,304},{320,336},{352,368},{384,400},{416,4... | collective-permute-start | bytes 884744 | tf_op jit(solution)/shard_map/ppermute | solution.py:546
  31.6 0.0 collective-permute-done.3.bulk_far.bulk_far_2
  31.6 1.7 %collective-permute-done.4.y_far = f32[112,256]{1,0:T(8,128)S(1)} collective-permute-done((f32[112,256]{1,0:T(8,128)S(1)}, f32[112,256]{1,0:T(8,128)S(1)}, u32[]{:S(2)}, u32[]{:S(2)}) %collective-permute-start.4) | collective-permute-done | bytes 114720 | tf_op jit(solution)/shard_map/ppermute | solution.py:546
  33.3 0.0 collective-permute-done.5.y_near
  33.3 0.8 %edges.1 = (f32[52,8,256]{2,1,0:T(8,128)S(1)}, f32[52,8,256]{2,1,0:T(8,128)S(1)}, f32[4,48,128]{2,1,0:T(8,128)S(1)}, f32[56,256]{1,0:T(8,128)S(1)}, f32[56,256]{1,0:T(8,128)S(1)}) custom-call(f32[288,256]{1,0:T(8,128)S(1)} %collective-permute-done.3.bulk_far.bulk_far_2, f32[3,4,32,256]{3,2,1,0:T(8,128)S(1)} %copy-done, f32[3,4,32,256]{3,2,1,0:T(8,128)S(1)} %copy-done.1, ...), custom_call_target="tpu_custom_call" | custom-call | flops 4000000000 | bytes 4000000 | tf_op jit(solution)/shard_map/edges/pallas_call | solution.py:527
  34.0 7.0 %collective-permute-start.7 = (f32[56,256]{1,0:T(8,128)S(1)}, f32[56,256]{1,0:T(8,128)S(1)}, u32[]{:S(2)}, u32[]{:S(2)}) collective-permute-start(f32[56,256]{1,0:T(8,128)S(1)} %get-tuple-element.31), channel_id=1, source_target_pairs={{16,32},{48,64},{80,96},{112,128},{144,160},{176,192},{208,224},{2... | collective-permute-start | bytes 172040 | tf_op jit(solution)/shard_map/ppermute | solution.py:546
  41.1 1.9 %collective-permute-start.8 = (f32[56,256]{1,0:T(8,128)S(1)}, f32[56,256]{1,0:T(8,128)S(1)}, u32[]{:S(2)}, u32[]{:S(2)}) collective-permute-start(f32[56,256]{1,0:T(8,128)S(1)} %get-tuple-element.32), channel_id=1, source_target_pairs={{0,16},{32,48},{64,80},{96,112},{128,144},{160,176},{192,208},{224... | collective-permute-start | bytes 172040 | tf_op jit(solution)/shard_map/ppermute | solution.py:546
  43.0 0.7 %first.1 = (f32[2,3,4,48,256]{4,3,2,1,0:T(8,128)S(1)}, f32[2,3,4,48,256]{4,3,2,1,0:T(8,128)S(1)}) custom-call(f32[3,4,32,256]{3,2,1,0:T(8,128)S(1)} %copy-done, f32[3,4,32,256]{3,2,1,0:T(8,128)S(1)} %copy-done.1, f32[3,4,32,256]{3,2,1,0:T(8,128)S(1)} %copy-done.2, f32[3,4,32,256]{3,2,1,0:T(8,128)S(1)} %copy-done.3, ...), custom_call_target="tpu_custom_call" | custom-call | flops 4000000 | bytes 4000000 | tf_op jit(solution)/shard_map/first/pallas_call | solution.py:527
  43.7 0.0 collective-permute-done.6.bulk_near_2
  43.7 0.0 collective-permute-done.7.x_far
  43.7 3.4 %collective-permute-done.8.x_near = f32[56,256]{1,0:T(8,128)S(1)} collective-permute-done((f32[56,256]{1,0:T(8,128)S(1)}, f32[56,256]{1,0:T(8,128)S(1)}, u32[]{:S(2)}, u32[]{:S(2)}) %collective-permute-start.8) | collective-permute-done | bytes 57376 | tf_op jit(solution)/shard_map/ppermute | solution.py:546
  47.2 3.3 %steps.1 = (f32[3,4,32,256]{3,2,1,0:T(8,128)}, f32[3,4,32,256]{3,2,1,0:T(8,128)}, f32[3,4,32,256]{3,2,1,0:T(8,128)}, f32[3,4,32,256]{3,2,1,0:T(8,128)}, f32[4,4,32]{2,1,0:T(4,128)}) custom-call(f32[3,4,32,256]{3,2,1,0:T(8,128)S(1)} %copy-done, f32[3,4,32,256]{3,2,1,0:T(8,128)S(1)} %copy-done.1, f32[3,4,32,256]{3,2,1,0:T(8,128)S(1)} %copy-done.2, ...), custom_call_target="tpu_custom_call" | custom-call | flops 4000000 | bytes 4000000 | tf_op jit(solution)/shard_map/steps/pallas_call | solution.py:527
  (1 shorter events, 0.0 us)
Async XLA Ops:
  0.6 23.5 %copy-start.3 = (f32[3,4,32,256]{3,2,1,0:T(8,128)S(1)}, f32[3,4,32,256]{3,2,1,0:T(8,128)}, u32[]{:S(2)}) copy-start(f32[3,4,32,256]{3,2,1,0:T(8,128)} %ha_in.1) | copy-start | bytes 1179652
  0.6 23.5 %copy-start.2 = (f32[3,4,32,256]{3,2,1,0:T(8,128)S(1)}, f32[3,4,32,256]{3,2,1,0:T(8,128)}, u32[]{:S(2)}) copy-start(f32[3,4,32,256]{3,2,1,0:T(8,128)} %ea_in.1) | copy-start | bytes 1179652
  0.7 23.5 %copy-start.1 = (f32[3,4,32,256]{3,2,1,0:T(8,128)S(1)}, f32[3,4,32,256]{3,2,1,0:T(8,128)}, u32[]{:S(2)}) copy-start(f32[3,4,32,256]{3,2,1,0:T(8,128)} %hf_in.1) | copy-start | bytes 1179652
  0.7 23.5 %copy-start = (f32[3,4,32,256]{3,2,1,0:T(8,128)S(1)}, f32[3,4,32,256]{3,2,1,0:T(8,128)}, u32[]{:S(2)}) copy-start(f32[3,4,32,256]{3,2,1,0:T(8,128)} %ef_in.1) | copy-start | bytes 1179652
  0.7 23.5 %copy-start.4 = (f32[4,32,256]{2,1,0:T(8,128)S(1)}, f32[4,32,256]{2,1,0:T(8,128)}, u32[]{:S(2)}) copy-start(f32[4,32,256]{2,1,0:T(8,128)} %eps.3) | copy-start | bytes 393220
  4.0 18.1 %collective-permute-start = (f32[288,256]{1,0:T(8,128)}, f32[288,256]{1,0:T(8,128)S(1)}, u32[]{:S(2)}, u32[]{:S(2)}) collective-permute-start(f32[288,256]{1,0:T(8,128)} %get-tuple-element.19), channel_id=1, source_target_pairs={{16,32},{48,64},{80,96},{112,128},{144,160},{176,192},{208,224},{3... | collective-permute-start | bytes 884744 | tf_op jit(solution)/shard_map/ppermute | solution.py:546
  7.7 16.5 %collective-permute-start.1 = (f32[288,256]{1,0:T(8,128)}, f32[288,256]{1,0:T(8,128)S(1)}, u32[]{:S(2)}, u32[]{:S(2)}) collective-permute-start(f32[288,256]{1,0:T(8,128)} %get-tuple-element.20), channel_id=1, source_target_pairs={{0,16},{32,48},{64,80},{96,112},{128,144},{160,176},{192,208},{16,... | collective-permute-start | bytes 884744 | tf_op jit(solution)/shard_map/ppermute | solution.py:546
  9.6 12.5 %collective-permute-start.2 = (f32[192,128]{1,0:T(8,128)}, f32[192,128]{1,0:T(8,128)S(1)}, u32[]{:S(2)}, u32[]{:S(2)}) collective-permute-start(f32[192,128]{1,0:T(8,128)} %get-tuple-element.21.message), channel_id=1, source_target_pairs={{0,496},{16,480},{32,464},{48,448},{64,432},{80,416},{96,400},{112... | collective-permute-start | bytes 294920 | tf_op jit(solution)/shard_map/ppermute | solution.py:551
  16.6 15.0 %collective-permute-start.3 = (f32[288,256]{1,0:T(8,128)}, f32[288,256]{1,0:T(8,128)S(1)}, u32[]{:S(2)}, u32[]{:S(2)}) collective-permute-start(f32[288,256]{1,0:T(8,128)} %get-tuple-element.19), channel_id=1, source_target_pairs={{240,256},{272,288},{304,320},{336,352},{368,384},{400,416},{432,4... | collective-permute-start | bytes 884744 | tf_op jit(solution)/shard_map/ppermute | solution.py:546
  17.3 0.9 %copy-start.5 = (f32[192,128]{1,0:T(8,128)S(1)}, f32[192,128]{1,0:T(8,128)}, u32[]{:S(2)}) copy-start(f32[192,128]{1,0:T(8,128)} %get-tuple-element.21.message) | copy-start | bytes 294916
  18.2 12.7 %copy-start.6 = (f32[288,256]{1,0:T(8,128)S(1)}, f32[288,256]{1,0:T(8,128)}, u32[]{:S(2)}) copy-start(f32[288,256]{1,0:T(8,128)} %get-tuple-element.20) | copy-start | bytes 884740
  24.7 8.6 %collective-permute-start.4 = (f32[112,256]{1,0:T(8,128)S(1)}, f32[112,256]{1,0:T(8,128)S(1)}, u32[]{:S(2)}, u32[]{:S(2)}) collective-permute-start(f32[112,256]{1,0:T(8,128)S(1)} %get-tuple-element.24), channel_id=1, source_target_pairs={{1,2},{3,4},{5,6},{7,8},{9,10},{11,12},{13,14},{2,1},{4,3},{6,5},{... | collective-permute-start | bytes 344072 | tf_op jit(solution)/shard_map/ppermute | solution.py:546
  28.5 4.8 %collective-permute-start.5 = (f32[112,256]{1,0:T(8,128)S(1)}, f32[112,256]{1,0:T(8,128)S(1)}, u32[]{:S(2)}, u32[]{:S(2)}) collective-permute-start(f32[112,256]{1,0:T(8,128)S(1)} %get-tuple-element.25), channel_id=1, source_target_pairs={{0,1},{2,3},{4,5},{6,7},{8,9},{10,11},{12,13},{14,15},{1,0},{3,2},... | collective-permute-start | bytes 344072 | tf_op jit(solution)/shard_map/ppermute | solution.py:546
  30.9 12.8 %collective-permute-start.6 = (f32[288,256]{1,0:T(8,128)S(1)}, f32[288,256]{1,0:T(8,128)S(1)}, u32[]{:S(2)}, u32[]{:S(2)}) collective-permute-start(f32[288,256]{1,0:T(8,128)S(1)} %copy-done.6), channel_id=1, source_target_pairs={{224,240},{256,272},{288,304},{320,336},{352,368},{384,400},{416,4... | collective-permute-start | bytes 884744 | tf_op jit(solution)/shard_map/ppermute | solution.py:546
  34.0 9.7 %collective-permute-start.7 = (f32[56,256]{1,0:T(8,128)S(1)}, f32[56,256]{1,0:T(8,128)S(1)}, u32[]{:S(2)}, u32[]{:S(2)}) collective-permute-start(f32[56,256]{1,0:T(8,128)S(1)} %get-tuple-element.31), channel_id=1, source_target_pairs={{16,32},{48,64},{80,96},{112,128},{144,160},{176,192},{208,224},{2... | collective-permute-start | bytes 172040 | tf_op jit(solution)/shard_map/ppermute | solution.py:546
  41.1 6.1 %collective-permute-start.8 = (f32[56,256]{1,0:T(8,128)S(1)}, f32[56,256]{1,0:T(8,128)S(1)}, u32[]{:S(2)}, u32[]{:S(2)}) collective-permute-start(f32[56,256]{1,0:T(8,128)S(1)} %get-tuple-element.32), channel_id=1, source_target_pairs={{0,16},{32,48},{64,80},{96,112},{128,144},{160,176},{192,208},{224... | collective-permute-start | bytes 172040 | tf_op jit(solution)/shard_map/ppermute | solution.py:546
